TPU v7x, 256 devices: a whole 4x4x8 slice. The times are simulated.
256 devices in a mesh: tok: 32 (over x, z_hi, y), feat: 8 (over z_lo, core).
Axes of the slice: x: 4, y: 4, z: 8 (z_hi: 2, z_lo: 4; z = z_hi * 4 + z_lo), core: 2. Of those that a mesh axis runs over, the one named last changes fastest.
Arguments:
- activations: bfloat16 [65536, 16384], P('tok', 'feat'), may hold values from -6 to 6
- probes: bfloat16 [256, 16384], P(None, 'feat'), may hold values from -6 to 6
Outputs:
- first_product: float32 [256, 16384], P('tok', 'feat')
- second_product: float32 [256, 16384], P('tok', 'feat')
All inputs are finite; a program needn't handle non-finite values.
Results may differ from a plain program's by a relative error of at most 0.0027.
Values may be sent and summed in bfloat16 or wider, within the bound.
No kernel may reach another device: no remote copies, remote signals or barrier semaphores. Data moves between devices by JAX's collectives and lax.ppermute only.
A program may use at most 64 MiB of HBM per device.

v0:
```python
import jax
import jax.numpy as jnp
from jax import lax
from jax.sharding import PartitionSpec as P


def score_rows(activations, left):
    partial_value = lax.dot_general(
        activations, left, (((1,), (1,)), ((), ())), preferred_element_type=jnp.float32
    )
    return lax.psum(partial_value, "feat").astype(jnp.bfloat16)


def token_reduce(activations, scores, with_full):
    total_tokens = activations.shape[0] * lax.axis_size("tok")
    probe_rows = scores.shape[1] // lax.axis_size("tok")
    term = lax.dot_general(
        scores, activations, (((0,), (0,)), ((), ())), preferred_element_type=jnp.float32
    )
    summed = lax.psum(term, "tok") / total_tokens
    start = lax.axis_index("tok") * probe_rows
    own_rows = lax.dynamic_slice_in_dim(summed, start, probe_rows, 0)
    full_rows = summed.astype(jnp.bfloat16) if with_full else None
    return (own_rows, full_rows)


def shards(activations, probes):
    token_scores = score_rows(activations, probes)
    first_product, first_rounded = token_reduce(activations, token_scores, True)
    second_scores = score_rows(activations, first_rounded)
    second_product, unused_rows = token_reduce(activations, second_scores, False)
    return (first_product, second_product)


def solution(mesh):
    in_specs = (P("tok", "feat"), P(None, "feat"))
    out_specs = (P("tok", "feat"), P("tok", "feat"))
    return jax.shard_map(shards, mesh=mesh, in_specs=in_specs, out_specs=out_specs, check_vma=False)
```

profile of v0, /device:TPU:8, one launch (start us, length us, event | category | flops | bytes accessed | tf_op | source)
XLA Modules:
  0.0 1041.0 jit_solution(15402865487962259801)
XLA Ops:
  7.2 0.0 copy-start
  7.2 0.0 all-reduce.5.cloned.1.call-start
  7.2 1.2 copy-done
  8.4 7.1 fusion.5
  15.5 66.0 %all-reduce.8 = bf16[2048,256]{1,0:T(8,128)(2,1)S(1)} all-reduce(f32[2048,256]{1,0:T(8,128)} %fusion.5), channel_id=1, replica_groups=mesh['tok'=32,'feat'=8] {'feat'}, use_global_device_ids=true, to_apply=%region_0.0 | all-reduce | flops 524288 | bytes 3145728 | tf_op jit(solution)/shard_map/psum | solution.py:11
  81.5 7.0 fusion.7
  88.5 0.0 all-reduce.5.cloned.1.call-update
  88.6 0.0 all-reduce.7.cloned.1.call-start
  88.6 434.1 %all-reduce.5.cloned.1.call-done = f32[256,2048]{1,0:T(8,128)} async-done(((f32[256,2048]{1,0:T(8,128)}), f32[256,2048]{1,0:T(8,128)}) %all-reduce.5.cloned.1.call-update) | async-done | bytes 2097168 | tf_op jit(solution)/shard_map/psum | solution.py:20
  522.7 6.4 convolution_bitcast_fusion
  529.1 62.5 %all-reduce.9 = bf16[2048,256]{0,1:T(8,128)(2,1)} all-reduce(f32[2048,256]{0,1:T(8,128)S(1)} %convolution_bitcast_fusion), channel_id=1, replica_groups=mesh['tok'=32,'feat'=8] {'feat'}, use_global_device_ids=true, to_apply=%region_2.0 | all-reduce | flops 524288 | bytes 3145728 | tf_op jit(solution)/shard_map/psum | solution.py:11
  591.7 7.3 fusion.6
  599.0 0.0 copy-start.1
  599.0 0.0 all-reduce.7.cloned.1.call-update
  599.0 1.6 copy-done.1
  600.6 0.2 broadcast_multiply_fusion
  600.8 0.6 constant_dynamic-slice_fusion
  601.4 431.2 %all-reduce.7.cloned.1.call-done = f32[256,2048]{1,0:T(8,128)} async-done(((f32[256,2048]{1,0:T(8,128)}), f32[256,2048]{1,0:T(8,128)}) %all-reduce.7.cloned.1.call-update) | async-done | bytes 2097168 | tf_op jit(solution)/shard_map/psum | solution.py:20
  1032.7 1.5 dynamic-slice_multiply_fusion
Async XLA Ops:
  7.2 1.2 copy-start
  7.2 515.6 %all-reduce.5.cloned.1.call-start = ((), (), s32[]{:S(2)}) async-start(), calls=%async_computation | async-start | bytes 4194304 | tf_op jit(solution)/shard_map/psum | solution.py:20
  88.6 944.1 %all-reduce.7.cloned.1.call-start = ((), (), s32[]{:S(2)}) async-start(), calls=%async_computation.1 | async-start | bytes 4194304 | tf_op jit(solution)/shard_map/psum | solution.py:20
  599.0 1.6 copy-start.1
Sparse Core Ops, SparseCore 0:
  88.7 433.9 all-reduce.4
  599.1 433.4 all-reduce.6
where the time goes:
time: 1040 us
  waiting for transfers between devices  865 us (83%)
  blocking collectives  129 us (12%)
  matrix products  27.9 us (3%)
  between operations  14.1 us (1%)
    psum x2, waiting for transfers between devices, token_reduce(): summed = lax.psum(term, 'tok') / total_tokens  865 us
    psum x2, blocking collectives, score_rows(): return lax.psum(partial_value, 'feat').astype(jnp.bfloat16)  129 us
  transfers between devices with their start and end apart: 2, of which 2 were waited for; matrix products, arithmetic and copies ran while one was open for 0% of the time, Pallas kernels for 0%

commit v1 on v0

v1 whole, which is shorter than its diff:
```python
import jax
import jax.numpy as jnp
from jax import lax
from jax.experimental import pallas as pl
from jax.experimental.pallas import tpu as pltpu
from jax.sharding import Mesh, PartitionSpec as P

SIZES = {"x": 4, "h": 2, "y": 4, "z": 4, "c": 2}
F32, BF16 = jnp.float32, jnp.bfloat16
VMEM = pl.BlockSpec(memory_space=pltpu.VMEM)
TILE = 512

ROWS = 16
PIECES = 2


def dot(a, b, dim_a, dim_b):
    return lax.dot_general(
        a, b, (((dim_a,), (dim_b,)), ((), ())), preferred_element_type=F32
    )


def place(index, outer, inner):
    return lax.bitwise_xor(index, outer ^ 3 * inner)


def swap(value, axis, mask):
    return lax.ppermute(value, axis, [(i, i ^ mask) for i in range(SIZES[axis])])


def swap_xy(value, stage, bits):
    pairs = []
    for x in range(4):
        for y in range(4):
            for c in range(2):
                unit = 1 if c == stage else 3
                to = (x ^ bits // 2 * unit) * 4 + (y ^ bits % 2 * unit)
                pairs.append(((x * 4 + y) * 2 + c, to * 2 + c))
    return lax.ppermute(value, ("x", "y", "c"), pairs)


def reduce_four(parts, stage, kind):
    total = parts[0].astype(F32)
    for got in [swap_xy(parts[i].astype(kind), stage, i) for i in (3, 1, 2)]:
        total = total + got.astype(F32)
    return total


def gather_four(part, stage):
    got = {i: swap_xy(part, stage, i) for i in (3, 1, 2)}
    return jnp.stack([part, got[1], got[2], got[3]])


def call(kernel, outs, *args, specs=None, scratch=(), flops=0, limit=16):
    return pl.pallas_call(
        kernel,
        in_specs=specs or [VMEM] * len(args),
        out_specs=[VMEM] * len(outs),
        out_shape=[pltpu.VMEM(shape, kind) for shape, kind in outs],
        scratch_shapes=list(scratch),
        compiler_params=pltpu.CompilerParams(vmem_limit_bytes=limit * 2**20),
        cost_estimate=pl.CostEstimate(
            flops=flops, bytes_accessed=2**20, transcendentals=0
        ),
    )(*args)


def token_rows(x_ref):
    parity = lax.rem(lax.axis_index("z"), 2)
    block = x_ref.shape[0] // (2 * PIECES)
    starts = []
    for piece in range(PIECES):
        for chip in (parity, 1 - parity):
            starts.append((chip * PIECES + piece) * block)
    return [pl.ds(pl.multiple_of(start, block), block) for start in starts]


def write_scores(x_ref, probes, s_ref):
    block = x_ref.shape[0] // (2 * PIECES)
    for i, rows in enumerate(token_rows(x_ref)):
        value = dot(x_ref[rows], probes, 1, 1)
        s_ref[pl.ds(i * block, block)] = value.astype(s_ref.dtype)


def load(activations, probes):
    tokens, features = activations.shape
    half, count = tokens // 2, probes.shape[0]

    def kernel(x_hbm, p_hbm, theirs_ref, own_ref, p_ref, s_ref, raw_ref, row_ref, sems):
        core, x, y = (lax.axis_index(name) for name in ("c", "x", "y"))

        def rows_of(c):
            return x_hbm.at[pl.ds(pl.multiple_of(c * half, half), half)]

        copies = [
            pltpu.make_async_copy(p_hbm, raw_ref, sems.at[0]),
            pltpu.make_async_copy(rows_of(1 - core), theirs_ref, sems.at[1]),
            pltpu.make_async_copy(rows_of(core), own_ref, sems.at[2]),
        ]
        for copy in copies:
            copy.start()
        copies[0].wait()
        row_ref[...] = raw_ref[...].astype(F32)
        for i in range(16):
            at_x = place(x, i // 8, i // 2 % 2)
            at_y = place(y, i // 4 % 2, i % 2)
            pair = [
                row_ref[pl.ds(pl.multiple_of(at_x * 64 + h * 32 + at_y * 8, 8), 8)]
                for h in range(2)
            ]
            p_ref[pl.ds(i * ROWS, ROWS)] = jnp.concatenate(pair, 0).astype(BF16)
        copies[1].wait()
        write_scores(theirs_ref, p_ref[...], s_ref)
        copies[2].wait()

    hbm = pl.BlockSpec(memory_space=pltpu.HBM)
    return call(
        kernel,
        [((half, features), BF16)] * 2 + [(probes.shape, BF16), ((half, count), BF16)],
        activations,
        probes,
        specs=[hbm, hbm],
        scratch=[
            pltpu.VMEM(probes.shape, BF16),
            pltpu.VMEM(probes.shape, F32),
            pltpu.SemaphoreType.DMA((3,)),
        ],
        flops=tokens * features * count,
        limit=48,
    )


def score(x_half, probes, out_type):
    tokens, features = x_half.shape

    def kernel(x_ref, p_ref, s_ref):
        write_scores(x_ref, p_ref[...], s_ref)

    return call(
        kernel,
        [((tokens, probes.shape[0]), out_type)],
        x_half,
        probes,
        flops=2 * tokens * features * probes.shape[0],
    )[0]


def add_piece(own, theirs, piece):
    block = own.shape[0] // (2 * PIECES)
    shape = (block, own.shape[1])

    def kernel(own_ref, theirs_ref, kept_ref, given_ref):
        for i, out_ref in enumerate((kept_ref, given_ref)):
            rows = pl.ds((2 * piece + i) * block, block)
            total = own_ref[rows] + theirs_ref[rows].astype(F32)
            out_ref[...] = total.astype(out_ref.dtype)

    return call(kernel, [(shape, F32), (shape, BF16)], own, theirs, flops=2**20)


def add(kept, got, kinds):
    def kernel(kept_ref, got_ref, *out_refs):
        total = kept_ref[...] + got_ref[...].astype(F32)
        for out_ref in out_refs:
            out_ref[...] = total.astype(out_ref.dtype)

    return call(kernel, [(kept.shape, kind) for kind in kinds], kept, got, flops=2**20)


def sum_scores(theirs, own):
    theirs = swap(theirs, "c", 1)
    pieces = []
    for piece in range(PIECES):
        kept, given = add_piece(own, theirs, piece)
        kept, given = add(kept, swap(given, "z", 1), (F32, BF16))
        (mine,) = add(kept, swap(given, "z", 2), (BF16,))
        other = swap(mine, "z", 1)
        pieces.append(((mine, other), (swap(mine, "c", 1), swap(other, "c", 1))))
    return pieces


def product_term(x_refs, s_refs, piece, cols):
    total = None
    for i, s_ref in enumerate(s_refs):
        x_ref = x_refs[i // 2]
        rows = token_rows(x_ref)[2 * piece + i % 2]
        term = dot(s_ref[...], x_ref[rows, cols], 0, 0)
        total = term if total is None else total + term
    return total


def product_part(y_before, x_own, x_theirs, scores, piece):
    features = x_own.shape[1]
    tokens, probes = scores[0].shape

    def kernel(*refs):
        *y_ref, xo_ref, xt_ref, s0_ref, s1_ref, s2_ref, s3_ref, out_ref = refs
        for i in range(0, features, TILE):
            cols = pl.ds(i, TILE)
            term = product_term(
                (xo_ref, xt_ref), (s0_ref, s1_ref, s2_ref, s3_ref), piece, cols
            )
            out_ref[:, cols] = y_ref[0][:, cols] + term if y_ref else term

    return call(
        kernel,
        [((probes, features), F32)],
        *([] if y_before is None else [y_before]),
        x_own,
        x_theirs,
        *scores,
        flops=8 * tokens * features * probes,
    )[0]


def in_order(value, order_a):
    if order_a:
        return value
    return jnp.concatenate(
        [
            value[(j * 4 + i) * ROWS : (j * 4 + i + 1) * ROWS]
            for i in range(4)
            for j in range(4)
        ],
        0,
    )


def product_last(y_before, x_own, x_theirs, scores):
    features = x_own.shape[1]
    tokens, probes = scores[0].shape
    cut = features // 2

    def kernel(*refs):
        y_ref, xo_ref, xt_ref, s0_ref, s1_ref, s2_ref, s3_ref = refs[:7]
        theirs_ref, own_ref, sum_ref = refs[7:]
        core = lax.axis_index("c")
        for i in range(0, features, TILE):
            cols = pl.ds(i, TILE)
            term = product_term(
                (xo_ref, xt_ref), (s0_ref, s1_ref, s2_ref, s3_ref), PIECES - 1, cols
            )
            sum_ref[:, cols] = y_ref[:, cols] + term

        @pl.when(core == 0)
        def _():
            own_ref[...] = in_order(sum_ref[:, pl.ds(0, cut)], True).astype(BF16)
            theirs_ref[...] = in_order(sum_ref[:, pl.ds(cut, cut)], False).astype(BF16)

        @pl.when(core == 1)
        def _():
            own_ref[...] = in_order(sum_ref[:, pl.ds(cut, cut)], False).astype(BF16)
            theirs_ref[...] = in_order(sum_ref[:, pl.ds(0, cut)], True).astype(BF16)

    return call(
        kernel,
        [((probes, cut), BF16)] * 2,
        y_before,
        x_own,
        x_theirs,
        *scores,
        scratch=[pltpu.VMEM((probes, features), F32)],
        flops=8 * tokens * features * probes,
    )


def product(x_theirs, x_own, pieces):
    y = None
    for piece, (own, theirs) in enumerate(pieces[:-1]):
        y = product_part(y, x_own, x_theirs, (*own, *theirs), piece)
    own, theirs = pieces[-1]
    theirs, own = product_last(y, x_own, x_theirs, (*own, *theirs))
    both = jnp.concatenate([own, swap(theirs, "c", 1)], 1)
    total = reduce_four(both.reshape(4, 4 * ROWS, -1), 0, BF16)
    return reduce_four(total.reshape(4, ROWS, -1), 1, F32)


def whole_features(rows, core):
    cut = rows.shape[1] // 2
    own, arrived = rows[:, :cut], swap(rows[:, cut:], "c", 1)
    return jnp.where(
        core == 0,
        jnp.concatenate([own, arrived], 1),
        jnp.concatenate([arrived, own], 1),
    )


def spread(rounded):
    part = gather_four(rounded, 1).reshape(4 * ROWS, -1)
    full = gather_four(part, 0).reshape(16 * ROWS, -1)
    cut = full.shape[1] // 2
    return assemble(full[:, :cut], swap(full[:, cut:], "c", 1))


def assemble(own, arrived):
    probes, cut = own.shape

    def kernel(own_ref, arrived_ref, full_ref):
        core = lax.axis_index("c")

        def write(ref, columns, order_a):
            value = in_order(ref[...].astype(F32), order_a)
            full_ref[:, columns] = value.astype(BF16)

        @pl.when(core == 0)
        def _():
            write(own_ref, pl.ds(0, cut), True)
            write(arrived_ref, pl.ds(cut, cut), False)

        @pl.when(core == 1)
        def _():
            write(own_ref, pl.ds(cut, cut), False)
            write(arrived_ref, pl.ds(0, cut), True)

    return call(kernel, [((probes, 2 * cut), BF16)], own, arrived)[0]


def shards(activations, probes):
    core, h = lax.axis_index("c"), lax.axis_index("h")
    total_tokens = activations.shape[0] * 32

    x_theirs, x_own, mine, theirs = load(activations, probes)
    scores = sum_scores(theirs, score(x_own, mine, F32))
    rows = product(x_theirs, x_own, scores)
    rows = (rows + swap(rows.astype(BF16), "h", 1).astype(F32)) / total_tokens
    first = lax.dynamic_slice_in_dim(rows, h * 8, 8, 0)

    full = spread(rows.astype(BF16))
    theirs = score(x_theirs, full, BF16)
    scores = sum_scores(theirs, score(x_own, full, F32))
    rows = product(x_theirs, x_own, scores)
    mine = lax.dynamic_slice_in_dim(rows, h * 8, 8, 0)
    other = lax.dynamic_slice_in_dim(rows, (1 - h) * 8, 8, 0)
    second = (mine + swap(other, "h", 1)) / total_tokens
    return whole_features(first, core), whole_features(second, core)


def solution(mesh):
    split = Mesh(mesh.devices.reshape(tuple(SIZES.values())), tuple(SIZES))
    tok, feat = ("x", "h", "y"), ("z", "c")
    return jax.shard_map(
        shards,
        mesh=split,
        in_specs=(P(tok, feat), P(None, feat)),
        out_specs=(P(tok, feat), P(tok, feat)),
        check_vma=False,
    )
```

time: 1040 us -> 160 us (0.15)
  waiting for transfers between devices: 865 us -> 81.8 us
  blocking collectives: 129 us -> 0 us
  starting transfers between devices: 0.08 us -> 58.9 us
  matrix products: 27.9 us -> 0 us
  Pallas kernels: 0 us -> 13.5 us
  between operations: 14.1 us -> 0.97 us
    psum x2 -> x0, waiting for transfers between devices: 865 us -> none  [token_reduce(): summed = lax.psum(term, 'tok') / total_tokens]
    psum x2 -> x0, blocking collectives: 129 us -> none  [score_rows(): return lax.psum(partial_value, 'feat').astype(jnp.bfloat16)]
    ppermute x0 -> x47, waiting for transfers between devices: none -> 81.8 us  [the longest x29 45.8 us: swap(): lax.ppermute(value, axis, [(i, i ^ mask) for i in range(SIZES[axis])])]
    ppermute x0 -> x47, starting transfers between devices: none -> 58.9 us  [the longest x29 32 us: swap(): lax.ppermute(value, axis, [(i, i ^ mask) for i in range(SIZES[axis])])]
    dot_general x4 -> x0, matrix products: 27.9 us -> none  [the longest x2 14.4 us: token_reduce(): lax.dot_general(scores, activations, (((0,), (0,)), ((), ())), preferred_...]
    pallas_call x0 -> x21, Pallas kernels: none -> 13.5 us  [call(): pl.pallas_call(kernel, in_specs=specs or [VMEM] * len(args), out_specs=[V...]
  transfers between devices with their start and end apart: 2 -> 47, of which waited for: 2 -> 32; matrix products, arithmetic and copies ran while one was open for 0% -> 0% of each run, Pallas kernels for 0% -> 3%
where the time goes in v1:
time: 160 us; the launch traced here: 157 us
  waiting for transfers between devices  81.8 us (51%)
  starting transfers between devices  58.9 us (37%)
  Pallas kernels  13.5 us (8%)
  other arithmetic  1.78 us (1%)
    ppermute x29, waiting for transfers between devices, swap(): lax.ppermute(value, axis, [(i, i ^ mask) for i in range(SIZES[axis])])  45.8 us
    ppermute x18, waiting for transfers between devices, swap_xy(): return lax.ppermute(value, ('x', 'y', 'c'), pairs)  36.1 us
    ppermute x29, starting transfers between devices, swap(): lax.ppermute(value, axis, [(i, i ^ mask) for i in range(SIZES[axis])])  32 us
    ppermute x18, starting transfers between devices, swap_xy(): return lax.ppermute(value, ('x', 'y', 'c'), pairs)  26.8 us
    pallas_call x21, Pallas kernels, call(): pl.pallas_call(kernel, in_specs=specs or [VMEM] * len(args), out_specs=[V...  13.5 us
  transfers between devices with their start and end apart: 47, of which 32 were waited for; matrix products, arithmetic and copies ran while one was open for 0% of the time, Pallas kernels for 3%

profile of v1, /device:TPU:8, one launch (start us, length us, event | category | flops | bytes accessed | tf_op | source)
XLA Modules:
  0.0 157.3 jit_solution(2740213533400980700)
XLA Ops:
  0.6 3.8 %shard_map.41 = (bf16[1024,2048]{1,0:T(8,128)(2,1)S(1)}, bf16[1024,2048]{1,0:T(8,128)(2,1)S(1)}, bf16[256,2048]{1,0:T(8,128)(2,1)S(1)}, bf16[1024,256]{1,0:T(8,128)(2,1)S(1)}) custom-call(bf16[2048,2048]{1,0:T(8,128)(2,1)} %x_hbm.1, bf16[256,2048]{1,0:T(8,128)(2,1)} %p_hbm.1), custom_call_target="tpu_custom_call" | custom-call | flops 1073741824 | bytes 1048576 | tf_op jit(solution)/shard_map/pallas_call | solution.py:55
  4.6 1.3 shard_map.42.own_ref
  6.5 2.0 %collective-permute-start.1 = (bf16[256,256]{1,0:T(8,128)(2,1)S(1)}, bf16[256,256]{1,0:T(8,128)(2,1)S(1)}, u32[]{:S(2)}, u32[]{:S(2)}) collective-permute-start(bf16[256,256]{1,0:T(8,128)(2,1)S(1)} %get-tuple-element.31), channel_id=1, source_target_pairs={{0,2},{2,0},{4,6},{6,4},{1,3},{3,1},{5,7},{7,5},{8,10},{10,8},{12,... | collective-permute-start | bytes 393224 | tf_op jit(solution)/shard_map/ppermute | solution.py:28
  8.8 4.2 %collective-permute-done.1.got_ref = bf16[256,256]{1,0:T(8,128)(2,1)S(1)} collective-permute-done((bf16[256,256]{1,0:T(8,128)(2,1)S(1)}, bf16[256,256]{1,0:T(8,128)(2,1)S(1)}, u32[]{:S(2)}, u32[]{:S(2)}) %collective-permute-start.1) | collective-permute-done | bytes 131104 | tf_op jit(solution)/shard_map/ppermute | solution.py:28
  13.0 3.4 %collective-permute-start.2 = (bf16[256,256]{1,0:T(8,128)(2,1)S(1)}, bf16[256,256]{1,0:T(8,128)(2,1)S(1)}, u32[]{:S(2)}, u32[]{:S(2)}) collective-permute-start(bf16[256,256]{1,0:T(8,128)(2,1)S(1)} %get-tuple-element.33), channel_id=1, source_target_pairs={{0,4},{2,6},{4,0},{6,2},{1,5},{3,7},{5,1},{7,3},{8,12},{10,14},{12... | collective-permute-start | bytes 393224 | tf_op jit(solution)/shard_map/ppermute | solution.py:28
  16.4 2.8 %collective-permute-start.7 = (bf16[256,256]{1,0:T(8,128)(2,1)S(1)}, bf16[256,256]{1,0:T(8,128)(2,1)S(1)}, u32[]{:S(2)}, u32[]{:S(2)}) collective-permute-start(bf16[256,256]{1,0:T(8,128)(2,1)S(1)} %get-tuple-element.37), channel_id=1, source_target_pairs={{0,4},{2,6},{4,0},{6,2},{1,5},{3,7},{5,1},{7,3},{8,12},{10,14},{12... | collective-permute-start | bytes 393224 | tf_op jit(solution)/shard_map/ppermute | solution.py:28
  19.1 6.5 %collective-permute-done.2.got_ref = bf16[256,256]{1,0:T(8,128)(2,1)S(1)} collective-permute-done((bf16[256,256]{1,0:T(8,128)(2,1)S(1)}, bf16[256,256]{1,0:T(8,128)(2,1)S(1)}, u32[]{:S(2)}, u32[]{:S(2)}) %collective-permute-start.2) | collective-permute-done | bytes 131104 | tf_op jit(solution)/shard_map/ppermute | solution.py:28
  26.2 1.3 collective-permute-done.7.got_ref
  28.1 3.8 %collective-permute-done.3.refs_3_ = bf16[256,256]{1,0:T(8,128)(2,1)S(1)} collective-permute-done((bf16[256,256]{1,0:T(8,128)(2,1)S(1)}, bf16[256,256]{1,0:T(8,128)(2,1)S(1)}, u32[]{:S(2)}, u32[]{:S(2)}) %collective-permute-start.3) | collective-permute-done | bytes 131104 | tf_op jit(solution)/shard_map/ppermute | solution.py:28
  33.4 1.3 shard_map.46.refs_0_
  34.7 1.4 shard_map.50
  36.7 1.5 collective-permute-done.11
  38.3 1.5 collective-permute-start.12
  41.9 3.9 %collective-permute-done.12 = bf16[64,2048]{1,0:T(8,128)(2,1)S(1)} collective-permute-done((bf16[64,2048]{1,0:T(8,128)(2,1)S(1)}, bf16[64,2048]{1,0:T(8,128)(2,1)S(1)}, u32[]{:S(2)}, u32[]{:S(2)}) %collective-permute-start.12) | collective-permute-done | bytes 262176 | tf_op jit(solution)/shard_map/ppermute | solution.py:39
  45.8 2.2 %collective-permute-done.14 = bf16[64,2048]{1,0:T(8,128)(2,1)S(1)} collective-permute-done((bf16[64,2048]{1,0:T(8,128)(2,1)S(1)}, bf16[64,2048]{1,0:T(8,128)(2,1)S(1)}, u32[]{:S(2)}, u32[]{:S(2)}) %collective-permute-start.14) | collective-permute-done | bytes 262176 | tf_op jit(solution)/shard_map/ppermute | solution.py:39
  48.7 3.9 %collective-permute-start.15 = (f32[16,2048]{1,0:T(8,128)S(1)}, f32[16,2048]{1,0:T(8,128)S(1)}, u32[]{:S(2)}, u32[]{:S(2)}) collective-permute-start(f32[16,2048]{1,0:T(8,128)S(1)} %get-tuple-element.65), channel_id=1, source_target_pairs={{0,216},{1,73},{8,208},{9,65},{16,200},{17,89},{24,192},{25,81},{6... | collective-permute-start | bytes 393224 | tf_op jit(solution)/shard_map/ppermute | solution.py:39
  53.5 2.4 %collective-permute-done.15 = f32[16,2048]{1,0:T(8,128)S(1)} collective-permute-done((f32[16,2048]{1,0:T(8,128)S(1)}, f32[16,2048]{1,0:T(8,128)S(1)}, u32[]{:S(2)}, u32[]{:S(2)}) %collective-permute-start.15) | collective-permute-done | bytes 131104 | tf_op jit(solution)/shard_map/ppermute | solution.py:39
  55.8 2.9 %collective-permute-done.17 = f32[16,2048]{1,0:T(8,128)S(1)} collective-permute-done((f32[16,2048]{1,0:T(8,128)S(1)}, f32[16,2048]{1,0:T(8,128)S(1)}, u32[]{:S(2)}, u32[]{:S(2)}) %collective-permute-start.17) | collective-permute-done | bytes 131104 | tf_op jit(solution)/shard_map/ppermute | solution.py:39
  58.8 6.1 %collective-permute-start.18 = (bf16[16,2048]{1,0:T(8,128)(2,1)S(1)}, bf16[16,2048]{1,0:T(8,128)(2,1)S(1)}, u32[]{:S(2)}, u32[]{:S(2)}) collective-permute-start(bf16[16,2048]{1,0:T(8,128)(2,1)S(1)} %get-tuple-element.52), channel_id=1, source_target_pairs={{0,32},{32,0},{1,33},{33,1},{2,34},{34,2},{3,35},{35,3},{4,36},{36... | collective-permute-start | bytes 196616 | tf_op jit(solution)/shard_map/ppermute | solution.py:28
  64.9 2.9 %collective-permute-done.18 = bf16[16,2048]{1,0:T(8,128)(2,1)S(1)} collective-permute-done((bf16[16,2048]{1,0:T(8,128)(2,1)S(1)}, bf16[16,2048]{1,0:T(8,128)(2,1)S(1)}, u32[]{:S(2)}, u32[]{:S(2)}) %collective-permute-start.18) | collective-permute-done | bytes 65568 | tf_op jit(solution)/shard_map/ppermute | solution.py:28
  67.8 1.8 %collective-permute-start.22 = (bf16[16,2048]{1,0:T(8,128)(2,1)S(1)}, bf16[16,2048]{1,0:T(8,128)(2,1)S(1)}, u32[]{:S(2)}, u32[]{:S(2)}) collective-permute-start(bf16[16,2048]{1,0:T(8,128)(2,1)S(1)} %get-tuple-element.50), channel_id=1, source_target_pairs={{0,216},{1,73},{8,208},{9,65},{16,200},{17,89},{24,192},{25,81},{6... | collective-permute-start | bytes 196616 | tf_op jit(solution)/shard_map/ppermute | solution.py:39
  70.4 2.2 %collective-permute-start.20 = (bf16[16,2048]{1,0:T(8,128)(2,1)S(1)}, bf16[16,2048]{1,0:T(8,128)(2,1)S(1)}, u32[]{:S(2)}, u32[]{:S(2)}) collective-permute-start(bf16[16,2048]{1,0:T(8,128)(2,1)S(1)} %get-tuple-element.50), channel_id=1, source_target_pairs={{0,24},{1,9},{8,16},{9,1},{16,8},{17,25},{24,0},{25,17},{64,88},{6... | collective-permute-start | bytes 196616 | tf_op jit(solution)/shard_map/ppermute | solution.py:39
  72.6 1.7 %collective-permute-done.22 = bf16[16,2048]{1,0:T(8,128)(2,1)S(1)} collective-permute-done((bf16[16,2048]{1,0:T(8,128)(2,1)S(1)}, bf16[16,2048]{1,0:T(8,128)(2,1)S(1)}, u32[]{:S(2)}, u32[]{:S(2)}) %collective-permute-start.22) | collective-permute-done | bytes 65568 | tf_op jit(solution)/shard_map/ppermute | solution.py:39
  75.5 2.0 %collective-permute-done.20 = bf16[16,2048]{1,0:T(8,128)(2,1)S(1)} collective-permute-done((bf16[16,2048]{1,0:T(8,128)(2,1)S(1)}, bf16[16,2048]{1,0:T(8,128)(2,1)S(1)}, u32[]{:S(2)}, u32[]{:S(2)}) %collective-permute-start.20) | collective-permute-done | bytes 65568 | tf_op jit(solution)/shard_map/ppermute | solution.py:39
  78.5 4.0 %collective-permute-start.24 = (bf16[64,2048]{1,0:T(8,128)(2,1)S(1)}, bf16[64,2048]{1,0:T(8,128)(2,1)S(1)}, u32[]{:S(2)}, u32[]{:S(2)}) collective-permute-start(bf16[64,2048]{1,0:T(8,128)(2,1)S(1)} %bitcast.12), channel_id=1, source_target_pairs={{0,64},{1,193},{8,72},{9,201},{16,80},{17,209},{24,88},{25,217},{6... | collective-permute-start | bytes 786440 | tf_op jit(solution)/shard_map/ppermute | solution.py:39
  82.4 2.5 %collective-permute-done.25 = bf16[64,2048]{1,0:T(8,128)(2,1)S(1)} collective-permute-done((bf16[64,2048]{1,0:T(8,128)(2,1)S(1)}, bf16[64,2048]{1,0:T(8,128)(2,1)S(1)}, u32[]{:S(2)}, u32[]{:S(2)}) %collective-permute-start.25) | collective-permute-done | bytes 262176 | tf_op jit(solution)/shard_map/ppermute | solution.py:39
  84.9 4.7 %collective-permute-done.24 = bf16[64,2048]{1,0:T(8,128)(2,1)S(1)} collective-permute-done((bf16[64,2048]{1,0:T(8,128)(2,1)S(1)}, bf16[64,2048]{1,0:T(8,128)(2,1)S(1)}, u32[]{:S(2)}, u32[]{:S(2)}) %collective-permute-start.24) | collective-permute-done | bytes 262176 | tf_op jit(solution)/shard_map/ppermute | solution.py:39
  90.0 1.9 %collective-permute-done.26.arrived_ref = bf16[256,1024]{1,0:T(8,128)(2,1)S(1)} collective-permute-done((bf16[256,1024]{1,0:T(8,128)(2,1)S(1)}, bf16[256,1024]{1,0:T(8,128)(2,1)S(1)}, u32[]{:S(2)}, u32[]{:S(2)}) %collective-permute-start.26) | collective-permute-done | bytes 524320 | tf_op jit(solution)/shard_map/ppermute | solution.py:28
  91.9 1.3 shard_map.53
  93.4 1.3 shard_map.52.own_ref
  95.8 1.8 %collective-permute-start.33 = (bf16[256,256]{1,0:T(8,128)(2,1)S(1)}, bf16[256,256]{1,0:T(8,128)(2,1)S(1)}, u32[]{:S(2)}, u32[]{:S(2)}) collective-permute-start(bf16[256,256]{1,0:T(8,128)(2,1)S(1)} %get-tuple-element.45), channel_id=1, source_target_pairs={{0,2},{2,0},{4,6},{6,4},{1,3},{3,1},{5,7},{7,5},{8,10},{10,8},{12,... | collective-permute-start | bytes 393224 | tf_op jit(solution)/shard_map/ppermute | solution.py:28
  97.5 4.2 %collective-permute-done.28.got_ref = bf16[256,256]{1,0:T(8,128)(2,1)S(1)} collective-permute-done((bf16[256,256]{1,0:T(8,128)(2,1)S(1)}, bf16[256,256]{1,0:T(8,128)(2,1)S(1)}, u32[]{:S(2)}, u32[]{:S(2)}) %collective-permute-start.28) | collective-permute-done | bytes 131104 | tf_op jit(solution)/shard_map/ppermute | solution.py:28
  101.7 2.0 %collective-permute-start.29 = (bf16[256,256]{1,0:T(8,128)(2,1)S(1)}, bf16[256,256]{1,0:T(8,128)(2,1)S(1)}, u32[]{:S(2)}, u32[]{:S(2)}) collective-permute-start(bf16[256,256]{1,0:T(8,128)(2,1)S(1)} %get-tuple-element.43), channel_id=1, source_target_pairs={{0,4},{2,6},{4,0},{6,2},{1,5},{3,7},{5,1},{7,3},{8,12},{10,14},{12... | collective-permute-start | bytes 393224 | tf_op jit(solution)/shard_map/ppermute | solution.py:28
  103.8 3.0 %collective-permute-start.34 = (bf16[256,256]{1,0:T(8,128)(2,1)S(1)}, bf16[256,256]{1,0:T(8,128)(2,1)S(1)}, u32[]{:S(2)}, u32[]{:S(2)}) collective-permute-start(bf16[256,256]{1,0:T(8,128)(2,1)S(1)} %get-tuple-element.47), channel_id=1, source_target_pairs={{0,4},{2,6},{4,0},{6,2},{1,5},{3,7},{5,1},{7,3},{8,12},{10,14},{12... | collective-permute-start | bytes 393224 | tf_op jit(solution)/shard_map/ppermute | solution.py:28
  106.8 7.0 %collective-permute-done.29.got_ref = bf16[256,256]{1,0:T(8,128)(2,1)S(1)} collective-permute-done((bf16[256,256]{1,0:T(8,128)(2,1)S(1)}, bf16[256,256]{1,0:T(8,128)(2,1)S(1)}, u32[]{:S(2)}, u32[]{:S(2)}) %collective-permute-start.29) | collective-permute-done | bytes 131104 | tf_op jit(solution)/shard_map/ppermute | solution.py:28
  113.9 1.3 collective-permute-done.34.got_ref
  116.0 3.3 %collective-permute-done.30.refs_3_ = bf16[256,256]{1,0:T(8,128)(2,1)S(1)} collective-permute-done((bf16[256,256]{1,0:T(8,128)(2,1)S(1)}, bf16[256,256]{1,0:T(8,128)(2,1)S(1)}, u32[]{:S(2)}, u32[]{:S(2)}) %collective-permute-start.30) | collective-permute-done | bytes 131104 | tf_op jit(solution)/shard_map/ppermute | solution.py:28
  120.7 1.3 shard_map.57.refs_0_
  122.1 1.4 shard_map.61
  124.1 1.5 collective-permute-done.38
  125.9 2.8 %collective-permute-start.41 = (bf16[64,2048]{1,0:T(8,128)(2,1)S(1)}, bf16[64,2048]{1,0:T(8,128)(2,1)S(1)}, u32[]{:S(2)}, u32[]{:S(2)}) collective-permute-start(bf16[64,2048]{1,0:T(8,128)(2,1)S(1)} %get-tuple-element.55), channel_id=1, source_target_pairs={{0,64},{1,193},{8,72},{9,201},{16,80},{17,209},{24,88},{25,217},{6... | collective-permute-start | bytes 786440 | tf_op jit(solution)/shard_map/ppermute | solution.py:39
  129.2 3.9 %collective-permute-done.39 = bf16[64,2048]{1,0:T(8,128)(2,1)S(1)} collective-permute-done((bf16[64,2048]{1,0:T(8,128)(2,1)S(1)}, bf16[64,2048]{1,0:T(8,128)(2,1)S(1)}, u32[]{:S(2)}, u32[]{:S(2)}) %collective-permute-start.39) | collective-permute-done | bytes 262176 | tf_op jit(solution)/shard_map/ppermute | solution.py:39
  133.1 2.7 %collective-permute-done.41 = bf16[64,2048]{1,0:T(8,128)(2,1)S(1)} collective-permute-done((bf16[64,2048]{1,0:T(8,128)(2,1)S(1)}, bf16[64,2048]{1,0:T(8,128)(2,1)S(1)}, u32[]{:S(2)}, u32[]{:S(2)}) %collective-permute-start.41) | collective-permute-done | bytes 262176 | tf_op jit(solution)/shard_map/ppermute | solution.py:39
  136.0 4.6 %collective-permute-start.42 = (f32[16,2048]{1,0:T(8,128)S(1)}, f32[16,2048]{1,0:T(8,128)S(1)}, u32[]{:S(2)}, u32[]{:S(2)}) collective-permute-start(f32[16,2048]{1,0:T(8,128)S(1)} %get-tuple-element.62), channel_id=1, source_target_pairs={{0,216},{1,73},{8,208},{9,65},{16,200},{17,89},{24,192},{25,81},{6... | collective-permute-start | bytes 393224 | tf_op jit(solution)/shard_map/ppermute | solution.py:39
  141.2 2.3 %collective-permute-done.42 = f32[16,2048]{1,0:T(8,128)S(1)} collective-permute-done((f32[16,2048]{1,0:T(8,128)S(1)}, f32[16,2048]{1,0:T(8,128)S(1)}, u32[]{:S(2)}, u32[]{:S(2)}) %collective-permute-start.42) | collective-permute-done | bytes 131104 | tf_op jit(solution)/shard_map/ppermute | solution.py:39
  143.5 3.2 %collective-permute-done.44 = f32[16,2048]{1,0:T(8,128)S(1)} collective-permute-done((f32[16,2048]{1,0:T(8,128)S(1)}, f32[16,2048]{1,0:T(8,128)S(1)}, u32[]{:S(2)}, u32[]{:S(2)}) %collective-permute-start.44) | collective-permute-done | bytes 131104 | tf_op jit(solution)/shard_map/ppermute | solution.py:39
  146.8 5.7 %collective-permute-start.45 = (f32[8,2048]{1,0:T(8,128)S(1)}, f32[8,2048]{1,0:T(8,128)S(1)}, u32[]{:S(2)}, u32[]{:S(2)}) collective-permute-start(f32[8,2048]{1,0:T(8,128)S(1)} %constant_dynamic-slice_fusion.1), channel_id=1, source_target_pairs={{0,32},{32,0},{1,33},{33,1},{2,34},{34,2},{3,35},{35,3},{4,36},{36... | collective-permute-start | bytes 196616 | tf_op jit(solution)/shard_map/ppermute | solution.py:28
  152.5 2.9 %collective-permute-done.45 = f32[8,2048]{1,0:T(8,128)S(1)} collective-permute-done((f32[8,2048]{1,0:T(8,128)S(1)}, f32[8,2048]{1,0:T(8,128)S(1)}, u32[]{:S(2)}, u32[]{:S(2)}) %collective-permute-start.45) | collective-permute-done | bytes 65568 | tf_op jit(solution)/shard_map/ppermute | solution.py:28
  (89 shorter events, 19.6 us)
Async XLA Ops:
  4.5 2.0 %collective-permute-start = (bf16[1024,256]{1,0:T(8,128)(2,1)S(1)}, bf16[1024,256]{1,0:T(8,128)(2,1)S(1)}, u32[]{:S(2)}, u32[]{:S(2)}) collective-permute-start(bf16[1024,256]{1,0:T(8,128)(2,1)S(1)} %get-tuple-element.29), channel_id=1, source_target_pairs={{0,1},{1,0},{2,3},{3,2},{4,5},{5,4},{6,7},{7,6},{8,9},{9,8},{10,11... | collective-permute-start | bytes 1572872 | tf_op jit(solution)/shard_map/ppermute | solution.py:28
  6.5 6.4 %collective-permute-start.1 = (bf16[256,256]{1,0:T(8,128)(2,1)S(1)}, bf16[256,256]{1,0:T(8,128)(2,1)S(1)}, u32[]{:S(2)}, u32[]{:S(2)}) collective-permute-start(bf16[256,256]{1,0:T(8,128)(2,1)S(1)} %get-tuple-element.31), channel_id=1, source_target_pairs={{0,2},{2,0},{4,6},{6,4},{1,3},{3,1},{5,7},{7,5},{8,10},{10,8},{12,... | collective-permute-start | bytes 393224 | tf_op jit(solution)/shard_map/ppermute | solution.py:28
  8.6 7.8 %collective-permute-start.6 = (bf16[256,256]{1,0:T(8,128)(2,1)S(1)}, bf16[256,256]{1,0:T(8,128)(2,1)S(1)}, u32[]{:S(2)}, u32[]{:S(2)}) collective-permute-start(bf16[256,256]{1,0:T(8,128)(2,1)S(1)} %get-tuple-element.35), channel_id=1, source_target_pairs={{0,2},{2,0},{4,6},{6,4},{1,3},{3,1},{5,7},{7,5},{8,10},{10,8},{12,... | collective-permute-start | bytes 393224 | tf_op jit(solution)/shard_map/ppermute | solution.py:28
  13.0 12.6 %collective-permute-start.2 = (bf16[256,256]{1,0:T(8,128)(2,1)S(1)}, bf16[256,256]{1,0:T(8,128)(2,1)S(1)}, u32[]{:S(2)}, u32[]{:S(2)}) collective-permute-start(bf16[256,256]{1,0:T(8,128)(2,1)S(1)} %get-tuple-element.33), channel_id=1, source_target_pairs={{0,4},{2,6},{4,0},{6,2},{1,5},{3,7},{5,1},{7,3},{8,12},{10,14},{12... | collective-permute-start | bytes 393224 | tf_op jit(solution)/shard_map/ppermute | solution.py:28
  16.4 11.1 %collective-permute-start.7 = (bf16[256,256]{1,0:T(8,128)(2,1)S(1)}, bf16[256,256]{1,0:T(8,128)(2,1)S(1)}, u32[]{:S(2)}, u32[]{:S(2)}) collective-permute-start(bf16[256,256]{1,0:T(8,128)(2,1)S(1)} %get-tuple-element.37), channel_id=1, source_target_pairs={{0,4},{2,6},{4,0},{6,2},{1,5},{3,7},{5,1},{7,3},{8,12},{10,14},{12... | collective-permute-start | bytes 393224 | tf_op jit(solution)/shard_map/ppermute | solution.py:28
  25.6 6.4 %collective-permute-start.3 = (bf16[256,256]{1,0:T(8,128)(2,1)S(1)}, bf16[256,256]{1,0:T(8,128)(2,1)S(1)}, u32[]{:S(2)}, u32[]{:S(2)}) collective-permute-start(bf16[256,256]{1,0:T(8,128)(2,1)S(1)} %shard_map.45.refs_2_), channel_id=1, source_target_pairs={{0,2},{2,0},{4,6},{6,4},{1,3},{3,1},{5,7},{7,5},{8,10},{10,8},{12,... | collective-permute-start | bytes 393224 | tf_op jit(solution)/shard_map/ppermute | solution.py:28
  27.5 5.9 %collective-permute-start.8 = (bf16[256,256]{1,0:T(8,128)(2,1)S(1)}, bf16[256,256]{1,0:T(8,128)(2,1)S(1)}, u32[]{:S(2)}, u32[]{:S(2)}) collective-permute-start(bf16[256,256]{1,0:T(8,128)(2,1)S(1)} %shard_map.49.refs_3_), channel_id=1, source_target_pairs={{0,2},{2,0},{4,6},{6,4},{1,3},{3,1},{5,7},{7,5},{8,10},{10,8},{12,... | collective-permute-start | bytes 393224 | tf_op jit(solution)/shard_map/ppermute | solution.py:28
  28.1 5.3 %collective-permute-start.4 = (bf16[256,256]{1,0:T(8,128)(2,1)S(1)}, bf16[256,256]{1,0:T(8,128)(2,1)S(1)}, u32[]{:S(2)}, u32[]{:S(2)}) collective-permute-start(bf16[256,256]{1,0:T(8,128)(2,1)S(1)} %shard_map.45.refs_2_), channel_id=1, source_target_pairs={{0,1},{1,0},{2,3},{3,2},{4,5},{5,4},{6,7},{7,6},{8,9},{9,8},{10,11... | collective-permute-start | bytes 393224 | tf_op jit(solution)/shard_map/ppermute | solution.py:28
  32.0 1.4 collective-permute-start.5
  32.0 2.7 %collective-permute-start.9 = (bf16[256,256]{1,0:T(8,128)(2,1)S(1)}, bf16[256,256]{1,0:T(8,128)(2,1)S(1)}, u32[]{:S(2)}, u32[]{:S(2)}) collective-permute-start(bf16[256,256]{1,0:T(8,128)(2,1)S(1)} %shard_map.49.refs_3_), channel_id=1, source_target_pairs={{0,1},{1,0},{2,3},{3,2},{4,5},{5,4},{6,7},{7,6},{8,9},{9,8},{10,11... | collective-permute-start | bytes 393224 | tf_op jit(solution)/shard_map/ppermute | solution.py:28
  33.4 1.3 collective-permute-start.10
  36.1 2.1 %collective-permute-start.11 = (bf16[256,1024]{1,0:T(8,128)(2,1)S(1)}, bf16[256,1024]{1,0:T(8,128)(2,1)S(1)}, u32[]{:S(2)}, u32[]{:S(2)}) collective-permute-start(bf16[256,1024]{1,0:T(8,128)(2,1)S(1)} %get-tuple-element.39), channel_id=1, source_target_pairs={{0,1},{1,0},{2,3},{3,2},{4,5},{5,4},{6,7},{7,6},{8,9},{9,8},{10,11... | collective-permute-start | bytes 1572872 | tf_op jit(solution)/shard_map/ppermute | solution.py:28
  38.3 7.5 %collective-permute-start.12 = (bf16[64,2048]{1,0:T(8,128)(2,1)S(1)}, bf16[64,2048]{1,0:T(8,128)(2,1)S(1)}, u32[]{:S(2)}, u32[]{:S(2)}) collective-permute-start(bf16[64,2048]{1,0:T(8,128)(2,1)S(1)} %get-tuple-element.59), channel_id=1, source_target_pairs={{0,72},{1,217},{8,64},{9,209},{16,88},{17,201},{24,80},{25,193},{6... | collective-permute-start | bytes 786440 | tf_op jit(solution)/shard_map/ppermute | solution.py:39
  39.8 8.2 %collective-permute-start.14 = (bf16[64,2048]{1,0:T(8,128)(2,1)S(1)}, bf16[64,2048]{1,0:T(8,128)(2,1)S(1)}, u32[]{:S(2)}, u32[]{:S(2)}) collective-permute-start(bf16[64,2048]{1,0:T(8,128)(2,1)S(1)} %get-tuple-element.60), channel_id=1, source_target_pairs={{0,64},{1,193},{8,72},{9,201},{16,80},{17,209},{24,88},{25,217},{6... | collective-permute-start | bytes 786440 | tf_op jit(solution)/shard_map/ppermute | solution.py:39
  40.8 7.7 %collective-permute-start.13 = (bf16[64,2048]{1,0:T(8,128)(2,1)S(1)}, bf16[64,2048]{1,0:T(8,128)(2,1)S(1)}, u32[]{:S(2)}, u32[]{:S(2)}) collective-permute-start(bf16[64,2048]{1,0:T(8,128)(2,1)S(1)} %get-tuple-element.61), channel_id=1, source_target_pairs={{0,8},{1,25},{8,0},{9,17},{16,24},{17,9},{24,16},{25,1},{64,72},{6... | collective-permute-start | bytes 786440 | tf_op jit(solution)/shard_map/ppermute | solution.py:39
  48.7 7.2 %collective-permute-start.15 = (f32[16,2048]{1,0:T(8,128)S(1)}, f32[16,2048]{1,0:T(8,128)S(1)}, u32[]{:S(2)}, u32[]{:S(2)}) collective-permute-start(f32[16,2048]{1,0:T(8,128)S(1)} %get-tuple-element.65), channel_id=1, source_target_pairs={{0,216},{1,73},{8,208},{9,65},{16,200},{17,89},{24,192},{25,81},{6... | collective-permute-start | bytes 393224 | tf_op jit(solution)/shard_map/ppermute | solution.py:39
  52.5 6.2 %collective-permute-start.17 = (f32[16,2048]{1,0:T(8,128)S(1)}, f32[16,2048]{1,0:T(8,128)S(1)}, u32[]{:S(2)}, u32[]{:S(2)}) collective-permute-start(f32[16,2048]{1,0:T(8,128)S(1)} %get-tuple-element.66), channel_id=1, source_target_pairs={{0,192},{1,65},{8,200},{9,73},{16,208},{17,81},{24,216},{25,89},{6... | collective-permute-start | bytes 393224 | tf_op jit(solution)/shard_map/ppermute | solution.py:39
  53.0 5.7 %collective-permute-start.16 = (f32[16,2048]{1,0:T(8,128)S(1)}, f32[16,2048]{1,0:T(8,128)S(1)}, u32[]{:S(2)}, u32[]{:S(2)}) collective-permute-start(f32[16,2048]{1,0:T(8,128)S(1)} %get-tuple-element.67), channel_id=1, source_target_pairs={{0,24},{1,9},{8,16},{9,1},{16,8},{17,25},{24,0},{25,17},{64,88},{6... | collective-permute-start | bytes 393224 | tf_op jit(solution)/shard_map/ppermute | solution.py:39
  58.8 9.0 %collective-permute-start.18 = (bf16[16,2048]{1,0:T(8,128)(2,1)S(1)}, bf16[16,2048]{1,0:T(8,128)(2,1)S(1)}, u32[]{:S(2)}, u32[]{:S(2)}) collective-permute-start(bf16[16,2048]{1,0:T(8,128)(2,1)S(1)} %get-tuple-element.52), channel_id=1, source_target_pairs={{0,32},{32,0},{1,33},{33,1},{2,34},{34,2},{3,35},{35,3},{4,36},{36... | collective-permute-start | bytes 196616 | tf_op jit(solution)/shard_map/ppermute | solution.py:28
  67.8 6.5 %collective-permute-start.22 = (bf16[16,2048]{1,0:T(8,128)(2,1)S(1)}, bf16[16,2048]{1,0:T(8,128)(2,1)S(1)}, u32[]{:S(2)}, u32[]{:S(2)}) collective-permute-start(bf16[16,2048]{1,0:T(8,128)(2,1)S(1)} %get-tuple-element.50), channel_id=1, source_target_pairs={{0,216},{1,73},{8,208},{9,65},{16,200},{17,89},{24,192},{25,81},{6... | collective-permute-start | bytes 196616 | tf_op jit(solution)/shard_map/ppermute | solution.py:39
  69.6 5.9 %collective-permute-start.21 = (bf16[16,2048]{1,0:T(8,128)(2,1)S(1)}, bf16[16,2048]{1,0:T(8,128)(2,1)S(1)}, u32[]{:S(2)}, u32[]{:S(2)}) collective-permute-start(bf16[16,2048]{1,0:T(8,128)(2,1)S(1)} %get-tuple-element.50), channel_id=1, source_target_pairs={{0,192},{1,65},{8,200},{9,73},{16,208},{17,81},{24,216},{25,89},{6... | collective-permute-start | bytes 196616 | tf_op jit(solution)/shard_map/ppermute | solution.py:39
  70.4 7.1 %collective-permute-start.20 = (bf16[16,2048]{1,0:T(8,128)(2,1)S(1)}, bf16[16,2048]{1,0:T(8,128)(2,1)S(1)}, u32[]{:S(2)}, u32[]{:S(2)}) collective-permute-start(bf16[16,2048]{1,0:T(8,128)(2,1)S(1)} %get-tuple-element.50), channel_id=1, source_target_pairs={{0,24},{1,9},{8,16},{9,1},{16,8},{17,25},{24,0},{25,17},{64,88},{6... | collective-permute-start | bytes 196616 | tf_op jit(solution)/shard_map/ppermute | solution.py:39
  77.6 7.4 %collective-permute-start.25 = (bf16[64,2048]{1,0:T(8,128)(2,1)S(1)}, bf16[64,2048]{1,0:T(8,128)(2,1)S(1)}, u32[]{:S(2)}, u32[]{:S(2)}) collective-permute-start(bf16[64,2048]{1,0:T(8,128)(2,1)S(1)} %bitcast.11), channel_id=1, source_target_pairs={{0,72},{1,217},{8,64},{9,209},{16,88},{17,201},{24,80},{25,193},{6... | collective-permute-start | bytes 786440 | tf_op jit(solution)/shard_map/ppermute | solution.py:39
  78.5 11.2 %collective-permute-start.24 = (bf16[64,2048]{1,0:T(8,128)(2,1)S(1)}, bf16[64,2048]{1,0:T(8,128)(2,1)S(1)}, u32[]{:S(2)}, u32[]{:S(2)}) collective-permute-start(bf16[64,2048]{1,0:T(8,128)(2,1)S(1)} %bitcast.12), channel_id=1, source_target_pairs={{0,64},{1,193},{8,72},{9,201},{16,80},{17,209},{24,88},{25,217},{6... | collective-permute-start | bytes 786440 | tf_op jit(solution)/shard_map/ppermute | solution.py:39
  82.4 7.2 %collective-permute-start.23 = (bf16[64,2048]{1,0:T(8,128)(2,1)S(1)}, bf16[64,2048]{1,0:T(8,128)(2,1)S(1)}, u32[]{:S(2)}, u32[]{:S(2)}) collective-permute-start(bf16[64,2048]{1,0:T(8,128)(2,1)S(1)} %bitcast.13), channel_id=1, source_target_pairs={{0,8},{1,25},{8,0},{9,17},{16,24},{17,9},{24,16},{25,1},{64,72},{6... | collective-permute-start | bytes 786440 | tf_op jit(solution)/shard_map/ppermute | solution.py:39
  89.9 2.0 %collective-permute-start.26 = (bf16[256,1024]{1,0:T(8,128)(2,1)S(1)}, bf16[256,1024]{1,0:T(8,128)(2,1)S(1)}, u32[]{:S(2)}, u32[]{:S(2)}) collective-permute-start(bf16[256,1024]{1,0:T(8,128)(2,1)S(1)} %get-tuple-element.57), channel_id=1, source_target_pairs={{0,1},{1,0},{2,3},{3,2},{4,5},{5,4},{6,7},{7,6},{8,9},{9,8},{10,11... | collective-permute-start | bytes 1572872 | tf_op jit(solution)/shard_map/ppermute | solution.py:28
  93.2 2.0 %collective-permute-start.27 = (bf16[1024,256]{1,0:T(8,128)(2,1)S(1)}, bf16[1024,256]{1,0:T(8,128)(2,1)S(1)}, u32[]{:S(2)}, u32[]{:S(2)}) collective-permute-start(bf16[1024,256]{1,0:T(8,128)(2,1)S(1)} %shard_map.53), channel_id=1, source_target_pairs={{0,1},{1,0},{2,3},{3,2},{4,5},{5,4},{6,7},{7,6},{8,9},{9,8},{10,11... | collective-permute-start | bytes 1572872 | tf_op jit(solution)/shard_map/ppermute | solution.py:28
  95.3 6.4 %collective-permute-start.28 = (bf16[256,256]{1,0:T(8,128)(2,1)S(1)}, bf16[256,256]{1,0:T(8,128)(2,1)S(1)}, u32[]{:S(2)}, u32[]{:S(2)}) collective-permute-start(bf16[256,256]{1,0:T(8,128)(2,1)S(1)} %get-tuple-element.41), channel_id=1, source_target_pairs={{0,2},{2,0},{4,6},{6,4},{1,3},{3,1},{5,7},{7,5},{8,10},{10,8},{12,... | collective-permute-start | bytes 393224 | tf_op jit(solution)/shard_map/ppermute | solution.py:28
  95.8 8.0 %collective-permute-start.33 = (bf16[256,256]{1,0:T(8,128)(2,1)S(1)}, bf16[256,256]{1,0:T(8,128)(2,1)S(1)}, u32[]{:S(2)}, u32[]{:S(2)}) collective-permute-start(bf16[256,256]{1,0:T(8,128)(2,1)S(1)} %get-tuple-element.45), channel_id=1, source_target_pairs={{0,2},{2,0},{4,6},{6,4},{1,3},{3,1},{5,7},{7,5},{8,10},{10,8},{12,... | collective-permute-start | bytes 393224 | tf_op jit(solution)/shard_map/ppermute | solution.py:28
  101.7 12.0 %collective-permute-start.29 = (bf16[256,256]{1,0:T(8,128)(2,1)S(1)}, bf16[256,256]{1,0:T(8,128)(2,1)S(1)}, u32[]{:S(2)}, u32[]{:S(2)}) collective-permute-start(bf16[256,256]{1,0:T(8,128)(2,1)S(1)} %get-tuple-element.43), channel_id=1, source_target_pairs={{0,4},{2,6},{4,0},{6,2},{1,5},{3,7},{5,1},{7,3},{8,12},{10,14},{12... | collective-permute-start | bytes 393224 | tf_op jit(solution)/shard_map/ppermute | solution.py:28
  103.8 11.4 %collective-permute-start.34 = (bf16[256,256]{1,0:T(8,128)(2,1)S(1)}, bf16[256,256]{1,0:T(8,128)(2,1)S(1)}, u32[]{:S(2)}, u32[]{:S(2)}) collective-permute-start(bf16[256,256]{1,0:T(8,128)(2,1)S(1)} %get-tuple-element.47), channel_id=1, source_target_pairs={{0,4},{2,6},{4,0},{6,2},{1,5},{3,7},{5,1},{7,3},{8,12},{10,14},{12... | collective-permute-start | bytes 393224 | tf_op jit(solution)/shard_map/ppermute | solution.py:28
  113.8 5.5 %collective-permute-start.30 = (bf16[256,256]{1,0:T(8,128)(2,1)S(1)}, bf16[256,256]{1,0:T(8,128)(2,1)S(1)}, u32[]{:S(2)}, u32[]{:S(2)}) collective-permute-start(bf16[256,256]{1,0:T(8,128)(2,1)S(1)} %shard_map.56.refs_2_), channel_id=1, source_target_pairs={{0,2},{2,0},{4,6},{6,4},{1,3},{3,1},{5,7},{7,5},{8,10},{10,8},{12,... | collective-permute-start | bytes 393224 | tf_op jit(solution)/shard_map/ppermute | solution.py:28
  115.2 5.5 %collective-permute-start.35 = (bf16[256,256]{1,0:T(8,128)(2,1)S(1)}, bf16[256,256]{1,0:T(8,128)(2,1)S(1)}, u32[]{:S(2)}, u32[]{:S(2)}) collective-permute-start(bf16[256,256]{1,0:T(8,128)(2,1)S(1)} %shard_map.60.refs_3_), channel_id=1, source_target_pairs={{0,2},{2,0},{4,6},{6,4},{1,3},{3,1},{5,7},{7,5},{8,10},{10,8},{12,... | collective-permute-start | bytes 393224 | tf_op jit(solution)/shard_map/ppermute | solution.py:28
  116.0 4.7 %collective-permute-start.31 = (bf16[256,256]{1,0:T(8,128)(2,1)S(1)}, bf16[256,256]{1,0:T(8,128)(2,1)S(1)}, u32[]{:S(2)}, u32[]{:S(2)}) collective-permute-start(bf16[256,256]{1,0:T(8,128)(2,1)S(1)} %shard_map.56.refs_2_), channel_id=1, source_target_pairs={{0,1},{1,0},{2,3},{3,2},{4,5},{5,4},{6,7},{7,6},{8,9},{9,8},{10,11... | collective-permute-start | bytes 393224 | tf_op jit(solution)/shard_map/ppermute | solution.py:28
  119.3 1.4 collective-permute-start.32
  119.3 2.7 %collective-permute-start.36 = (bf16[256,256]{1,0:T(8,128)(2,1)S(1)}, bf16[256,256]{1,0:T(8,128)(2,1)S(1)}, u32[]{:S(2)}, u32[]{:S(2)}) collective-permute-start(bf16[256,256]{1,0:T(8,128)(2,1)S(1)} %shard_map.60.refs_3_), channel_id=1, source_target_pairs={{0,1},{1,0},{2,3},{3,2},{4,5},{5,4},{6,7},{7,6},{8,9},{9,8},{10,11... | collective-permute-start | bytes 393224 | tf_op jit(solution)/shard_map/ppermute | solution.py:28
  120.7 1.3 collective-permute-start.37
  123.4 2.1 %collective-permute-start.38 = (bf16[256,1024]{1,0:T(8,128)(2,1)S(1)}, bf16[256,1024]{1,0:T(8,128)(2,1)S(1)}, u32[]{:S(2)}, u32[]{:S(2)}) collective-permute-start(bf16[256,1024]{1,0:T(8,128)(2,1)S(1)} %get-tuple-element.49), channel_id=1, source_target_pairs={{0,1},{1,0},{2,3},{3,2},{4,5},{5,4},{6,7},{7,6},{8,9},{9,8},{10,11... | collective-permute-start | bytes 1572872 | tf_op jit(solution)/shard_map/ppermute | solution.py:28
  125.7 7.4 %collective-permute-start.39 = (bf16[64,2048]{1,0:T(8,128)(2,1)S(1)}, bf16[64,2048]{1,0:T(8,128)(2,1)S(1)}, u32[]{:S(2)}, u32[]{:S(2)}) collective-permute-start(bf16[64,2048]{1,0:T(8,128)(2,1)S(1)} %get-tuple-element.54), channel_id=1, source_target_pairs={{0,72},{1,217},{8,64},{9,209},{16,88},{17,201},{24,80},{25,193},{6... | collective-permute-start | bytes 786440 | tf_op jit(solution)/shard_map/ppermute | solution.py:39
  125.9 9.9 %collective-permute-start.41 = (bf16[64,2048]{1,0:T(8,128)(2,1)S(1)}, bf16[64,2048]{1,0:T(8,128)(2,1)S(1)}, u32[]{:S(2)}, u32[]{:S(2)}) collective-permute-start(bf16[64,2048]{1,0:T(8,128)(2,1)S(1)} %get-tuple-element.55), channel_id=1, source_target_pairs={{0,64},{1,193},{8,72},{9,201},{16,80},{17,209},{24,88},{25,217},{6... | collective-permute-start | bytes 786440 | tf_op jit(solution)/shard_map/ppermute | solution.py:39
  128.6 7.2 %collective-permute-start.40 = (bf16[64,2048]{1,0:T(8,128)(2,1)S(1)}, bf16[64,2048]{1,0:T(8,128)(2,1)S(1)}, u32[]{:S(2)}, u32[]{:S(2)}) collective-permute-start(bf16[64,2048]{1,0:T(8,128)(2,1)S(1)} %get-tuple-element.56), channel_id=1, source_target_pairs={{0,8},{1,25},{8,0},{9,17},{16,24},{17,9},{24,16},{25,1},{64,72},{6... | collective-permute-start | bytes 786440 | tf_op jit(solution)/shard_map/ppermute | solution.py:39
  136.0 7.5 %collective-permute-start.42 = (f32[16,2048]{1,0:T(8,128)S(1)}, f32[16,2048]{1,0:T(8,128)S(1)}, u32[]{:S(2)}, u32[]{:S(2)}) collective-permute-start(f32[16,2048]{1,0:T(8,128)S(1)} %get-tuple-element.62), channel_id=1, source_target_pairs={{0,216},{1,73},{8,208},{9,65},{16,200},{17,89},{24,192},{25,81},{6... | collective-permute-start | bytes 393224 | tf_op jit(solution)/shard_map/ppermute | solution.py:39
  140.6 6.2 %collective-permute-start.44 = (f32[16,2048]{1,0:T(8,128)S(1)}, f32[16,2048]{1,0:T(8,128)S(1)}, u32[]{:S(2)}, u32[]{:S(2)}) collective-permute-start(f32[16,2048]{1,0:T(8,128)S(1)} %get-tuple-element.63), channel_id=1, source_target_pairs={{0,192},{1,65},{8,200},{9,73},{16,208},{17,81},{24,216},{25,89},{6... | collective-permute-start | bytes 393224 | tf_op jit(solution)/shard_map/ppermute | solution.py:39
  140.6 6.2 %collective-permute-start.43 = (f32[16,2048]{1,0:T(8,128)S(1)}, f32[16,2048]{1,0:T(8,128)S(1)}, u32[]{:S(2)}, u32[]{:S(2)}) collective-permute-start(f32[16,2048]{1,0:T(8,128)S(1)} %get-tuple-element.64), channel_id=1, source_target_pairs={{0,24},{1,9},{8,16},{9,1},{16,8},{17,25},{24,0},{25,17},{64,88},{6... | collective-permute-start | bytes 393224 | tf_op jit(solution)/shard_map/ppermute | solution.py:39
  146.8 8.6 %collective-permute-start.45 = (f32[8,2048]{1,0:T(8,128)S(1)}, f32[8,2048]{1,0:T(8,128)S(1)}, u32[]{:S(2)}, u32[]{:S(2)}) collective-permute-start(f32[8,2048]{1,0:T(8,128)S(1)} %constant_dynamic-slice_fusion.1), channel_id=1, source_target_pairs={{0,32},{32,0},{1,33},{33,1},{2,34},{34,2},{3,35},{35,3},{4,36},{36... | collective-permute-start | bytes 196616 | tf_op jit(solution)/shard_map/ppermute | solution.py:28
  152.5 3.0 %collective-permute-start.19 = (f32[8,1024]{1,0:T(8,128)S(1)}, f32[8,1024]{1,0:T(8,128)S(1)}, u32[]{:S(2)}, u32[]{:S(2)}) collective-permute-start(f32[8,1024]{1,0:T(8,128)S(1)} %get-tuple-element.69), channel_id=1, source_target_pairs={{0,1},{1,0},{2,3},{3,2},{4,5},{5,4},{6,7},{7,6},{8,9},{9,8},{10,11... | collective-permute-start | bytes 98312 | tf_op jit(solution)/shard_map/ppermute | solution.py:28
  155.4 1.3 collective-permute-start.46

commit v2 on v1

v2 whole, which is shorter than its diff:
```python
import jax
import jax.numpy as jnp
from jax import lax
from jax.experimental import pallas as pl
from jax.experimental.pallas import tpu as pltpu
from jax.sharding import Mesh, PartitionSpec as P

SIZES = {"x": 4, "h": 2, "y": 4, "z": 4, "c": 2}
F32, BF16 = jnp.float32, jnp.bfloat16
VMEM = pl.BlockSpec(memory_space=pltpu.VMEM)
TILE = 512

ROWS = 16
PIECES = 2


def dot(a, b, dim_a, dim_b):
    return lax.dot_general(
        a, b, (((dim_a,), (dim_b,)), ((), ())), preferred_element_type=F32
    )


def swap(value, axis, mask):
    return lax.ppermute(value, axis, [(i, i ^ mask) for i in range(SIZES[axis])])


def swap_xy(value, stage, bits):
    pairs = []
    for x in range(4):
        for y in range(4):
            for c in range(2):
                to = (x ^ bits) * 4 + y if c == stage else x * 4 + (y ^ bits)
                pairs.append(((x * 4 + y) * 2 + c, to * 2 + c))
    return lax.ppermute(value, ("x", "y", "c"), pairs)


def reduce_four(kept, given, stage):
    total = kept
    for got in [swap_xy(given[i - 1], stage, i) for i in (2, 1, 3)]:
        total = total + got.astype(F32)
    return total


def gather_four(part, stage):
    got = {i: swap_xy(part, stage, i) for i in (2, 1, 3)}
    return jnp.stack([part, got[1], got[2], got[3]])


def call(kernel, outs, *args, specs=None, scratch=(), flops=0, limit=16):
    return pl.pallas_call(
        kernel,
        in_specs=specs or [VMEM] * len(args),
        out_specs=[VMEM] * len(outs),
        out_shape=[pltpu.VMEM(shape, kind) for shape, kind in outs],
        scratch_shapes=list(scratch),
        compiler_params=pltpu.CompilerParams(vmem_limit_bytes=limit * 2**20),
        cost_estimate=pl.CostEstimate(
            flops=flops, bytes_accessed=2**20, transcendentals=0
        ),
    )(*args)


def token_rows(x_ref):
    parity = lax.rem(lax.axis_index("z"), 2)
    block = x_ref.shape[0] // (2 * PIECES)
    starts = []
    for piece in range(PIECES):
        for chip in (parity, 1 - parity):
            starts.append((chip * PIECES + piece) * block)
    return [pl.ds(pl.multiple_of(start, block), block) for start in starts]


def write_scores(x_ref, probes, s_ref):
    block = x_ref.shape[0] // (2 * PIECES)
    for i, rows in enumerate(token_rows(x_ref)):
        value = dot(x_ref[rows], probes, 1, 1)
        s_ref[pl.ds(i * block, block)] = value.astype(s_ref.dtype)


def load(activations, probes):
    tokens, features = activations.shape
    half, count = tokens // 2, probes.shape[0]

    def kernel(x_hbm, p_hbm, theirs_ref, own_ref, p_ref, s_ref, raw_ref, row_ref, sems):
        core, x, y = (lax.axis_index(name) for name in ("c", "x", "y"))

        def rows_of(c):
            return x_hbm.at[pl.ds(pl.multiple_of(c * half, half), half)]

        copies = [
            pltpu.make_async_copy(p_hbm, raw_ref, sems.at[0]),
            pltpu.make_async_copy(rows_of(1 - core), theirs_ref, sems.at[1]),
            pltpu.make_async_copy(rows_of(core), own_ref, sems.at[2]),
        ]
        for copy in copies:
            copy.start()
        copies[0].wait()
        row_ref[...] = raw_ref[...].astype(F32)
        for i in range(16):
            at_x = lax.bitwise_xor(x, i // 4)
            at_y = lax.bitwise_xor(y, i % 4)
            pair = [
                row_ref[pl.ds(pl.multiple_of(at_x * 64 + h * 32 + at_y * 8, 8), 8)]
                for h in range(2)
            ]
            p_ref[pl.ds(i * ROWS, ROWS)] = jnp.concatenate(pair, 0).astype(BF16)
        copies[1].wait()
        write_scores(theirs_ref, p_ref[...], s_ref)
        copies[2].wait()

    hbm = pl.BlockSpec(memory_space=pltpu.HBM)
    return call(
        kernel,
        [((half, features), BF16)] * 2 + [(probes.shape, BF16), ((half, count), BF16)],
        activations,
        probes,
        specs=[hbm, hbm],
        scratch=[
            pltpu.VMEM(probes.shape, BF16),
            pltpu.VMEM(probes.shape, F32),
            pltpu.SemaphoreType.DMA((3,)),
        ],
        flops=tokens * features * count,
        limit=48,
    )


def score(x_half, probes, out_type):
    tokens, features = x_half.shape

    def kernel(x_ref, p_ref, s_ref):
        write_scores(x_ref, p_ref[...], s_ref)

    return call(
        kernel,
        [((tokens, probes.shape[0]), out_type)],
        x_half,
        probes,
        flops=2 * tokens * features * probes.shape[0],
    )[0]


def reorder(ref, out_ref):
    core = lax.axis_index("c")

    @pl.when(core == 0)
    def _():
        out_ref[...] = ref[...]

    @pl.when(core == 1)
    def _():
        blocks = [
            ref[pl.ds((inner * 4 + outer) * ROWS, ROWS)]
            for outer in range(4)
            for inner in range(4)
        ]
        out_ref[...] = jnp.concatenate(blocks, 0)


def in_order_a(rows):
    def kernel(rows_ref, out_ref):
        reorder(rows_ref, out_ref)

    return call(kernel, [(rows.shape, BF16)], rows, flops=2**20)[0]


def add_piece(own, theirs, piece):
    block = own.shape[0] // (2 * PIECES)
    shape = (block, own.shape[1])

    def kernel(own_ref, theirs_ref, kept_ref, given_ref):
        for i, out_ref in enumerate((kept_ref, given_ref)):
            rows = pl.ds((2 * piece + i) * block, block)
            total = own_ref[rows] + theirs_ref[rows].astype(F32)
            out_ref[...] = total.astype(out_ref.dtype)

    return call(kernel, [(shape, F32), (shape, BF16)], own, theirs, flops=2**20)


def add(kept, got, kinds):
    def kernel(kept_ref, got_ref, *out_refs):
        total = kept_ref[...] + got_ref[...].astype(F32)
        for out_ref in out_refs:
            out_ref[...] = total.astype(out_ref.dtype)

    return call(kernel, [(kept.shape, kind) for kind in kinds], kept, got, flops=2**20)


def sum_scores(theirs, own):
    theirs = swap(theirs, "c", 1)
    mine, other = [], []
    for piece in range(PIECES):
        kept, given = add_piece(own, theirs, piece)
        kept, given = add(kept, swap(given, "z", 1), (F32, BF16))
        (whole,) = add(kept, swap(given, "z", 2), (BF16,))
        arrived = swap(whole, "z", 1)
        mine += [whole, swap(whole, "c", 1)]
        other += [arrived, swap(arrived, "c", 1)]
    return mine, other


def product_term(x_refs, s_refs, share, cols):
    total = None
    for i, s_ref in enumerate(s_refs):
        x_ref = x_refs[i % 2]
        rows = token_rows(x_ref)[i // 2 * 2 + share]
        term = dot(s_ref[...], x_ref[rows, cols], 0, 0)
        total = term if total is None else total + term
    return total


def product_mine(x_own, x_theirs, scores):
    features = x_own.shape[1]
    tokens, probes = scores[0].shape

    def kernel(xo_ref, xt_ref, *refs):
        *s_refs, y_ref = refs
        for i in range(0, features, TILE):
            cols = pl.ds(i, TILE)
            y_ref[:, cols] = product_term((xo_ref, xt_ref), s_refs, 0, cols)

    return call(
        kernel,
        [((probes, features), F32)],
        x_own,
        x_theirs,
        *scores,
        flops=2 * len(scores) * tokens * features * probes,
    )[0]


def product_all(y_mine, x_own, x_theirs, scores):
    features = x_own.shape[1]
    tokens, probes = scores[0].shape

    def kernel(y_ref, xo_ref, xt_ref, *refs):
        *s_refs, kept_ref, given_ref, sum_ref, order_ref = refs
        for i in range(0, features, TILE):
            cols = pl.ds(i, TILE)
            term = product_term((xo_ref, xt_ref), s_refs, 1, cols)
            sum_ref[:, cols] = y_ref[:, cols] + term
        reorder(sum_ref, order_ref)
        kept_ref[...] = order_ref[pl.ds(0, probes // 4)]
        for i in range(3):
            rows = pl.ds((i + 1) * (probes // 4), probes // 4)
            given_ref[i] = order_ref[rows].astype(BF16)

    return call(
        kernel,
        [((probes // 4, features), F32), ((3, probes // 4, features), BF16)],
        y_mine,
        x_own,
        x_theirs,
        *scores,
        scratch=[pltpu.VMEM((probes, features), F32)] * 2,
        flops=2 * len(scores) * tokens * features * probes,
    )


def product(x_theirs, x_own, scores):
    mine, other = scores
    y = product_mine(x_own, x_theirs, mine)
    kept, given = product_all(y, x_own, x_theirs, other)
    total = reduce_four(kept, given, 0).reshape(4, ROWS, -1)
    return reduce_four(total[0], total[1:], 1)


def spread(rounded):
    part = gather_four(rounded, 1).reshape(4 * ROWS, -1)
    full = gather_four(part, 0).reshape(16 * ROWS, -1)
    return in_order_a(full)


def shards(activations, probes):
    h = lax.axis_index("h")
    total_tokens = activations.shape[0] * 32

    x_theirs, x_own, mine, theirs = load(activations, probes)
    scores = sum_scores(theirs, score(x_own, mine, F32))
    rows = product(x_theirs, x_own, scores)
    rows = (rows + swap(rows.astype(BF16), "h", 1).astype(F32)) / total_tokens
    first = lax.dynamic_slice_in_dim(rows, h * 8, 8, 0)

    full = spread(rows.astype(BF16))
    theirs = score(x_theirs, full, BF16)
    own = score(x_own, full, F32)
    rows = product(x_theirs, x_own, sum_scores(theirs, own))
    mine = lax.dynamic_slice_in_dim(rows, h * 8, 8, 0)
    other = lax.dynamic_slice_in_dim(rows, (1 - h) * 8, 8, 0)
    return first, (mine + swap(other, "h", 1)) / total_tokens


def solution(mesh):
    split = Mesh(mesh.devices.reshape(tuple(SIZES.values())), tuple(SIZES))
    tok, feat = ("x", "h", "y"), ("z", "c")
    return jax.shard_map(
        shards,
        mesh=split,
        in_specs=(P(tok, feat), P(None, feat)),
        out_specs=(P(tok, feat), P(tok, feat)),
        check_vma=False,
    )
```

time: 160 us -> 147 us (0.919)
  waiting for transfers between devices: 81.8 us -> 71.4 us
  starting transfers between devices: 58.9 us -> 56.9 us
    ppermute x29 -> x24, waiting for transfers between devices: 45.8 us -> 40.3 us  [swap(): lax.ppermute(value, axis, [(i, i ^ mask) for i in range(SIZES[axis])])]
    ppermute x18, waiting for transfers between devices: 36.1 us -> 31.2 us  [swap_xy(): return lax.ppermute(value, ('x', 'y', 'c'), pairs)]
    ppermute x29 -> x24, starting transfers between devices: 32 us -> 29.8 us  [swap(): lax.ppermute(value, axis, [(i, i ^ mask) for i in range(SIZES[axis])])]
  transfers between devices with their start and end apart: 47 -> 42, of which waited for: 32 -> 32; matrix products, arithmetic and copies ran while one was open for 0% -> 0% of each run, Pallas kernels for 3% -> 4%
where the time goes in v2:
time: 147 us; the launch traced here: 145 us
  waiting for transfers between devices  71.4 us (49%)
  starting transfers between devices  56.9 us (39%)
  Pallas kernels  13.8 us (9%)
    ppermute x24, waiting for transfers between devices, swap(): lax.ppermute(value, axis, [(i, i ^ mask) for i in range(SIZES[axis])])  40.3 us
    ppermute x18, waiting for transfers between devices, swap_xy(): return lax.ppermute(value, ('x', 'y', 'c'), pairs)  31.2 us
    ppermute x24, starting transfers between devices, swap(): lax.ppermute(value, axis, [(i, i ^ mask) for i in range(SIZES[axis])])  29.8 us
    ppermute x18, starting transfers between devices, swap_xy(): return lax.ppermute(value, ('x', 'y', 'c'), pairs)  27.1 us
    pallas_call x21, Pallas kernels, call(): pl.pallas_call(kernel, in_specs=specs or [VMEM] * len(args), out_specs=[V...  13.8 us
  transfers between devices with their start and end apart: 42, of which 32 were waited for; matrix products, arithmetic and copies ran while one was open for 0% of the time, Pallas kernels for 4%

profile of v2, /device:TPU:8, one launch (start us, length us, event | category | flops | bytes accessed | tf_op | source)
XLA Modules:
  0.0 145.0 jit_solution(12604552599457433379)
XLA Ops:
  0.6 3.8 %shard_map.41 = (bf16[1024,2048]{1,0:T(8,128)(2,1)S(1)}, bf16[1024,2048]{1,0:T(8,128)(2,1)S(1)}, bf16[256,2048]{1,0:T(8,128)(2,1)S(1)}, bf16[1024,256]{1,0:T(8,128)(2,1)S(1)}) custom-call(bf16[2048,2048]{1,0:T(8,128)(2,1)} %x_hbm.1, bf16[256,2048]{1,0:T(8,128)(2,1)} %p_hbm.1), custom_call_target="tpu_custom_call" | custom-call | flops 1073741824 | bytes 1048576 | tf_op jit(solution)/shard_map/pallas_call | solution.py:50
  4.6 1.3 shard_map.42.own_ref
  6.5 2.0 %collective-permute-start.4 = (bf16[256,256]{1,0:T(8,128)(2,1)S(1)}, bf16[256,256]{1,0:T(8,128)(2,1)S(1)}, u32[]{:S(2)}, u32[]{:S(2)}) collective-permute-start(bf16[256,256]{1,0:T(8,128)(2,1)S(1)} %get-tuple-element.35), channel_id=1, source_target_pairs={{0,2},{2,0},{4,6},{6,4},{1,3},{3,1},{5,7},{7,5},{8,10},{10,8},{12,... | collective-permute-start | bytes 393224 | tf_op jit(solution)/shard_map/ppermute | solution.py:24
  8.8 4.2 %collective-permute-done.4.got_ref = bf16[256,256]{1,0:T(8,128)(2,1)S(1)} collective-permute-done((bf16[256,256]{1,0:T(8,128)(2,1)S(1)}, bf16[256,256]{1,0:T(8,128)(2,1)S(1)}, u32[]{:S(2)}, u32[]{:S(2)}) %collective-permute-start.4) | collective-permute-done | bytes 131104 | tf_op jit(solution)/shard_map/ppermute | solution.py:24
  13.0 3.4 %collective-permute-start.5 = (bf16[256,256]{1,0:T(8,128)(2,1)S(1)}, bf16[256,256]{1,0:T(8,128)(2,1)S(1)}, u32[]{:S(2)}, u32[]{:S(2)}) collective-permute-start(bf16[256,256]{1,0:T(8,128)(2,1)S(1)} %get-tuple-element.37), channel_id=1, source_target_pairs={{0,4},{2,6},{4,0},{6,2},{1,5},{3,7},{5,1},{7,3},{8,12},{10,14},{12... | collective-permute-start | bytes 393224 | tf_op jit(solution)/shard_map/ppermute | solution.py:24
  16.4 2.8 %collective-permute-start.2 = (bf16[256,256]{1,0:T(8,128)(2,1)S(1)}, bf16[256,256]{1,0:T(8,128)(2,1)S(1)}, u32[]{:S(2)}, u32[]{:S(2)}) collective-permute-start(bf16[256,256]{1,0:T(8,128)(2,1)S(1)} %get-tuple-element.33), channel_id=1, source_target_pairs={{0,4},{2,6},{4,0},{6,2},{1,5},{3,7},{5,1},{7,3},{8,12},{10,14},{12... | collective-permute-start | bytes 393224 | tf_op jit(solution)/shard_map/ppermute | solution.py:24
  19.1 6.5 %collective-permute-done.5.got_ref = bf16[256,256]{1,0:T(8,128)(2,1)S(1)} collective-permute-done((bf16[256,256]{1,0:T(8,128)(2,1)S(1)}, bf16[256,256]{1,0:T(8,128)(2,1)S(1)}, u32[]{:S(2)}, u32[]{:S(2)}) %collective-permute-start.5) | collective-permute-done | bytes 131104 | tf_op jit(solution)/shard_map/ppermute | solution.py:24
  26.2 1.3 collective-permute-done.2.got_ref
  28.7 3.3 %collective-permute-done.9.refs_2_ = bf16[256,256]{1,0:T(8,128)(2,1)S(1)} collective-permute-done((bf16[256,256]{1,0:T(8,128)(2,1)S(1)}, bf16[256,256]{1,0:T(8,128)(2,1)S(1)}, u32[]{:S(2)}, u32[]{:S(2)}) %collective-permute-start.9) | collective-permute-done | bytes 131104 | tf_op jit(solution)/shard_map/ppermute | solution.py:24
  32.0 1.4 collective-permute-done.7.refs_0_
  33.4 1.3 shard_map.49.y_ref
  34.7 1.5 %shard_map.50 = (f32[64,2048]{1,0:T(8,128)S(1)}, bf16[3,64,2048]{2,1,0:T(8,128)(2,1)S(1)}) custom-call(f32[256,2048]{1,0:T(8,128)S(1)} %shard_map.49.y_ref, bf16[1024,2048]{1,0:T(8,128)(2,1)S(1)} %get-tuple-element.26.x_ref.xo_ref, bf16[1024,2048]{1,0:T(8,128)(2,1)S(1)} %get-tuple-element.27.xt_ref.x_ref, ...), custom_call_target="tpu_custom_call" | custom-call | flops 1073741824 | bytes 1048576 | tf_op jit(solution)/shard_map/pallas_call | solution.py:50
  36.3 3.1 %collective-permute-start.11 = (bf16[64,2048]{1,0:T(8,128)(2,1)S(1)}, bf16[64,2048]{1,0:T(8,128)(2,1)S(1)}, u32[]{:S(2)}, u32[]{:S(2)}) collective-permute-start(bf16[64,2048]{1,0:T(8,128)(2,1)S(1)} %get-tuple-element.57), channel_id=1, source_target_pairs={{0,128},{1,17},{8,136},{9,25},{16,144},{17,1},{24,152},{25,9},{64,... | collective-permute-start | bytes 786440 | tf_op jit(solution)/shard_map/ppermute | solution.py:34
  40.6 3.7 %collective-permute-done.11 = bf16[64,2048]{1,0:T(8,128)(2,1)S(1)} collective-permute-done((bf16[64,2048]{1,0:T(8,128)(2,1)S(1)}, bf16[64,2048]{1,0:T(8,128)(2,1)S(1)}, u32[]{:S(2)}, u32[]{:S(2)}) %collective-permute-start.11) | collective-permute-done | bytes 262176 | tf_op jit(solution)/shard_map/ppermute | solution.py:34
  44.3 2.8 %collective-permute-done.13 = bf16[64,2048]{1,0:T(8,128)(2,1)S(1)} collective-permute-done((bf16[64,2048]{1,0:T(8,128)(2,1)S(1)}, bf16[64,2048]{1,0:T(8,128)(2,1)S(1)}, u32[]{:S(2)}, u32[]{:S(2)}) %collective-permute-start.13) | collective-permute-done | bytes 262176 | tf_op jit(solution)/shard_map/ppermute | solution.py:34
  47.4 2.4 %collective-permute-start.14 = (f32[16,2048]{1,0:T(8,128)S(1)}, f32[16,2048]{1,0:T(8,128)S(1)}, u32[]{:S(2)}, u32[]{:S(2)}) collective-permute-start(f32[16,2048]{1,0:T(8,128)S(1)} %get-tuple-element.63), channel_id=1, source_target_pairs={{0,16},{1,129},{8,24},{9,137},{16,0},{17,145},{24,8},{25,153},{64,... | collective-permute-start | bytes 393224 | tf_op jit(solution)/shard_map/ppermute | solution.py:34
  49.8 2.4 %collective-permute-start.15 = (f32[16,2048]{1,0:T(8,128)S(1)}, f32[16,2048]{1,0:T(8,128)S(1)}, u32[]{:S(2)}, u32[]{:S(2)}) collective-permute-start(f32[16,2048]{1,0:T(8,128)S(1)} %get-tuple-element.65), channel_id=1, source_target_pairs={{0,8},{1,65},{8,0},{9,73},{16,24},{17,81},{24,16},{25,89},{64,72},... | collective-permute-start | bytes 393224 | tf_op jit(solution)/shard_map/ppermute | solution.py:34
  52.2 1.8 %collective-permute-done.14 = f32[16,2048]{1,0:T(8,128)S(1)} collective-permute-done((f32[16,2048]{1,0:T(8,128)S(1)}, f32[16,2048]{1,0:T(8,128)S(1)}, u32[]{:S(2)}, u32[]{:S(2)}) %collective-permute-start.14) | collective-permute-done | bytes 131104 | tf_op jit(solution)/shard_map/ppermute | solution.py:34
  54.0 1.3 collective-permute-done.16
  55.5 6.1 %collective-permute-start.17 = (bf16[16,2048]{1,0:T(8,128)(2,1)S(1)}, bf16[16,2048]{1,0:T(8,128)(2,1)S(1)}, u32[]{:S(2)}, u32[]{:S(2)}) collective-permute-start(bf16[16,2048]{1,0:T(8,128)(2,1)S(1)} %get-tuple-element.52), channel_id=1, source_target_pairs={{0,32},{32,0},{1,33},{33,1},{2,34},{34,2},{3,35},{35,3},{4,36},{36... | collective-permute-start | bytes 196616 | tf_op jit(solution)/shard_map/ppermute | solution.py:24
  61.7 2.3 %collective-permute-done.17 = bf16[16,2048]{1,0:T(8,128)(2,1)S(1)} collective-permute-done((bf16[16,2048]{1,0:T(8,128)(2,1)S(1)}, bf16[16,2048]{1,0:T(8,128)(2,1)S(1)}, u32[]{:S(2)}, u32[]{:S(2)}) %collective-permute-start.17) | collective-permute-done | bytes 65568 | tf_op jit(solution)/shard_map/ppermute | solution.py:24
  64.0 1.3 collective-permute-start.20
  65.4 2.6 %collective-permute-start.19 = (bf16[16,2048]{1,0:T(8,128)(2,1)S(1)}, bf16[16,2048]{1,0:T(8,128)(2,1)S(1)}, u32[]{:S(2)}, u32[]{:S(2)}) collective-permute-start(bf16[16,2048]{1,0:T(8,128)(2,1)S(1)} %get-tuple-element.50), channel_id=1, source_target_pairs={{0,16},{1,129},{8,24},{9,137},{16,0},{17,145},{24,8},{25,153},{64,... | collective-permute-start | bytes 196616 | tf_op jit(solution)/shard_map/ppermute | solution.py:34
  68.4 2.8 %collective-permute-done.19 = bf16[16,2048]{1,0:T(8,128)(2,1)S(1)} collective-permute-done((bf16[16,2048]{1,0:T(8,128)(2,1)S(1)}, bf16[16,2048]{1,0:T(8,128)(2,1)S(1)}, u32[]{:S(2)}, u32[]{:S(2)}) %collective-permute-start.19) | collective-permute-done | bytes 65568 | tf_op jit(solution)/shard_map/ppermute | solution.py:34
  72.3 4.0 %collective-permute-start.23 = (bf16[64,2048]{1,0:T(8,128)(2,1)S(1)}, bf16[64,2048]{1,0:T(8,128)(2,1)S(1)}, u32[]{:S(2)}, u32[]{:S(2)}) collective-permute-start(bf16[64,2048]{1,0:T(8,128)(2,1)S(1)} %bitcast.23), channel_id=1, source_target_pairs={{0,192},{1,25},{8,200},{9,17},{16,208},{17,9},{24,216},{25,1},{64,... | collective-permute-start | bytes 786440 | tf_op jit(solution)/shard_map/ppermute | solution.py:34
  77.3 5.7 %collective-permute-done.23 = bf16[64,2048]{1,0:T(8,128)(2,1)S(1)} collective-permute-done((bf16[64,2048]{1,0:T(8,128)(2,1)S(1)}, bf16[64,2048]{1,0:T(8,128)(2,1)S(1)}, u32[]{:S(2)}, u32[]{:S(2)}) %collective-permute-start.23) | collective-permute-done | bytes 262176 | tf_op jit(solution)/shard_map/ppermute | solution.py:34
  84.7 1.3 shard_map.53
  86.1 1.3 shard_map.52.own_ref
  88.3 2.0 %collective-permute-start.25 = (bf16[256,256]{1,0:T(8,128)(2,1)S(1)}, bf16[256,256]{1,0:T(8,128)(2,1)S(1)}, u32[]{:S(2)}, u32[]{:S(2)}) collective-permute-start(bf16[256,256]{1,0:T(8,128)(2,1)S(1)} %get-tuple-element.41), channel_id=1, source_target_pairs={{0,2},{2,0},{4,6},{6,4},{1,3},{3,1},{5,7},{7,5},{8,10},{10,8},{12,... | collective-permute-start | bytes 393224 | tf_op jit(solution)/shard_map/ppermute | solution.py:24
  90.3 4.2 %collective-permute-done.28.got_ref = bf16[256,256]{1,0:T(8,128)(2,1)S(1)} collective-permute-done((bf16[256,256]{1,0:T(8,128)(2,1)S(1)}, bf16[256,256]{1,0:T(8,128)(2,1)S(1)}, u32[]{:S(2)}, u32[]{:S(2)}) %collective-permute-start.28) | collective-permute-done | bytes 131104 | tf_op jit(solution)/shard_map/ppermute | solution.py:24
  94.5 1.8 %collective-permute-start.29 = (bf16[256,256]{1,0:T(8,128)(2,1)S(1)}, bf16[256,256]{1,0:T(8,128)(2,1)S(1)}, u32[]{:S(2)}, u32[]{:S(2)}) collective-permute-start(bf16[256,256]{1,0:T(8,128)(2,1)S(1)} %get-tuple-element.47), channel_id=1, source_target_pairs={{0,4},{2,6},{4,0},{6,2},{1,5},{3,7},{5,1},{7,3},{8,12},{10,14},{12... | collective-permute-start | bytes 393224 | tf_op jit(solution)/shard_map/ppermute | solution.py:24
  96.5 2.6 %collective-permute-start.26 = (bf16[256,256]{1,0:T(8,128)(2,1)S(1)}, bf16[256,256]{1,0:T(8,128)(2,1)S(1)}, u32[]{:S(2)}, u32[]{:S(2)}) collective-permute-start(bf16[256,256]{1,0:T(8,128)(2,1)S(1)} %get-tuple-element.43), channel_id=1, source_target_pairs={{0,4},{2,6},{4,0},{6,2},{1,5},{3,7},{5,1},{7,3},{8,12},{10,14},{12... | collective-permute-start | bytes 393224 | tf_op jit(solution)/shard_map/ppermute | solution.py:24
  99.1 7.1 %collective-permute-done.29.got_ref = bf16[256,256]{1,0:T(8,128)(2,1)S(1)} collective-permute-done((bf16[256,256]{1,0:T(8,128)(2,1)S(1)}, bf16[256,256]{1,0:T(8,128)(2,1)S(1)}, u32[]{:S(2)}, u32[]{:S(2)}) %collective-permute-start.29) | collective-permute-done | bytes 131104 | tf_op jit(solution)/shard_map/ppermute | solution.py:24
  106.3 1.6 %collective-permute-done.26.got_ref = bf16[256,256]{1,0:T(8,128)(2,1)S(1)} collective-permute-done((bf16[256,256]{1,0:T(8,128)(2,1)S(1)}, bf16[256,256]{1,0:T(8,128)(2,1)S(1)}, u32[]{:S(2)}, u32[]{:S(2)}) %collective-permute-start.26) | collective-permute-done | bytes 131104 | tf_op jit(solution)/shard_map/ppermute | solution.py:24
  109.2 3.3 %collective-permute-done.33.refs_2_ = bf16[256,256]{1,0:T(8,128)(2,1)S(1)} collective-permute-done((bf16[256,256]{1,0:T(8,128)(2,1)S(1)}, bf16[256,256]{1,0:T(8,128)(2,1)S(1)}, u32[]{:S(2)}, u32[]{:S(2)}) %collective-permute-start.33) | collective-permute-done | bytes 131104 | tf_op jit(solution)/shard_map/ppermute | solution.py:24
  112.5 1.4 collective-permute-done.31.refs_0_
  113.9 1.3 shard_map.60.y_ref
  115.3 1.5 %shard_map.61 = (f32[64,2048]{1,0:T(8,128)S(1)}, bf16[3,64,2048]{2,1,0:T(8,128)(2,1)S(1)}) custom-call(f32[256,2048]{1,0:T(8,128)S(1)} %shard_map.60.y_ref, bf16[1024,2048]{1,0:T(8,128)(2,1)S(1)} %get-tuple-element.26.x_ref.xo_ref, bf16[1024,2048]{1,0:T(8,128)(2,1)S(1)} %get-tuple-element.27.xt_ref.x_ref, ...), custom_call_target="tpu_custom_call" | custom-call | flops 1073741824 | bytes 1048576 | tf_op jit(solution)/shard_map/pallas_call | solution.py:50
  116.9 2.0 %collective-permute-start.35 = (bf16[64,2048]{1,0:T(8,128)(2,1)S(1)}, bf16[64,2048]{1,0:T(8,128)(2,1)S(1)}, u32[]{:S(2)}, u32[]{:S(2)}) collective-permute-start(bf16[64,2048]{1,0:T(8,128)(2,1)S(1)} %get-tuple-element.54), channel_id=1, source_target_pairs={{0,128},{1,17},{8,136},{9,25},{16,144},{17,1},{24,152},{25,9},{64,... | collective-permute-start | bytes 786440 | tf_op jit(solution)/shard_map/ppermute | solution.py:34
  118.8 2.1 %collective-permute-start.37 = (bf16[64,2048]{1,0:T(8,128)(2,1)S(1)}, bf16[64,2048]{1,0:T(8,128)(2,1)S(1)}, u32[]{:S(2)}, u32[]{:S(2)}) collective-permute-start(bf16[64,2048]{1,0:T(8,128)(2,1)S(1)} %get-tuple-element.55), channel_id=1, source_target_pairs={{0,192},{1,25},{8,200},{9,17},{16,208},{17,9},{24,216},{25,1},{64,... | collective-permute-start | bytes 786440 | tf_op jit(solution)/shard_map/ppermute | solution.py:34
  121.0 3.9 %collective-permute-done.35 = bf16[64,2048]{1,0:T(8,128)(2,1)S(1)} collective-permute-done((bf16[64,2048]{1,0:T(8,128)(2,1)S(1)}, bf16[64,2048]{1,0:T(8,128)(2,1)S(1)}, u32[]{:S(2)}, u32[]{:S(2)}) %collective-permute-start.35) | collective-permute-done | bytes 262176 | tf_op jit(solution)/shard_map/ppermute | solution.py:34
  124.9 2.7 %collective-permute-done.37 = bf16[64,2048]{1,0:T(8,128)(2,1)S(1)} collective-permute-done((bf16[64,2048]{1,0:T(8,128)(2,1)S(1)}, bf16[64,2048]{1,0:T(8,128)(2,1)S(1)}, u32[]{:S(2)}, u32[]{:S(2)}) %collective-permute-start.37) | collective-permute-done | bytes 262176 | tf_op jit(solution)/shard_map/ppermute | solution.py:34
  128.1 1.4 collective-permute-start.38
  129.5 1.4 collective-permute-start.40
  130.9 1.9 %collective-permute-start.39 = (f32[16,2048]{1,0:T(8,128)S(1)}, f32[16,2048]{1,0:T(8,128)S(1)}, u32[]{:S(2)}, u32[]{:S(2)}) collective-permute-start(f32[16,2048]{1,0:T(8,128)S(1)} %get-tuple-element.62), channel_id=1, source_target_pairs={{0,8},{1,65},{8,0},{9,73},{16,24},{17,81},{24,16},{25,89},{64,72},... | collective-permute-start | bytes 393224 | tf_op jit(solution)/shard_map/ppermute | solution.py:34
  132.9 1.9 %collective-permute-done.38 = f32[16,2048]{1,0:T(8,128)S(1)} collective-permute-done((f32[16,2048]{1,0:T(8,128)S(1)}, f32[16,2048]{1,0:T(8,128)S(1)}, u32[]{:S(2)}, u32[]{:S(2)}) %collective-permute-start.38) | collective-permute-done | bytes 131104 | tf_op jit(solution)/shard_map/ppermute | solution.py:34
  136.0 5.6 %collective-permute-start.41 = (f32[8,2048]{1,0:T(8,128)S(1)}, f32[8,2048]{1,0:T(8,128)S(1)}, u32[]{:S(2)}, u32[]{:S(2)}) collective-permute-start(f32[8,2048]{1,0:T(8,128)S(1)} %constant_dynamic-slice_fusion), channel_id=1, source_target_pairs={{0,32},{32,0},{1,33},{33,1},{2,34},{34,2},{3,35},{35,3},{4,36},{36... | collective-permute-start | bytes 196616 | tf_op jit(solution)/shard_map/ppermute | solution.py:24
  142.2 2.1 %collective-permute-done.41 = f32[8,2048]{1,0:T(8,128)S(1)} collective-permute-done((f32[8,2048]{1,0:T(8,128)S(1)}, f32[8,2048]{1,0:T(8,128)S(1)}, u32[]{:S(2)}, u32[]{:S(2)}) %collective-permute-start.41) | collective-permute-done | bytes 65568 | tf_op jit(solution)/shard_map/ppermute | solution.py:24
  (71 shorter events, 14.3 us)
Async XLA Ops:
  4.5 2.0 %collective-permute-start = (bf16[1024,256]{1,0:T(8,128)(2,1)S(1)}, bf16[1024,256]{1,0:T(8,128)(2,1)S(1)}, u32[]{:S(2)}, u32[]{:S(2)}) collective-permute-start(bf16[1024,256]{1,0:T(8,128)(2,1)S(1)} %get-tuple-element.29), channel_id=1, source_target_pairs={{0,1},{1,0},{2,3},{3,2},{4,5},{5,4},{6,7},{7,6},{8,9},{9,8},{10,11... | collective-permute-start | bytes 1572872 | tf_op jit(solution)/shard_map/ppermute | solution.py:24
  6.5 6.4 %collective-permute-start.4 = (bf16[256,256]{1,0:T(8,128)(2,1)S(1)}, bf16[256,256]{1,0:T(8,128)(2,1)S(1)}, u32[]{:S(2)}, u32[]{:S(2)}) collective-permute-start(bf16[256,256]{1,0:T(8,128)(2,1)S(1)} %get-tuple-element.35), channel_id=1, source_target_pairs={{0,2},{2,0},{4,6},{6,4},{1,3},{3,1},{5,7},{7,5},{8,10},{10,8},{12,... | collective-permute-start | bytes 393224 | tf_op jit(solution)/shard_map/ppermute | solution.py:24
  8.6 7.8 %collective-permute-start.1 = (bf16[256,256]{1,0:T(8,128)(2,1)S(1)}, bf16[256,256]{1,0:T(8,128)(2,1)S(1)}, u32[]{:S(2)}, u32[]{:S(2)}) collective-permute-start(bf16[256,256]{1,0:T(8,128)(2,1)S(1)} %get-tuple-element.31), channel_id=1, source_target_pairs={{0,2},{2,0},{4,6},{6,4},{1,3},{3,1},{5,7},{7,5},{8,10},{10,8},{12,... | collective-permute-start | bytes 393224 | tf_op jit(solution)/shard_map/ppermute | solution.py:24
  13.0 12.6 %collective-permute-start.5 = (bf16[256,256]{1,0:T(8,128)(2,1)S(1)}, bf16[256,256]{1,0:T(8,128)(2,1)S(1)}, u32[]{:S(2)}, u32[]{:S(2)}) collective-permute-start(bf16[256,256]{1,0:T(8,128)(2,1)S(1)} %get-tuple-element.37), channel_id=1, source_target_pairs={{0,4},{2,6},{4,0},{6,2},{1,5},{3,7},{5,1},{7,3},{8,12},{10,14},{12... | collective-permute-start | bytes 393224 | tf_op jit(solution)/shard_map/ppermute | solution.py:24
  16.4 11.1 %collective-permute-start.2 = (bf16[256,256]{1,0:T(8,128)(2,1)S(1)}, bf16[256,256]{1,0:T(8,128)(2,1)S(1)}, u32[]{:S(2)}, u32[]{:S(2)}) collective-permute-start(bf16[256,256]{1,0:T(8,128)(2,1)S(1)} %get-tuple-element.33), channel_id=1, source_target_pairs={{0,4},{2,6},{4,0},{6,2},{1,5},{3,7},{5,1},{7,3},{8,12},{10,14},{12... | collective-permute-start | bytes 393224 | tf_op jit(solution)/shard_map/ppermute | solution.py:24
  25.6 6.4 %collective-permute-start.9 = (bf16[256,256]{1,0:T(8,128)(2,1)S(1)}, bf16[256,256]{1,0:T(8,128)(2,1)S(1)}, u32[]{:S(2)}, u32[]{:S(2)}) collective-permute-start(bf16[256,256]{1,0:T(8,128)(2,1)S(1)} %shard_map.48.refs_2_), channel_id=1, source_target_pairs={{0,2},{2,0},{4,6},{6,4},{1,3},{3,1},{5,7},{7,5},{8,10},{10,8},{12,... | collective-permute-start | bytes 393224 | tf_op jit(solution)/shard_map/ppermute | solution.py:24
  27.5 5.9 %collective-permute-start.7 = (bf16[256,256]{1,0:T(8,128)(2,1)S(1)}, bf16[256,256]{1,0:T(8,128)(2,1)S(1)}, u32[]{:S(2)}, u32[]{:S(2)}) collective-permute-start(bf16[256,256]{1,0:T(8,128)(2,1)S(1)} %shard_map.45.refs_0_), channel_id=1, source_target_pairs={{0,2},{2,0},{4,6},{6,4},{1,3},{3,1},{5,7},{7,5},{8,10},{10,8},{12,... | collective-permute-start | bytes 393224 | tf_op jit(solution)/shard_map/ppermute | solution.py:24
  28.1 5.3 %collective-permute-start.6 = (bf16[256,256]{1,0:T(8,128)(2,1)S(1)}, bf16[256,256]{1,0:T(8,128)(2,1)S(1)}, u32[]{:S(2)}, u32[]{:S(2)}) collective-permute-start(bf16[256,256]{1,0:T(8,128)(2,1)S(1)} %shard_map.48.refs_2_), channel_id=1, source_target_pairs={{0,1},{1,0},{2,3},{3,2},{4,5},{5,4},{6,7},{7,6},{8,9},{9,8},{10,11... | collective-permute-start | bytes 393224 | tf_op jit(solution)/shard_map/ppermute | solution.py:24
  28.1 5.3 %collective-permute-start.3 = (bf16[256,256]{1,0:T(8,128)(2,1)S(1)}, bf16[256,256]{1,0:T(8,128)(2,1)S(1)}, u32[]{:S(2)}, u32[]{:S(2)}) collective-permute-start(bf16[256,256]{1,0:T(8,128)(2,1)S(1)} %shard_map.45.refs_0_), channel_id=1, source_target_pairs={{0,1},{1,0},{2,3},{3,2},{4,5},{5,4},{6,7},{7,6},{8,9},{9,8},{10,11... | collective-permute-start | bytes 393224 | tf_op jit(solution)/shard_map/ppermute | solution.py:24
  32.0 2.7 %collective-permute-start.10 = (bf16[256,256]{1,0:T(8,128)(2,1)S(1)}, bf16[256,256]{1,0:T(8,128)(2,1)S(1)}, u32[]{:S(2)}, u32[]{:S(2)}) collective-permute-start(bf16[256,256]{1,0:T(8,128)(2,1)S(1)} %collective-permute-done.9.refs_2_), channel_id=1, source_target_pairs={{0,1},{1,0},{2,3},{3,2},{4,5},{5,4},{6,7},{7,6},{8,9},{9,8},{10,11... | collective-permute-start | bytes 393224 | tf_op jit(solution)/shard_map/ppermute | solution.py:24
  33.4 1.3 collective-permute-start.8
  36.3 8.0 %collective-permute-start.11 = (bf16[64,2048]{1,0:T(8,128)(2,1)S(1)}, bf16[64,2048]{1,0:T(8,128)(2,1)S(1)}, u32[]{:S(2)}, u32[]{:S(2)}) collective-permute-start(bf16[64,2048]{1,0:T(8,128)(2,1)S(1)} %get-tuple-element.57), channel_id=1, source_target_pairs={{0,128},{1,17},{8,136},{9,25},{16,144},{17,1},{24,152},{25,9},{64,... | collective-permute-start | bytes 786440 | tf_op jit(solution)/shard_map/ppermute | solution.py:34
  39.5 7.7 %collective-permute-start.13 = (bf16[64,2048]{1,0:T(8,128)(2,1)S(1)}, bf16[64,2048]{1,0:T(8,128)(2,1)S(1)}, u32[]{:S(2)}, u32[]{:S(2)}) collective-permute-start(bf16[64,2048]{1,0:T(8,128)(2,1)S(1)} %get-tuple-element.58), channel_id=1, source_target_pairs={{0,192},{1,25},{8,200},{9,17},{16,208},{17,9},{24,216},{25,1},{64,... | collective-permute-start | bytes 786440 | tf_op jit(solution)/shard_map/ppermute | solution.py:34
  40.6 6.6 %collective-permute-start.12 = (bf16[64,2048]{1,0:T(8,128)(2,1)S(1)}, bf16[64,2048]{1,0:T(8,128)(2,1)S(1)}, u32[]{:S(2)}, u32[]{:S(2)}) collective-permute-start(bf16[64,2048]{1,0:T(8,128)(2,1)S(1)} %get-tuple-element.59), channel_id=1, source_target_pairs={{0,64},{1,9},{8,72},{9,1},{16,80},{17,25},{24,88},{25,17},{64,0},{... | collective-permute-start | bytes 786440 | tf_op jit(solution)/shard_map/ppermute | solution.py:34
  47.4 6.6 %collective-permute-start.14 = (f32[16,2048]{1,0:T(8,128)S(1)}, f32[16,2048]{1,0:T(8,128)S(1)}, u32[]{:S(2)}, u32[]{:S(2)}) collective-permute-start(f32[16,2048]{1,0:T(8,128)S(1)} %get-tuple-element.63), channel_id=1, source_target_pairs={{0,16},{1,129},{8,24},{9,137},{16,0},{17,145},{24,8},{25,153},{64,... | collective-permute-start | bytes 393224 | tf_op jit(solution)/shard_map/ppermute | solution.py:34
  49.8 5.6 %collective-permute-start.16 = (f32[16,2048]{1,0:T(8,128)S(1)}, f32[16,2048]{1,0:T(8,128)S(1)}, u32[]{:S(2)}, u32[]{:S(2)}) collective-permute-start(f32[16,2048]{1,0:T(8,128)S(1)} %get-tuple-element.64), channel_id=1, source_target_pairs={{0,24},{1,193},{8,16},{9,201},{16,8},{17,209},{24,0},{25,217},{64,... | collective-permute-start | bytes 393224 | tf_op jit(solution)/shard_map/ppermute | solution.py:34
  49.8 5.7 %collective-permute-start.15 = (f32[16,2048]{1,0:T(8,128)S(1)}, f32[16,2048]{1,0:T(8,128)S(1)}, u32[]{:S(2)}, u32[]{:S(2)}) collective-permute-start(f32[16,2048]{1,0:T(8,128)S(1)} %get-tuple-element.65), channel_id=1, source_target_pairs={{0,8},{1,65},{8,0},{9,73},{16,24},{17,81},{24,16},{25,89},{64,72},... | collective-permute-start | bytes 393224 | tf_op jit(solution)/shard_map/ppermute | solution.py:34
  55.5 8.5 %collective-permute-start.17 = (bf16[16,2048]{1,0:T(8,128)(2,1)S(1)}, bf16[16,2048]{1,0:T(8,128)(2,1)S(1)}, u32[]{:S(2)}, u32[]{:S(2)}) collective-permute-start(bf16[16,2048]{1,0:T(8,128)(2,1)S(1)} %get-tuple-element.52), channel_id=1, source_target_pairs={{0,32},{32,0},{1,33},{33,1},{2,34},{34,2},{3,35},{35,3},{4,36},{36... | collective-permute-start | bytes 196616 | tf_op jit(solution)/shard_map/ppermute | solution.py:24
  64.0 4.4 %collective-permute-start.20 = (bf16[16,2048]{1,0:T(8,128)(2,1)S(1)}, bf16[16,2048]{1,0:T(8,128)(2,1)S(1)}, u32[]{:S(2)}, u32[]{:S(2)}) collective-permute-start(bf16[16,2048]{1,0:T(8,128)(2,1)S(1)} %get-tuple-element.50), channel_id=1, source_target_pairs={{0,24},{1,193},{8,16},{9,201},{16,8},{17,209},{24,0},{25,217},{64,... | collective-permute-start | bytes 196616 | tf_op jit(solution)/shard_map/ppermute | solution.py:34
  65.4 5.8 %collective-permute-start.19 = (bf16[16,2048]{1,0:T(8,128)(2,1)S(1)}, bf16[16,2048]{1,0:T(8,128)(2,1)S(1)}, u32[]{:S(2)}, u32[]{:S(2)}) collective-permute-start(bf16[16,2048]{1,0:T(8,128)(2,1)S(1)} %get-tuple-element.50), channel_id=1, source_target_pairs={{0,16},{1,129},{8,24},{9,137},{16,0},{17,145},{24,8},{25,153},{64,... | collective-permute-start | bytes 196616 | tf_op jit(solution)/shard_map/ppermute | solution.py:34
  68.0 4.3 %collective-permute-start.18 = (bf16[16,2048]{1,0:T(8,128)(2,1)S(1)}, bf16[16,2048]{1,0:T(8,128)(2,1)S(1)}, u32[]{:S(2)}, u32[]{:S(2)}) collective-permute-start(bf16[16,2048]{1,0:T(8,128)(2,1)S(1)} %get-tuple-element.50), channel_id=1, source_target_pairs={{0,8},{1,65},{8,0},{9,73},{16,24},{17,81},{24,16},{25,89},{64,72},... | collective-permute-start | bytes 196616 | tf_op jit(solution)/shard_map/ppermute | solution.py:34
  72.3 10.7 %collective-permute-start.23 = (bf16[64,2048]{1,0:T(8,128)(2,1)S(1)}, bf16[64,2048]{1,0:T(8,128)(2,1)S(1)}, u32[]{:S(2)}, u32[]{:S(2)}) collective-permute-start(bf16[64,2048]{1,0:T(8,128)(2,1)S(1)} %bitcast.23), channel_id=1, source_target_pairs={{0,192},{1,25},{8,200},{9,17},{16,208},{17,9},{24,216},{25,1},{64,... | collective-permute-start | bytes 786440 | tf_op jit(solution)/shard_map/ppermute | solution.py:34
  76.3 7.9 %collective-permute-start.22 = (bf16[64,2048]{1,0:T(8,128)(2,1)S(1)}, bf16[64,2048]{1,0:T(8,128)(2,1)S(1)}, u32[]{:S(2)}, u32[]{:S(2)}) collective-permute-start(bf16[64,2048]{1,0:T(8,128)(2,1)S(1)} %bitcast.24), channel_id=1, source_target_pairs={{0,128},{1,17},{8,136},{9,25},{16,144},{17,1},{24,152},{25,9},{64,... | collective-permute-start | bytes 786440 | tf_op jit(solution)/shard_map/ppermute | solution.py:34
  76.9 7.5 %collective-permute-start.21 = (bf16[64,2048]{1,0:T(8,128)(2,1)S(1)}, bf16[64,2048]{1,0:T(8,128)(2,1)S(1)}, u32[]{:S(2)}, u32[]{:S(2)}) collective-permute-start(bf16[64,2048]{1,0:T(8,128)(2,1)S(1)} %bitcast.25), channel_id=1, source_target_pairs={{0,64},{1,9},{8,72},{9,1},{16,80},{17,25},{24,88},{25,17},{64,0},{... | collective-permute-start | bytes 786440 | tf_op jit(solution)/shard_map/ppermute | solution.py:34
  86.0 2.0 %collective-permute-start.24 = (bf16[1024,256]{1,0:T(8,128)(2,1)S(1)}, bf16[1024,256]{1,0:T(8,128)(2,1)S(1)}, u32[]{:S(2)}, u32[]{:S(2)}) collective-permute-start(bf16[1024,256]{1,0:T(8,128)(2,1)S(1)} %shard_map.53), channel_id=1, source_target_pairs={{0,1},{1,0},{2,3},{3,2},{4,5},{5,4},{6,7},{7,6},{8,9},{9,8},{10,11... | collective-permute-start | bytes 1572872 | tf_op jit(solution)/shard_map/ppermute | solution.py:24
  88.0 6.4 %collective-permute-start.28 = (bf16[256,256]{1,0:T(8,128)(2,1)S(1)}, bf16[256,256]{1,0:T(8,128)(2,1)S(1)}, u32[]{:S(2)}, u32[]{:S(2)}) collective-permute-start(bf16[256,256]{1,0:T(8,128)(2,1)S(1)} %get-tuple-element.45), channel_id=1, source_target_pairs={{0,2},{2,0},{4,6},{6,4},{1,3},{3,1},{5,7},{7,5},{8,10},{10,8},{12,... | collective-permute-start | bytes 393224 | tf_op jit(solution)/shard_map/ppermute | solution.py:24
  88.3 8.2 %collective-permute-start.25 = (bf16[256,256]{1,0:T(8,128)(2,1)S(1)}, bf16[256,256]{1,0:T(8,128)(2,1)S(1)}, u32[]{:S(2)}, u32[]{:S(2)}) collective-permute-start(bf16[256,256]{1,0:T(8,128)(2,1)S(1)} %get-tuple-element.41), channel_id=1, source_target_pairs={{0,2},{2,0},{4,6},{6,4},{1,3},{3,1},{5,7},{7,5},{8,10},{10,8},{12,... | collective-permute-start | bytes 393224 | tf_op jit(solution)/shard_map/ppermute | solution.py:24
  94.5 11.7 %collective-permute-start.29 = (bf16[256,256]{1,0:T(8,128)(2,1)S(1)}, bf16[256,256]{1,0:T(8,128)(2,1)S(1)}, u32[]{:S(2)}, u32[]{:S(2)}) collective-permute-start(bf16[256,256]{1,0:T(8,128)(2,1)S(1)} %get-tuple-element.47), channel_id=1, source_target_pairs={{0,4},{2,6},{4,0},{6,2},{1,5},{3,7},{5,1},{7,3},{8,12},{10,14},{12... | collective-permute-start | bytes 393224 | tf_op jit(solution)/shard_map/ppermute | solution.py:24
  96.5 11.4 %collective-permute-start.26 = (bf16[256,256]{1,0:T(8,128)(2,1)S(1)}, bf16[256,256]{1,0:T(8,128)(2,1)S(1)}, u32[]{:S(2)}, u32[]{:S(2)}) collective-permute-start(bf16[256,256]{1,0:T(8,128)(2,1)S(1)} %get-tuple-element.43), channel_id=1, source_target_pairs={{0,4},{2,6},{4,0},{6,2},{1,5},{3,7},{5,1},{7,3},{8,12},{10,14},{12... | collective-permute-start | bytes 393224 | tf_op jit(solution)/shard_map/ppermute | solution.py:24
  106.2 6.3 %collective-permute-start.33 = (bf16[256,256]{1,0:T(8,128)(2,1)S(1)}, bf16[256,256]{1,0:T(8,128)(2,1)S(1)}, u32[]{:S(2)}, u32[]{:S(2)}) collective-permute-start(bf16[256,256]{1,0:T(8,128)(2,1)S(1)} %shard_map.59.refs_2_), channel_id=1, source_target_pairs={{0,2},{2,0},{4,6},{6,4},{1,3},{3,1},{5,7},{7,5},{8,10},{10,8},{12,... | collective-permute-start | bytes 393224 | tf_op jit(solution)/shard_map/ppermute | solution.py:24
  108.0 5.9 %collective-permute-start.31 = (bf16[256,256]{1,0:T(8,128)(2,1)S(1)}, bf16[256,256]{1,0:T(8,128)(2,1)S(1)}, u32[]{:S(2)}, u32[]{:S(2)}) collective-permute-start(bf16[256,256]{1,0:T(8,128)(2,1)S(1)} %shard_map.56.refs_0_), channel_id=1, source_target_pairs={{0,2},{2,0},{4,6},{6,4},{1,3},{3,1},{5,7},{7,5},{8,10},{10,8},{12,... | collective-permute-start | bytes 393224 | tf_op jit(solution)/shard_map/ppermute | solution.py:24
  108.7 5.2 %collective-permute-start.30 = (bf16[256,256]{1,0:T(8,128)(2,1)S(1)}, bf16[256,256]{1,0:T(8,128)(2,1)S(1)}, u32[]{:S(2)}, u32[]{:S(2)}) collective-permute-start(bf16[256,256]{1,0:T(8,128)(2,1)S(1)} %shard_map.59.refs_2_), channel_id=1, source_target_pairs={{0,1},{1,0},{2,3},{3,2},{4,5},{5,4},{6,7},{7,6},{8,9},{9,8},{10,11... | collective-permute-start | bytes 393224 | tf_op jit(solution)/shard_map/ppermute | solution.py:24
  108.7 5.2 %collective-permute-start.27 = (bf16[256,256]{1,0:T(8,128)(2,1)S(1)}, bf16[256,256]{1,0:T(8,128)(2,1)S(1)}, u32[]{:S(2)}, u32[]{:S(2)}) collective-permute-start(bf16[256,256]{1,0:T(8,128)(2,1)S(1)} %shard_map.56.refs_0_), channel_id=1, source_target_pairs={{0,1},{1,0},{2,3},{3,2},{4,5},{5,4},{6,7},{7,6},{8,9},{9,8},{10,11... | collective-permute-start | bytes 393224 | tf_op jit(solution)/shard_map/ppermute | solution.py:24
  112.5 2.7 %collective-permute-start.34 = (bf16[256,256]{1,0:T(8,128)(2,1)S(1)}, bf16[256,256]{1,0:T(8,128)(2,1)S(1)}, u32[]{:S(2)}, u32[]{:S(2)}) collective-permute-start(bf16[256,256]{1,0:T(8,128)(2,1)S(1)} %collective-permute-done.33.refs_2_), channel_id=1, source_target_pairs={{0,1},{1,0},{2,3},{3,2},{4,5},{5,4},{6,7},{7,6},{8,9},{9,8},{10,11... | collective-permute-start | bytes 393224 | tf_op jit(solution)/shard_map/ppermute | solution.py:24
  113.9 1.3 collective-permute-start.32
  116.9 8.1 %collective-permute-start.35 = (bf16[64,2048]{1,0:T(8,128)(2,1)S(1)}, bf16[64,2048]{1,0:T(8,128)(2,1)S(1)}, u32[]{:S(2)}, u32[]{:S(2)}) collective-permute-start(bf16[64,2048]{1,0:T(8,128)(2,1)S(1)} %get-tuple-element.54), channel_id=1, source_target_pairs={{0,128},{1,17},{8,136},{9,25},{16,144},{17,1},{24,152},{25,9},{64,... | collective-permute-start | bytes 786440 | tf_op jit(solution)/shard_map/ppermute | solution.py:34
  118.8 8.8 %collective-permute-start.37 = (bf16[64,2048]{1,0:T(8,128)(2,1)S(1)}, bf16[64,2048]{1,0:T(8,128)(2,1)S(1)}, u32[]{:S(2)}, u32[]{:S(2)}) collective-permute-start(bf16[64,2048]{1,0:T(8,128)(2,1)S(1)} %get-tuple-element.55), channel_id=1, source_target_pairs={{0,192},{1,25},{8,200},{9,17},{16,208},{17,9},{24,216},{25,1},{64,... | collective-permute-start | bytes 786440 | tf_op jit(solution)/shard_map/ppermute | solution.py:34
  121.0 6.9 %collective-permute-start.36 = (bf16[64,2048]{1,0:T(8,128)(2,1)S(1)}, bf16[64,2048]{1,0:T(8,128)(2,1)S(1)}, u32[]{:S(2)}, u32[]{:S(2)}) collective-permute-start(bf16[64,2048]{1,0:T(8,128)(2,1)S(1)} %get-tuple-element.56), channel_id=1, source_target_pairs={{0,64},{1,9},{8,72},{9,1},{16,80},{17,25},{24,88},{25,17},{64,0},{... | collective-permute-start | bytes 786440 | tf_op jit(solution)/shard_map/ppermute | solution.py:34
  128.1 6.7 %collective-permute-start.38 = (f32[16,2048]{1,0:T(8,128)S(1)}, f32[16,2048]{1,0:T(8,128)S(1)}, u32[]{:S(2)}, u32[]{:S(2)}) collective-permute-start(f32[16,2048]{1,0:T(8,128)S(1)} %get-tuple-element.60), channel_id=1, source_target_pairs={{0,16},{1,129},{8,24},{9,137},{16,0},{17,145},{24,8},{25,153},{64,... | collective-permute-start | bytes 393224 | tf_op jit(solution)/shard_map/ppermute | solution.py:34
  129.5 6.4 %collective-permute-start.40 = (f32[16,2048]{1,0:T(8,128)S(1)}, f32[16,2048]{1,0:T(8,128)S(1)}, u32[]{:S(2)}, u32[]{:S(2)}) collective-permute-start(f32[16,2048]{1,0:T(8,128)S(1)} %get-tuple-element.61), channel_id=1, source_target_pairs={{0,24},{1,193},{8,16},{9,201},{16,8},{17,209},{24,0},{25,217},{64,... | collective-permute-start | bytes 393224 | tf_op jit(solution)/shard_map/ppermute | solution.py:34
  130.9 5.0 %collective-permute-start.39 = (f32[16,2048]{1,0:T(8,128)S(1)}, f32[16,2048]{1,0:T(8,128)S(1)}, u32[]{:S(2)}, u32[]{:S(2)}) collective-permute-start(f32[16,2048]{1,0:T(8,128)S(1)} %get-tuple-element.62), channel_id=1, source_target_pairs={{0,8},{1,65},{8,0},{9,73},{16,24},{17,81},{24,16},{25,89},{64,72},... | collective-permute-start | bytes 393224 | tf_op jit(solution)/shard_map/ppermute | solution.py:34
  136.0 8.4 %collective-permute-start.41 = (f32[8,2048]{1,0:T(8,128)S(1)}, f32[8,2048]{1,0:T(8,128)S(1)}, u32[]{:S(2)}, u32[]{:S(2)}) collective-permute-start(f32[8,2048]{1,0:T(8,128)S(1)} %constant_dynamic-slice_fusion), channel_id=1, source_target_pairs={{0,32},{32,0},{1,33},{33,1},{2,34},{34,2},{3,35},{35,3},{4,36},{36... | collective-permute-start | bytes 196616 | tf_op jit(solution)/shard_map/ppermute | solution.py:24

commit v3 on v2

--- a/solution.py
+++ b/solution.py
@@ -262,7 +262,7 @@
     y = product_mine(x_own, x_theirs, mine)
     kept, given = product_all(y, x_own, x_theirs, other)
     total = reduce_four(kept, given, 0).reshape(4, ROWS, -1)
-    return reduce_four(total[0], total[1:], 1)
+    return reduce_four(total[0], total[1:].astype(BF16), 1)
 
 
 def spread(rounded):

time: 147 us -> 145 us (0.986)
  waiting for transfers between devices: 71.4 us -> 69.6 us
    ppermute x18, waiting for transfers between devices: 31.2 us -> 29.7 us  [swap_xy(): return lax.ppermute(value, ('x', 'y', 'c'), pairs)]
  transfers between devices with their start and end apart: 42 -> 42, of which waited for: 32 -> 31; matrix products, arithmetic and copies ran while one was open for 0% -> 0% of each run, Pallas kernels for 4% -> 4%
where the time goes in v3:
time: 145 us; the launch traced here: 143 us
  waiting for transfers between devices  69.6 us (48%)
  starting transfers between devices  57.2 us (39%)
  Pallas kernels  13.8 us (10%)
    ppermute x24, waiting for transfers between devices, swap(): lax.ppermute(value, axis, [(i, i ^ mask) for i in range(SIZES[axis])])  40 us
    ppermute x24, starting transfers between devices, swap(): lax.ppermute(value, axis, [(i, i ^ mask) for i in range(SIZES[axis])])  29.8 us
    ppermute x18, waiting for transfers between devices, swap_xy(): return lax.ppermute(value, ('x', 'y', 'c'), pairs)  29.7 us
    ppermute x18, starting transfers between devices, swap_xy(): return lax.ppermute(value, ('x', 'y', 'c'), pairs)  27.5 us
    pallas_call x21, Pallas kernels, call(): pl.pallas_call(kernel, in_specs=specs or [VMEM] * len(args), out_specs=[V...  13.8 us
  transfers between devices with their start and end apart: 42, of which 31 were waited for; matrix products, arithmetic and copies ran while one was open for 0% of the time, Pallas kernels for 4%

profile of v3, /device:TPU:8, one launch (start us, length us, event | category | flops | bytes accessed | tf_op | source)
XLA Modules:
  0.0 143.5 jit_solution(11055468253379978621)
XLA Ops:
  0.6 3.8 %shard_map.41 = (bf16[1024,2048]{1,0:T(8,128)(2,1)S(1)}, bf16[1024,2048]{1,0:T(8,128)(2,1)S(1)}, bf16[256,2048]{1,0:T(8,128)(2,1)S(1)}, bf16[1024,256]{1,0:T(8,128)(2,1)S(1)}) custom-call(bf16[2048,2048]{1,0:T(8,128)(2,1)} %x_hbm.1, bf16[256,2048]{1,0:T(8,128)(2,1)} %p_hbm.1), custom_call_target="tpu_custom_call" | custom-call | flops 1073741824 | bytes 1048576 | tf_op jit(solution)/shard_map/pallas_call | solution.py:50
  4.6 1.3 shard_map.42.own_ref
  6.5 2.0 %collective-permute-start.4 = (bf16[256,256]{1,0:T(8,128)(2,1)S(1)}, bf16[256,256]{1,0:T(8,128)(2,1)S(1)}, u32[]{:S(2)}, u32[]{:S(2)}) collective-permute-start(bf16[256,256]{1,0:T(8,128)(2,1)S(1)} %get-tuple-element.35), channel_id=1, source_target_pairs={{0,2},{2,0},{4,6},{6,4},{1,3},{3,1},{5,7},{7,5},{8,10},{10,8},{12,... | collective-permute-start | bytes 393224 | tf_op jit(solution)/shard_map/ppermute | solution.py:24
  8.8 4.2 %collective-permute-done.4.got_ref = bf16[256,256]{1,0:T(8,128)(2,1)S(1)} collective-permute-done((bf16[256,256]{1,0:T(8,128)(2,1)S(1)}, bf16[256,256]{1,0:T(8,128)(2,1)S(1)}, u32[]{:S(2)}, u32[]{:S(2)}) %collective-permute-start.4) | collective-permute-done | bytes 131104 | tf_op jit(solution)/shard_map/ppermute | solution.py:24
  13.0 3.4 %collective-permute-start.5 = (bf16[256,256]{1,0:T(8,128)(2,1)S(1)}, bf16[256,256]{1,0:T(8,128)(2,1)S(1)}, u32[]{:S(2)}, u32[]{:S(2)}) collective-permute-start(bf16[256,256]{1,0:T(8,128)(2,1)S(1)} %get-tuple-element.37), channel_id=1, source_target_pairs={{0,4},{2,6},{4,0},{6,2},{1,5},{3,7},{5,1},{7,3},{8,12},{10,14},{12... | collective-permute-start | bytes 393224 | tf_op jit(solution)/shard_map/ppermute | solution.py:24
  16.4 2.8 %collective-permute-start.2 = (bf16[256,256]{1,0:T(8,128)(2,1)S(1)}, bf16[256,256]{1,0:T(8,128)(2,1)S(1)}, u32[]{:S(2)}, u32[]{:S(2)}) collective-permute-start(bf16[256,256]{1,0:T(8,128)(2,1)S(1)} %get-tuple-element.33), channel_id=1, source_target_pairs={{0,4},{2,6},{4,0},{6,2},{1,5},{3,7},{5,1},{7,3},{8,12},{10,14},{12... | collective-permute-start | bytes 393224 | tf_op jit(solution)/shard_map/ppermute | solution.py:24
  19.1 6.5 %collective-permute-done.5.got_ref = bf16[256,256]{1,0:T(8,128)(2,1)S(1)} collective-permute-done((bf16[256,256]{1,0:T(8,128)(2,1)S(1)}, bf16[256,256]{1,0:T(8,128)(2,1)S(1)}, u32[]{:S(2)}, u32[]{:S(2)}) %collective-permute-start.5) | collective-permute-done | bytes 131104 | tf_op jit(solution)/shard_map/ppermute | solution.py:24
  26.2 1.3 collective-permute-done.2.got_ref
  28.7 3.3 %collective-permute-done.9.refs_2_ = bf16[256,256]{1,0:T(8,128)(2,1)S(1)} collective-permute-done((bf16[256,256]{1,0:T(8,128)(2,1)S(1)}, bf16[256,256]{1,0:T(8,128)(2,1)S(1)}, u32[]{:S(2)}, u32[]{:S(2)}) %collective-permute-start.9) | collective-permute-done | bytes 131104 | tf_op jit(solution)/shard_map/ppermute | solution.py:24
  32.0 1.4 collective-permute-done.7.refs_0_
  33.4 1.3 shard_map.49.y_ref
  34.7 1.5 %shard_map.50 = (f32[64,2048]{1,0:T(8,128)S(1)}, bf16[3,64,2048]{2,1,0:T(8,128)(2,1)S(1)}) custom-call(f32[256,2048]{1,0:T(8,128)S(1)} %shard_map.49.y_ref, bf16[1024,2048]{1,0:T(8,128)(2,1)S(1)} %get-tuple-element.26.x_ref.xo_ref, bf16[1024,2048]{1,0:T(8,128)(2,1)S(1)} %get-tuple-element.27.xt_ref.x_ref, ...), custom_call_target="tpu_custom_call" | custom-call | flops 1073741824 | bytes 1048576 | tf_op jit(solution)/shard_map/pallas_call | solution.py:50
  36.3 3.1 %collective-permute-start.11 = (bf16[64,2048]{1,0:T(8,128)(2,1)S(1)}, bf16[64,2048]{1,0:T(8,128)(2,1)S(1)}, u32[]{:S(2)}, u32[]{:S(2)}) collective-permute-start(bf16[64,2048]{1,0:T(8,128)(2,1)S(1)} %get-tuple-element.59), channel_id=1, source_target_pairs={{0,128},{1,17},{8,136},{9,25},{16,144},{17,1},{24,152},{25,9},{64,... | collective-permute-start | bytes 786440 | tf_op jit(solution)/shard_map/ppermute | solution.py:34
  39.5 1.1 collective-permute-start.13
  40.6 3.7 %collective-permute-done.11 = bf16[64,2048]{1,0:T(8,128)(2,1)S(1)} collective-permute-done((bf16[64,2048]{1,0:T(8,128)(2,1)S(1)}, bf16[64,2048]{1,0:T(8,128)(2,1)S(1)}, u32[]{:S(2)}, u32[]{:S(2)}) %collective-permute-start.11) | collective-permute-done | bytes 262176 | tf_op jit(solution)/shard_map/ppermute | solution.py:34
  44.3 2.8 %collective-permute-done.13 = bf16[64,2048]{1,0:T(8,128)(2,1)S(1)} collective-permute-done((bf16[64,2048]{1,0:T(8,128)(2,1)S(1)}, bf16[64,2048]{1,0:T(8,128)(2,1)S(1)}, u32[]{:S(2)}, u32[]{:S(2)}) %collective-permute-start.13) | collective-permute-done | bytes 262176 | tf_op jit(solution)/shard_map/ppermute | solution.py:34
  47.4 2.4 %collective-permute-start.14 = (bf16[16,2048]{1,0:T(8,128)(2,1)S(1)}, bf16[16,2048]{1,0:T(8,128)(2,1)S(1)}, u32[]{:S(2)}, u32[]{:S(2)}) collective-permute-start(bf16[16,2048]{1,0:T(8,128)(2,1)S(1)} %get-tuple-element.65), channel_id=1, source_target_pairs={{0,16},{1,129},{8,24},{9,137},{16,0},{17,145},{24,8},{25,153},{64,... | collective-permute-start | bytes 196616 | tf_op jit(solution)/shard_map/ppermute | solution.py:34
  49.8 2.4 %collective-permute-start.15 = (bf16[16,2048]{1,0:T(8,128)(2,1)S(1)}, bf16[16,2048]{1,0:T(8,128)(2,1)S(1)}, u32[]{:S(2)}, u32[]{:S(2)}) collective-permute-start(bf16[16,2048]{1,0:T(8,128)(2,1)S(1)} %get-tuple-element.67), channel_id=1, source_target_pairs={{0,8},{1,65},{8,0},{9,73},{16,24},{17,81},{24,16},{25,89},{64,72},... | collective-permute-start | bytes 196616 | tf_op jit(solution)/shard_map/ppermute | solution.py:34
  54.5 6.1 %collective-permute-start.17 = (bf16[16,2048]{1,0:T(8,128)(2,1)S(1)}, bf16[16,2048]{1,0:T(8,128)(2,1)S(1)}, u32[]{:S(2)}, u32[]{:S(2)}) collective-permute-start(bf16[16,2048]{1,0:T(8,128)(2,1)S(1)} %fusion.4), channel_id=1, source_target_pairs={{0,32},{32,0},{1,33},{33,1},{2,34},{34,2},{3,35},{35,3},{4,36},{36... | collective-permute-start | bytes 196616 | tf_op jit(solution)/shard_map/ppermute | solution.py:24
  60.5 2.3 %collective-permute-done.17 = bf16[16,2048]{1,0:T(8,128)(2,1)S(1)} collective-permute-done((bf16[16,2048]{1,0:T(8,128)(2,1)S(1)}, bf16[16,2048]{1,0:T(8,128)(2,1)S(1)}, u32[]{:S(2)}, u32[]{:S(2)}) %collective-permute-start.17) | collective-permute-done | bytes 65568 | tf_op jit(solution)/shard_map/ppermute | solution.py:24
  62.9 1.8 %collective-permute-start.20 = (bf16[16,2048]{1,0:T(8,128)(2,1)S(1)}, bf16[16,2048]{1,0:T(8,128)(2,1)S(1)}, u32[]{:S(2)}, u32[]{:S(2)}) collective-permute-start(bf16[16,2048]{1,0:T(8,128)(2,1)S(1)} %get-tuple-element.52), channel_id=1, source_target_pairs={{0,24},{1,193},{8,16},{9,201},{16,8},{17,209},{24,0},{25,217},{64,... | collective-permute-start | bytes 196616 | tf_op jit(solution)/shard_map/ppermute | solution.py:34
  64.7 2.6 %collective-permute-start.19 = (bf16[16,2048]{1,0:T(8,128)(2,1)S(1)}, bf16[16,2048]{1,0:T(8,128)(2,1)S(1)}, u32[]{:S(2)}, u32[]{:S(2)}) collective-permute-start(bf16[16,2048]{1,0:T(8,128)(2,1)S(1)} %get-tuple-element.52), channel_id=1, source_target_pairs={{0,16},{1,129},{8,24},{9,137},{16,0},{17,145},{24,8},{25,153},{64,... | collective-permute-start | bytes 196616 | tf_op jit(solution)/shard_map/ppermute | solution.py:34
  67.3 3.2 %collective-permute-done.19 = bf16[16,2048]{1,0:T(8,128)(2,1)S(1)} collective-permute-done((bf16[16,2048]{1,0:T(8,128)(2,1)S(1)}, bf16[16,2048]{1,0:T(8,128)(2,1)S(1)}, u32[]{:S(2)}, u32[]{:S(2)}) %collective-permute-start.19) | collective-permute-done | bytes 65568 | tf_op jit(solution)/shard_map/ppermute | solution.py:34
  71.6 4.0 %collective-permute-start.23 = (bf16[64,2048]{1,0:T(8,128)(2,1)S(1)}, bf16[64,2048]{1,0:T(8,128)(2,1)S(1)}, u32[]{:S(2)}, u32[]{:S(2)}) collective-permute-start(bf16[64,2048]{1,0:T(8,128)(2,1)S(1)} %bitcast.23), channel_id=1, source_target_pairs={{0,192},{1,25},{8,200},{9,17},{16,208},{17,9},{24,216},{25,1},{64,... | collective-permute-start | bytes 786440 | tf_op jit(solution)/shard_map/ppermute | solution.py:34
  76.6 5.7 %collective-permute-done.23 = bf16[64,2048]{1,0:T(8,128)(2,1)S(1)} collective-permute-done((bf16[64,2048]{1,0:T(8,128)(2,1)S(1)}, bf16[64,2048]{1,0:T(8,128)(2,1)S(1)}, u32[]{:S(2)}, u32[]{:S(2)}) %collective-permute-start.23) | collective-permute-done | bytes 262176 | tf_op jit(solution)/shard_map/ppermute | solution.py:34
  82.3 1.2 collective-permute-done.22
  84.0 1.3 shard_map.53
  85.4 1.3 shard_map.52.own_ref
  87.6 2.0 %collective-permute-start.25 = (bf16[256,256]{1,0:T(8,128)(2,1)S(1)}, bf16[256,256]{1,0:T(8,128)(2,1)S(1)}, u32[]{:S(2)}, u32[]{:S(2)}) collective-permute-start(bf16[256,256]{1,0:T(8,128)(2,1)S(1)} %get-tuple-element.41), channel_id=1, source_target_pairs={{0,2},{2,0},{4,6},{6,4},{1,3},{3,1},{5,7},{7,5},{8,10},{10,8},{12,... | collective-permute-start | bytes 393224 | tf_op jit(solution)/shard_map/ppermute | solution.py:24
  89.6 4.2 %collective-permute-done.28.got_ref = bf16[256,256]{1,0:T(8,128)(2,1)S(1)} collective-permute-done((bf16[256,256]{1,0:T(8,128)(2,1)S(1)}, bf16[256,256]{1,0:T(8,128)(2,1)S(1)}, u32[]{:S(2)}, u32[]{:S(2)}) %collective-permute-start.28) | collective-permute-done | bytes 131104 | tf_op jit(solution)/shard_map/ppermute | solution.py:24
  93.8 1.9 %collective-permute-start.29 = (bf16[256,256]{1,0:T(8,128)(2,1)S(1)}, bf16[256,256]{1,0:T(8,128)(2,1)S(1)}, u32[]{:S(2)}, u32[]{:S(2)}) collective-permute-start(bf16[256,256]{1,0:T(8,128)(2,1)S(1)} %get-tuple-element.47), channel_id=1, source_target_pairs={{0,4},{2,6},{4,0},{6,2},{1,5},{3,7},{5,1},{7,3},{8,12},{10,14},{12... | collective-permute-start | bytes 393224 | tf_op jit(solution)/shard_map/ppermute | solution.py:24
  95.8 2.7 %collective-permute-start.26 = (bf16[256,256]{1,0:T(8,128)(2,1)S(1)}, bf16[256,256]{1,0:T(8,128)(2,1)S(1)}, u32[]{:S(2)}, u32[]{:S(2)}) collective-permute-start(bf16[256,256]{1,0:T(8,128)(2,1)S(1)} %get-tuple-element.43), channel_id=1, source_target_pairs={{0,4},{2,6},{4,0},{6,2},{1,5},{3,7},{5,1},{7,3},{8,12},{10,14},{12... | collective-permute-start | bytes 393224 | tf_op jit(solution)/shard_map/ppermute | solution.py:24
  98.5 7.1 %collective-permute-done.29.got_ref = bf16[256,256]{1,0:T(8,128)(2,1)S(1)} collective-permute-done((bf16[256,256]{1,0:T(8,128)(2,1)S(1)}, bf16[256,256]{1,0:T(8,128)(2,1)S(1)}, u32[]{:S(2)}, u32[]{:S(2)}) %collective-permute-start.29) | collective-permute-done | bytes 131104 | tf_op jit(solution)/shard_map/ppermute | solution.py:24
  105.8 1.5 %collective-permute-done.26.got_ref = bf16[256,256]{1,0:T(8,128)(2,1)S(1)} collective-permute-done((bf16[256,256]{1,0:T(8,128)(2,1)S(1)}, bf16[256,256]{1,0:T(8,128)(2,1)S(1)}, u32[]{:S(2)}, u32[]{:S(2)}) %collective-permute-start.26) | collective-permute-done | bytes 131104 | tf_op jit(solution)/shard_map/ppermute | solution.py:24
  108.6 3.0 %collective-permute-done.33.refs_2_ = bf16[256,256]{1,0:T(8,128)(2,1)S(1)} collective-permute-done((bf16[256,256]{1,0:T(8,128)(2,1)S(1)}, bf16[256,256]{1,0:T(8,128)(2,1)S(1)}, u32[]{:S(2)}, u32[]{:S(2)}) %collective-permute-start.33) | collective-permute-done | bytes 131104 | tf_op jit(solution)/shard_map/ppermute | solution.py:24
  111.7 1.4 collective-permute-done.31.refs_0_
  113.1 1.3 shard_map.60.y_ref
  114.4 1.5 %shard_map.61 = (f32[64,2048]{1,0:T(8,128)S(1)}, bf16[3,64,2048]{2,1,0:T(8,128)(2,1)S(1)}) custom-call(f32[256,2048]{1,0:T(8,128)S(1)} %shard_map.60.y_ref, bf16[1024,2048]{1,0:T(8,128)(2,1)S(1)} %get-tuple-element.26.x_ref.xo_ref, bf16[1024,2048]{1,0:T(8,128)(2,1)S(1)} %get-tuple-element.27.xt_ref.x_ref, ...), custom_call_target="tpu_custom_call" | custom-call | flops 1073741824 | bytes 1048576 | tf_op jit(solution)/shard_map/pallas_call | solution.py:50
  116.0 2.0 %collective-permute-start.35 = (bf16[64,2048]{1,0:T(8,128)(2,1)S(1)}, bf16[64,2048]{1,0:T(8,128)(2,1)S(1)}, u32[]{:S(2)}, u32[]{:S(2)}) collective-permute-start(bf16[64,2048]{1,0:T(8,128)(2,1)S(1)} %get-tuple-element.56), channel_id=1, source_target_pairs={{0,128},{1,17},{8,136},{9,25},{16,144},{17,1},{24,152},{25,9},{64,... | collective-permute-start | bytes 786440 | tf_op jit(solution)/shard_map/ppermute | solution.py:34
  118.0 2.3 %collective-permute-start.37 = (bf16[64,2048]{1,0:T(8,128)(2,1)S(1)}, bf16[64,2048]{1,0:T(8,128)(2,1)S(1)}, u32[]{:S(2)}, u32[]{:S(2)}) collective-permute-start(bf16[64,2048]{1,0:T(8,128)(2,1)S(1)} %get-tuple-element.57), channel_id=1, source_target_pairs={{0,192},{1,25},{8,200},{9,17},{16,208},{17,9},{24,216},{25,1},{64,... | collective-permute-start | bytes 786440 | tf_op jit(solution)/shard_map/ppermute | solution.py:34
  120.3 3.8 %collective-permute-done.35 = bf16[64,2048]{1,0:T(8,128)(2,1)S(1)} collective-permute-done((bf16[64,2048]{1,0:T(8,128)(2,1)S(1)}, bf16[64,2048]{1,0:T(8,128)(2,1)S(1)}, u32[]{:S(2)}, u32[]{:S(2)}) %collective-permute-start.35) | collective-permute-done | bytes 262176 | tf_op jit(solution)/shard_map/ppermute | solution.py:34
  124.1 2.7 %collective-permute-done.37 = bf16[64,2048]{1,0:T(8,128)(2,1)S(1)} collective-permute-done((bf16[64,2048]{1,0:T(8,128)(2,1)S(1)}, bf16[64,2048]{1,0:T(8,128)(2,1)S(1)}, u32[]{:S(2)}, u32[]{:S(2)}) %collective-permute-start.37) | collective-permute-done | bytes 262176 | tf_op jit(solution)/shard_map/ppermute | solution.py:34
  127.2 1.6 %collective-permute-start.38 = (bf16[16,2048]{1,0:T(8,128)(2,1)S(1)}, bf16[16,2048]{1,0:T(8,128)(2,1)S(1)}, u32[]{:S(2)}, u32[]{:S(2)}) collective-permute-start(bf16[16,2048]{1,0:T(8,128)(2,1)S(1)} %get-tuple-element.62), channel_id=1, source_target_pairs={{0,16},{1,129},{8,24},{9,137},{16,0},{17,145},{24,8},{25,153},{64,... | collective-permute-start | bytes 196616 | tf_op jit(solution)/shard_map/ppermute | solution.py:34
  128.8 1.4 collective-permute-start.40
  130.3 1.7 %collective-permute-start.39 = (bf16[16,2048]{1,0:T(8,128)(2,1)S(1)}, bf16[16,2048]{1,0:T(8,128)(2,1)S(1)}, u32[]{:S(2)}, u32[]{:S(2)}) collective-permute-start(bf16[16,2048]{1,0:T(8,128)(2,1)S(1)} %get-tuple-element.64), channel_id=1, source_target_pairs={{0,8},{1,65},{8,0},{9,73},{16,24},{17,81},{24,16},{25,89},{64,72},... | collective-permute-start | bytes 196616 | tf_op jit(solution)/shard_map/ppermute | solution.py:34
  132.0 1.1 collective-permute-done.38
  134.6 5.2 %collective-permute-start.41 = (f32[8,2048]{1,0:T(8,128)S(1)}, f32[8,2048]{1,0:T(8,128)S(1)}, u32[]{:S(2)}, u32[]{:S(2)}) collective-permute-start(f32[8,2048]{1,0:T(8,128)S(1)} %constant_dynamic-slice_fusion), channel_id=1, source_target_pairs={{0,32},{32,0},{1,33},{33,1},{2,34},{34,2},{3,35},{35,3},{4,36},{36... | collective-permute-start | bytes 196616 | tf_op jit(solution)/shard_map/ppermute | solution.py:24
  140.4 2.5 %collective-permute-done.41 = f32[8,2048]{1,0:T(8,128)S(1)} collective-permute-done((f32[8,2048]{1,0:T(8,128)S(1)}, f32[8,2048]{1,0:T(8,128)S(1)}, u32[]{:S(2)}, u32[]{:S(2)}) %collective-permute-start.41) | collective-permute-done | bytes 65568 | tf_op jit(solution)/shard_map/ppermute | solution.py:24
  (71 shorter events, 14.0 us)
Async XLA Ops:
  4.5 2.0 %collective-permute-start = (bf16[1024,256]{1,0:T(8,128)(2,1)S(1)}, bf16[1024,256]{1,0:T(8,128)(2,1)S(1)}, u32[]{:S(2)}, u32[]{:S(2)}) collective-permute-start(bf16[1024,256]{1,0:T(8,128)(2,1)S(1)} %get-tuple-element.29), channel_id=1, source_target_pairs={{0,1},{1,0},{2,3},{3,2},{4,5},{5,4},{6,7},{7,6},{8,9},{9,8},{10,11... | collective-permute-start | bytes 1572872 | tf_op jit(solution)/shard_map/ppermute | solution.py:24
  6.5 6.4 %collective-permute-start.4 = (bf16[256,256]{1,0:T(8,128)(2,1)S(1)}, bf16[256,256]{1,0:T(8,128)(2,1)S(1)}, u32[]{:S(2)}, u32[]{:S(2)}) collective-permute-start(bf16[256,256]{1,0:T(8,128)(2,1)S(1)} %get-tuple-element.35), channel_id=1, source_target_pairs={{0,2},{2,0},{4,6},{6,4},{1,3},{3,1},{5,7},{7,5},{8,10},{10,8},{12,... | collective-permute-start | bytes 393224 | tf_op jit(solution)/shard_map/ppermute | solution.py:24
  8.6 7.8 %collective-permute-start.1 = (bf16[256,256]{1,0:T(8,128)(2,1)S(1)}, bf16[256,256]{1,0:T(8,128)(2,1)S(1)}, u32[]{:S(2)}, u32[]{:S(2)}) collective-permute-start(bf16[256,256]{1,0:T(8,128)(2,1)S(1)} %get-tuple-element.31), channel_id=1, source_target_pairs={{0,2},{2,0},{4,6},{6,4},{1,3},{3,1},{5,7},{7,5},{8,10},{10,8},{12,... | collective-permute-start | bytes 393224 | tf_op jit(solution)/shard_map/ppermute | solution.py:24
  13.0 12.6 %collective-permute-start.5 = (bf16[256,256]{1,0:T(8,128)(2,1)S(1)}, bf16[256,256]{1,0:T(8,128)(2,1)S(1)}, u32[]{:S(2)}, u32[]{:S(2)}) collective-permute-start(bf16[256,256]{1,0:T(8,128)(2,1)S(1)} %get-tuple-element.37), channel_id=1, source_target_pairs={{0,4},{2,6},{4,0},{6,2},{1,5},{3,7},{5,1},{7,3},{8,12},{10,14},{12... | collective-permute-start | bytes 393224 | tf_op jit(solution)/shard_map/ppermute | solution.py:24
  16.4 11.1 %collective-permute-start.2 = (bf16[256,256]{1,0:T(8,128)(2,1)S(1)}, bf16[256,256]{1,0:T(8,128)(2,1)S(1)}, u32[]{:S(2)}, u32[]{:S(2)}) collective-permute-start(bf16[256,256]{1,0:T(8,128)(2,1)S(1)} %get-tuple-element.33), channel_id=1, source_target_pairs={{0,4},{2,6},{4,0},{6,2},{1,5},{3,7},{5,1},{7,3},{8,12},{10,14},{12... | collective-permute-start | bytes 393224 | tf_op jit(solution)/shard_map/ppermute | solution.py:24
  25.6 6.4 %collective-permute-start.9 = (bf16[256,256]{1,0:T(8,128)(2,1)S(1)}, bf16[256,256]{1,0:T(8,128)(2,1)S(1)}, u32[]{:S(2)}, u32[]{:S(2)}) collective-permute-start(bf16[256,256]{1,0:T(8,128)(2,1)S(1)} %shard_map.48.refs_2_), channel_id=1, source_target_pairs={{0,2},{2,0},{4,6},{6,4},{1,3},{3,1},{5,7},{7,5},{8,10},{10,8},{12,... | collective-permute-start | bytes 393224 | tf_op jit(solution)/shard_map/ppermute | solution.py:24
  27.5 5.9 %collective-permute-start.7 = (bf16[256,256]{1,0:T(8,128)(2,1)S(1)}, bf16[256,256]{1,0:T(8,128)(2,1)S(1)}, u32[]{:S(2)}, u32[]{:S(2)}) collective-permute-start(bf16[256,256]{1,0:T(8,128)(2,1)S(1)} %shard_map.45.refs_0_), channel_id=1, source_target_pairs={{0,2},{2,0},{4,6},{6,4},{1,3},{3,1},{5,7},{7,5},{8,10},{10,8},{12,... | collective-permute-start | bytes 393224 | tf_op jit(solution)/shard_map/ppermute | solution.py:24
  28.1 5.3 %collective-permute-start.6 = (bf16[256,256]{1,0:T(8,128)(2,1)S(1)}, bf16[256,256]{1,0:T(8,128)(2,1)S(1)}, u32[]{:S(2)}, u32[]{:S(2)}) collective-permute-start(bf16[256,256]{1,0:T(8,128)(2,1)S(1)} %shard_map.48.refs_2_), channel_id=1, source_target_pairs={{0,1},{1,0},{2,3},{3,2},{4,5},{5,4},{6,7},{7,6},{8,9},{9,8},{10,11... | collective-permute-start | bytes 393224 | tf_op jit(solution)/shard_map/ppermute | solution.py:24
  28.1 5.3 %collective-permute-start.3 = (bf16[256,256]{1,0:T(8,128)(2,1)S(1)}, bf16[256,256]{1,0:T(8,128)(2,1)S(1)}, u32[]{:S(2)}, u32[]{:S(2)}) collective-permute-start(bf16[256,256]{1,0:T(8,128)(2,1)S(1)} %shard_map.45.refs_0_), channel_id=1, source_target_pairs={{0,1},{1,0},{2,3},{3,2},{4,5},{5,4},{6,7},{7,6},{8,9},{9,8},{10,11... | collective-permute-start | bytes 393224 | tf_op jit(solution)/shard_map/ppermute | solution.py:24
  32.0 2.7 %collective-permute-start.10 = (bf16[256,256]{1,0:T(8,128)(2,1)S(1)}, bf16[256,256]{1,0:T(8,128)(2,1)S(1)}, u32[]{:S(2)}, u32[]{:S(2)}) collective-permute-start(bf16[256,256]{1,0:T(8,128)(2,1)S(1)} %collective-permute-done.9.refs_2_), channel_id=1, source_target_pairs={{0,1},{1,0},{2,3},{3,2},{4,5},{5,4},{6,7},{7,6},{8,9},{9,8},{10,11... | collective-permute-start | bytes 393224 | tf_op jit(solution)/shard_map/ppermute | solution.py:24
  33.4 1.3 collective-permute-start.8
  36.3 8.0 %collective-permute-start.11 = (bf16[64,2048]{1,0:T(8,128)(2,1)S(1)}, bf16[64,2048]{1,0:T(8,128)(2,1)S(1)}, u32[]{:S(2)}, u32[]{:S(2)}) collective-permute-start(bf16[64,2048]{1,0:T(8,128)(2,1)S(1)} %get-tuple-element.59), channel_id=1, source_target_pairs={{0,128},{1,17},{8,136},{9,25},{16,144},{17,1},{24,152},{25,9},{64,... | collective-permute-start | bytes 786440 | tf_op jit(solution)/shard_map/ppermute | solution.py:34
  39.5 7.7 %collective-permute-start.13 = (bf16[64,2048]{1,0:T(8,128)(2,1)S(1)}, bf16[64,2048]{1,0:T(8,128)(2,1)S(1)}, u32[]{:S(2)}, u32[]{:S(2)}) collective-permute-start(bf16[64,2048]{1,0:T(8,128)(2,1)S(1)} %get-tuple-element.60), channel_id=1, source_target_pairs={{0,192},{1,25},{8,200},{9,17},{16,208},{17,9},{24,216},{25,1},{64,... | collective-permute-start | bytes 786440 | tf_op jit(solution)/shard_map/ppermute | solution.py:34
  40.6 6.6 %collective-permute-start.12 = (bf16[64,2048]{1,0:T(8,128)(2,1)S(1)}, bf16[64,2048]{1,0:T(8,128)(2,1)S(1)}, u32[]{:S(2)}, u32[]{:S(2)}) collective-permute-start(bf16[64,2048]{1,0:T(8,128)(2,1)S(1)} %get-tuple-element.61), channel_id=1, source_target_pairs={{0,64},{1,9},{8,72},{9,1},{16,80},{17,25},{24,88},{25,17},{64,0},{... | collective-permute-start | bytes 786440 | tf_op jit(solution)/shard_map/ppermute | solution.py:34
  47.4 5.9 %collective-permute-start.14 = (bf16[16,2048]{1,0:T(8,128)(2,1)S(1)}, bf16[16,2048]{1,0:T(8,128)(2,1)S(1)}, u32[]{:S(2)}, u32[]{:S(2)}) collective-permute-start(bf16[16,2048]{1,0:T(8,128)(2,1)S(1)} %get-tuple-element.65), channel_id=1, source_target_pairs={{0,16},{1,129},{8,24},{9,137},{16,0},{17,145},{24,8},{25,153},{64,... | collective-permute-start | bytes 196616 | tf_op jit(solution)/shard_map/ppermute | solution.py:34
  49.8 4.3 %collective-permute-start.16 = (bf16[16,2048]{1,0:T(8,128)(2,1)S(1)}, bf16[16,2048]{1,0:T(8,128)(2,1)S(1)}, u32[]{:S(2)}, u32[]{:S(2)}) collective-permute-start(bf16[16,2048]{1,0:T(8,128)(2,1)S(1)} %get-tuple-element.66), channel_id=1, source_target_pairs={{0,24},{1,193},{8,16},{9,201},{16,8},{17,209},{24,0},{25,217},{64,... | collective-permute-start | bytes 196616 | tf_op jit(solution)/shard_map/ppermute | solution.py:34
  49.8 4.7 %collective-permute-start.15 = (bf16[16,2048]{1,0:T(8,128)(2,1)S(1)}, bf16[16,2048]{1,0:T(8,128)(2,1)S(1)}, u32[]{:S(2)}, u32[]{:S(2)}) collective-permute-start(bf16[16,2048]{1,0:T(8,128)(2,1)S(1)} %get-tuple-element.67), channel_id=1, source_target_pairs={{0,8},{1,65},{8,0},{9,73},{16,24},{17,81},{24,16},{25,89},{64,72},... | collective-permute-start | bytes 196616 | tf_op jit(solution)/shard_map/ppermute | solution.py:34
  54.5 8.4 %collective-permute-start.17 = (bf16[16,2048]{1,0:T(8,128)(2,1)S(1)}, bf16[16,2048]{1,0:T(8,128)(2,1)S(1)}, u32[]{:S(2)}, u32[]{:S(2)}) collective-permute-start(bf16[16,2048]{1,0:T(8,128)(2,1)S(1)} %fusion.4), channel_id=1, source_target_pairs={{0,32},{32,0},{1,33},{33,1},{2,34},{34,2},{3,35},{35,3},{4,36},{36... | collective-permute-start | bytes 196616 | tf_op jit(solution)/shard_map/ppermute | solution.py:24
  62.9 4.4 %collective-permute-start.20 = (bf16[16,2048]{1,0:T(8,128)(2,1)S(1)}, bf16[16,2048]{1,0:T(8,128)(2,1)S(1)}, u32[]{:S(2)}, u32[]{:S(2)}) collective-permute-start(bf16[16,2048]{1,0:T(8,128)(2,1)S(1)} %get-tuple-element.52), channel_id=1, source_target_pairs={{0,24},{1,193},{8,16},{9,201},{16,8},{17,209},{24,0},{25,217},{64,... | collective-permute-start | bytes 196616 | tf_op jit(solution)/shard_map/ppermute | solution.py:34
  64.7 5.8 %collective-permute-start.19 = (bf16[16,2048]{1,0:T(8,128)(2,1)S(1)}, bf16[16,2048]{1,0:T(8,128)(2,1)S(1)}, u32[]{:S(2)}, u32[]{:S(2)}) collective-permute-start(bf16[16,2048]{1,0:T(8,128)(2,1)S(1)} %get-tuple-element.52), channel_id=1, source_target_pairs={{0,16},{1,129},{8,24},{9,137},{16,0},{17,145},{24,8},{25,153},{64,... | collective-permute-start | bytes 196616 | tf_op jit(solution)/shard_map/ppermute | solution.py:34
  67.3 4.3 %collective-permute-start.18 = (bf16[16,2048]{1,0:T(8,128)(2,1)S(1)}, bf16[16,2048]{1,0:T(8,128)(2,1)S(1)}, u32[]{:S(2)}, u32[]{:S(2)}) collective-permute-start(bf16[16,2048]{1,0:T(8,128)(2,1)S(1)} %get-tuple-element.52), channel_id=1, source_target_pairs={{0,8},{1,65},{8,0},{9,73},{16,24},{17,81},{24,16},{25,89},{64,72},... | collective-permute-start | bytes 196616 | tf_op jit(solution)/shard_map/ppermute | solution.py:34
  71.6 10.7 %collective-permute-start.23 = (bf16[64,2048]{1,0:T(8,128)(2,1)S(1)}, bf16[64,2048]{1,0:T(8,128)(2,1)S(1)}, u32[]{:S(2)}, u32[]{:S(2)}) collective-permute-start(bf16[64,2048]{1,0:T(8,128)(2,1)S(1)} %bitcast.23), channel_id=1, source_target_pairs={{0,192},{1,25},{8,200},{9,17},{16,208},{17,9},{24,216},{25,1},{64,... | collective-permute-start | bytes 786440 | tf_op jit(solution)/shard_map/ppermute | solution.py:34
  75.6 7.9 %collective-permute-start.22 = (bf16[64,2048]{1,0:T(8,128)(2,1)S(1)}, bf16[64,2048]{1,0:T(8,128)(2,1)S(1)}, u32[]{:S(2)}, u32[]{:S(2)}) collective-permute-start(bf16[64,2048]{1,0:T(8,128)(2,1)S(1)} %bitcast.24), channel_id=1, source_target_pairs={{0,128},{1,17},{8,136},{9,25},{16,144},{17,1},{24,152},{25,9},{64,... | collective-permute-start | bytes 786440 | tf_op jit(solution)/shard_map/ppermute | solution.py:34
  75.9 7.9 %collective-permute-start.21 = (bf16[64,2048]{1,0:T(8,128)(2,1)S(1)}, bf16[64,2048]{1,0:T(8,128)(2,1)S(1)}, u32[]{:S(2)}, u32[]{:S(2)}) collective-permute-start(bf16[64,2048]{1,0:T(8,128)(2,1)S(1)} %bitcast.25), channel_id=1, source_target_pairs={{0,64},{1,9},{8,72},{9,1},{16,80},{17,25},{24,88},{25,17},{64,0},{... | collective-permute-start | bytes 786440 | tf_op jit(solution)/shard_map/ppermute | solution.py:34
  85.3 2.0 %collective-permute-start.24 = (bf16[1024,256]{1,0:T(8,128)(2,1)S(1)}, bf16[1024,256]{1,0:T(8,128)(2,1)S(1)}, u32[]{:S(2)}, u32[]{:S(2)}) collective-permute-start(bf16[1024,256]{1,0:T(8,128)(2,1)S(1)} %shard_map.53), channel_id=1, source_target_pairs={{0,1},{1,0},{2,3},{3,2},{4,5},{5,4},{6,7},{7,6},{8,9},{9,8},{10,11... | collective-permute-start | bytes 1572872 | tf_op jit(solution)/shard_map/ppermute | solution.py:24
  87.3 6.4 %collective-permute-start.28 = (bf16[256,256]{1,0:T(8,128)(2,1)S(1)}, bf16[256,256]{1,0:T(8,128)(2,1)S(1)}, u32[]{:S(2)}, u32[]{:S(2)}) collective-permute-start(bf16[256,256]{1,0:T(8,128)(2,1)S(1)} %get-tuple-element.45), channel_id=1, source_target_pairs={{0,2},{2,0},{4,6},{6,4},{1,3},{3,1},{5,7},{7,5},{8,10},{10,8},{12,... | collective-permute-start | bytes 393224 | tf_op jit(solution)/shard_map/ppermute | solution.py:24
  87.6 8.2 %collective-permute-start.25 = (bf16[256,256]{1,0:T(8,128)(2,1)S(1)}, bf16[256,256]{1,0:T(8,128)(2,1)S(1)}, u32[]{:S(2)}, u32[]{:S(2)}) collective-permute-start(bf16[256,256]{1,0:T(8,128)(2,1)S(1)} %get-tuple-element.41), channel_id=1, source_target_pairs={{0,2},{2,0},{4,6},{6,4},{1,3},{3,1},{5,7},{7,5},{8,10},{10,8},{12,... | collective-permute-start | bytes 393224 | tf_op jit(solution)/shard_map/ppermute | solution.py:24
  93.8 11.8 %collective-permute-start.29 = (bf16[256,256]{1,0:T(8,128)(2,1)S(1)}, bf16[256,256]{1,0:T(8,128)(2,1)S(1)}, u32[]{:S(2)}, u32[]{:S(2)}) collective-permute-start(bf16[256,256]{1,0:T(8,128)(2,1)S(1)} %get-tuple-element.47), channel_id=1, source_target_pairs={{0,4},{2,6},{4,0},{6,2},{1,5},{3,7},{5,1},{7,3},{8,12},{10,14},{12... | collective-permute-start | bytes 393224 | tf_op jit(solution)/shard_map/ppermute | solution.py:24
  95.8 11.4 %collective-permute-start.26 = (bf16[256,256]{1,0:T(8,128)(2,1)S(1)}, bf16[256,256]{1,0:T(8,128)(2,1)S(1)}, u32[]{:S(2)}, u32[]{:S(2)}) collective-permute-start(bf16[256,256]{1,0:T(8,128)(2,1)S(1)} %get-tuple-element.43), channel_id=1, source_target_pairs={{0,4},{2,6},{4,0},{6,2},{1,5},{3,7},{5,1},{7,3},{8,12},{10,14},{12... | collective-permute-start | bytes 393224 | tf_op jit(solution)/shard_map/ppermute | solution.py:24
  105.7 6.0 %collective-permute-start.33 = (bf16[256,256]{1,0:T(8,128)(2,1)S(1)}, bf16[256,256]{1,0:T(8,128)(2,1)S(1)}, u32[]{:S(2)}, u32[]{:S(2)}) collective-permute-start(bf16[256,256]{1,0:T(8,128)(2,1)S(1)} %shard_map.59.refs_2_), channel_id=1, source_target_pairs={{0,2},{2,0},{4,6},{6,4},{1,3},{3,1},{5,7},{7,5},{8,10},{10,8},{12,... | collective-permute-start | bytes 393224 | tf_op jit(solution)/shard_map/ppermute | solution.py:24
  107.3 5.8 %collective-permute-start.31 = (bf16[256,256]{1,0:T(8,128)(2,1)S(1)}, bf16[256,256]{1,0:T(8,128)(2,1)S(1)}, u32[]{:S(2)}, u32[]{:S(2)}) collective-permute-start(bf16[256,256]{1,0:T(8,128)(2,1)S(1)} %shard_map.56.refs_0_), channel_id=1, source_target_pairs={{0,2},{2,0},{4,6},{6,4},{1,3},{3,1},{5,7},{7,5},{8,10},{10,8},{12,... | collective-permute-start | bytes 393224 | tf_op jit(solution)/shard_map/ppermute | solution.py:24
  108.1 5.0 %collective-permute-start.30 = (bf16[256,256]{1,0:T(8,128)(2,1)S(1)}, bf16[256,256]{1,0:T(8,128)(2,1)S(1)}, u32[]{:S(2)}, u32[]{:S(2)}) collective-permute-start(bf16[256,256]{1,0:T(8,128)(2,1)S(1)} %shard_map.59.refs_2_), channel_id=1, source_target_pairs={{0,1},{1,0},{2,3},{3,2},{4,5},{5,4},{6,7},{7,6},{8,9},{9,8},{10,11... | collective-permute-start | bytes 393224 | tf_op jit(solution)/shard_map/ppermute | solution.py:24
  108.1 5.0 %collective-permute-start.27 = (bf16[256,256]{1,0:T(8,128)(2,1)S(1)}, bf16[256,256]{1,0:T(8,128)(2,1)S(1)}, u32[]{:S(2)}, u32[]{:S(2)}) collective-permute-start(bf16[256,256]{1,0:T(8,128)(2,1)S(1)} %shard_map.56.refs_0_), channel_id=1, source_target_pairs={{0,1},{1,0},{2,3},{3,2},{4,5},{5,4},{6,7},{7,6},{8,9},{9,8},{10,11... | collective-permute-start | bytes 393224 | tf_op jit(solution)/shard_map/ppermute | solution.py:24
  111.7 2.7 %collective-permute-start.34 = (bf16[256,256]{1,0:T(8,128)(2,1)S(1)}, bf16[256,256]{1,0:T(8,128)(2,1)S(1)}, u32[]{:S(2)}, u32[]{:S(2)}) collective-permute-start(bf16[256,256]{1,0:T(8,128)(2,1)S(1)} %collective-permute-done.33.refs_2_), channel_id=1, source_target_pairs={{0,1},{1,0},{2,3},{3,2},{4,5},{5,4},{6,7},{7,6},{8,9},{9,8},{10,11... | collective-permute-start | bytes 393224 | tf_op jit(solution)/shard_map/ppermute | solution.py:24
  113.1 1.3 collective-permute-start.32
  116.0 8.1 %collective-permute-start.35 = (bf16[64,2048]{1,0:T(8,128)(2,1)S(1)}, bf16[64,2048]{1,0:T(8,128)(2,1)S(1)}, u32[]{:S(2)}, u32[]{:S(2)}) collective-permute-start(bf16[64,2048]{1,0:T(8,128)(2,1)S(1)} %get-tuple-element.56), channel_id=1, source_target_pairs={{0,128},{1,17},{8,136},{9,25},{16,144},{17,1},{24,152},{25,9},{64,... | collective-permute-start | bytes 786440 | tf_op jit(solution)/shard_map/ppermute | solution.py:34
  118.0 8.8 %collective-permute-start.37 = (bf16[64,2048]{1,0:T(8,128)(2,1)S(1)}, bf16[64,2048]{1,0:T(8,128)(2,1)S(1)}, u32[]{:S(2)}, u32[]{:S(2)}) collective-permute-start(bf16[64,2048]{1,0:T(8,128)(2,1)S(1)} %get-tuple-element.57), channel_id=1, source_target_pairs={{0,192},{1,25},{8,200},{9,17},{16,208},{17,9},{24,216},{25,1},{64,... | collective-permute-start | bytes 786440 | tf_op jit(solution)/shard_map/ppermute | solution.py:34
  120.3 6.8 %collective-permute-start.36 = (bf16[64,2048]{1,0:T(8,128)(2,1)S(1)}, bf16[64,2048]{1,0:T(8,128)(2,1)S(1)}, u32[]{:S(2)}, u32[]{:S(2)}) collective-permute-start(bf16[64,2048]{1,0:T(8,128)(2,1)S(1)} %get-tuple-element.58), channel_id=1, source_target_pairs={{0,64},{1,9},{8,72},{9,1},{16,80},{17,25},{24,88},{25,17},{64,0},{... | collective-permute-start | bytes 786440 | tf_op jit(solution)/shard_map/ppermute | solution.py:34
  127.2 5.9 %collective-permute-start.38 = (bf16[16,2048]{1,0:T(8,128)(2,1)S(1)}, bf16[16,2048]{1,0:T(8,128)(2,1)S(1)}, u32[]{:S(2)}, u32[]{:S(2)}) collective-permute-start(bf16[16,2048]{1,0:T(8,128)(2,1)S(1)} %get-tuple-element.62), channel_id=1, source_target_pairs={{0,16},{1,129},{8,24},{9,137},{16,0},{17,145},{24,8},{25,153},{64,... | collective-permute-start | bytes 196616 | tf_op jit(solution)/shard_map/ppermute | solution.py:34
  128.8 4.9 %collective-permute-start.40 = (bf16[16,2048]{1,0:T(8,128)(2,1)S(1)}, bf16[16,2048]{1,0:T(8,128)(2,1)S(1)}, u32[]{:S(2)}, u32[]{:S(2)}) collective-permute-start(bf16[16,2048]{1,0:T(8,128)(2,1)S(1)} %get-tuple-element.63), channel_id=1, source_target_pairs={{0,24},{1,193},{8,16},{9,201},{16,8},{17,209},{24,0},{25,217},{64,... | collective-permute-start | bytes 196616 | tf_op jit(solution)/shard_map/ppermute | solution.py:34
  130.3 4.3 %collective-permute-start.39 = (bf16[16,2048]{1,0:T(8,128)(2,1)S(1)}, bf16[16,2048]{1,0:T(8,128)(2,1)S(1)}, u32[]{:S(2)}, u32[]{:S(2)}) collective-permute-start(bf16[16,2048]{1,0:T(8,128)(2,1)S(1)} %get-tuple-element.64), channel_id=1, source_target_pairs={{0,8},{1,65},{8,0},{9,73},{16,24},{17,81},{24,16},{25,89},{64,72},... | collective-permute-start | bytes 196616 | tf_op jit(solution)/shard_map/ppermute | solution.py:34
  134.6 8.3 %collective-permute-start.41 = (f32[8,2048]{1,0:T(8,128)S(1)}, f32[8,2048]{1,0:T(8,128)S(1)}, u32[]{:S(2)}, u32[]{:S(2)}) collective-permute-start(f32[8,2048]{1,0:T(8,128)S(1)} %constant_dynamic-slice_fusion), channel_id=1, source_target_pairs={{0,32},{32,0},{1,33},{33,1},{2,34},{34,2},{3,35},{35,3},{4,36},{36... | collective-permute-start | bytes 196616 | tf_op jit(solution)/shard_map/ppermute | solution.py:24

commit v4 on v3

--- a/solution.py
+++ b/solution.py
@@ -43,7 +43,7 @@
 
 def gather_four(part, stage):
     got = {i: swap_xy(part, stage, i) for i in (2, 1, 3)}
-    return jnp.stack([part, got[1], got[2], got[3]])
+    return [part, got[1], got[2], got[3]]
 
 
 def call(kernel, outs, *args, specs=None, scratch=(), flops=0, limit=16):
@@ -157,11 +157,26 @@
         out_ref[...] = jnp.concatenate(blocks, 0)
 
 
-def in_order_a(rows):
-    def kernel(rows_ref, out_ref):
-        reorder(rows_ref, out_ref)
-
-    return call(kernel, [(rows.shape, BF16)], rows, flops=2**20)[0]
+def in_order_a(parts):
+    rows, features = parts[0].shape
+
+    def kernel(*refs):
+        *part_refs, out_ref = refs
+        core = lax.axis_index("c")
+
+        @pl.when(core == 0)
+        def _():
+            for outer, ref in enumerate(part_refs):
+                out_ref[pl.ds(outer * rows, rows)] = ref[...]
+
+        @pl.when(core == 1)
+        def _():
+            for outer, ref in enumerate(part_refs):
+                for inner in range(4):
+                    at = pl.ds((inner * 4 + outer) * ROWS, ROWS)
+                    out_ref[at] = ref[pl.ds(inner * ROWS, ROWS)]
+
+    return call(kernel, [((4 * rows, features), BF16)], *parts, flops=2**20)[0]
 
 
 def add_piece(own, theirs, piece):
@@ -266,9 +281,8 @@
 
 
 def spread(rounded):
-    part = gather_four(rounded, 1).reshape(4 * ROWS, -1)
-    full = gather_four(part, 0).reshape(16 * ROWS, -1)
-    return in_order_a(full)
+    part = jnp.concatenate(gather_four(rounded, 1), 0)
+    return in_order_a(gather_four(part, 0))
 
 
 def shards(activations, probes):

time: 145 us -> 145 us (level)
  no operation moved by 1% of the time
where the time goes in v4:
time: 145 us; the launch traced here: 143 us
  waiting for transfers between devices  69.6 us (48%)
  starting transfers between devices  57.3 us (40%)
  Pallas kernels  13.8 us (10%)
    ppermute x24, waiting for transfers between devices, swap(): lax.ppermute(value, axis, [(i, i ^ mask) for i in range(SIZES[axis])])  40 us
    ppermute x24, starting transfers between devices, swap(): lax.ppermute(value, axis, [(i, i ^ mask) for i in range(SIZES[axis])])  29.8 us
    ppermute x18, waiting for transfers between devices, swap_xy(): return lax.ppermute(value, ('x', 'y', 'c'), pairs)  29.7 us
    ppermute x18, starting transfers between devices, swap_xy(): return lax.ppermute(value, ('x', 'y', 'c'), pairs)  27.5 us
    pallas_call x21, Pallas kernels, call(): pl.pallas_call(kernel, in_specs=specs or [VMEM] * len(args), out_specs=[V...  13.8 us
  transfers between devices with their start and end apart: 42, of which 31 were waited for; matrix products, arithmetic and copies ran while one was open for 0% of the time, Pallas kernels for 4%

profile of v4, /device:TPU:8, one launch (start us, length us, event | category | flops | bytes accessed | tf_op | source)
XLA Modules:
  0.0 143.4 jit_solution(10576085941751535943)
XLA Ops:
  0.6 3.8 %shard_map.41 = (bf16[1024,2048]{1,0:T(8,128)(2,1)S(1)}, bf16[1024,2048]{1,0:T(8,128)(2,1)S(1)}, bf16[256,2048]{1,0:T(8,128)(2,1)S(1)}, bf16[1024,256]{1,0:T(8,128)(2,1)S(1)}) custom-call(bf16[2048,2048]{1,0:T(8,128)(2,1)} %x_hbm.1, bf16[256,2048]{1,0:T(8,128)(2,1)} %p_hbm.1), custom_call_target="tpu_custom_call" | custom-call | flops 1073741824 | bytes 1048576 | tf_op jit(solution)/shard_map/pallas_call | solution.py:50
  4.6 1.3 shard_map.42.own_ref
  6.5 2.0 %collective-permute-start.4 = (bf16[256,256]{1,0:T(8,128)(2,1)S(1)}, bf16[256,256]{1,0:T(8,128)(2,1)S(1)}, u32[]{:S(2)}, u32[]{:S(2)}) collective-permute-start(bf16[256,256]{1,0:T(8,128)(2,1)S(1)} %get-tuple-element.35), channel_id=1, source_target_pairs={{0,2},{2,0},{4,6},{6,4},{1,3},{3,1},{5,7},{7,5},{8,10},{10,8},{12,... | collective-permute-start | bytes 393224 | tf_op jit(solution)/shard_map/ppermute | solution.py:24
  8.8 4.2 %collective-permute-done.4.got_ref = bf16[256,256]{1,0:T(8,128)(2,1)S(1)} collective-permute-done((bf16[256,256]{1,0:T(8,128)(2,1)S(1)}, bf16[256,256]{1,0:T(8,128)(2,1)S(1)}, u32[]{:S(2)}, u32[]{:S(2)}) %collective-permute-start.4) | collective-permute-done | bytes 131104 | tf_op jit(solution)/shard_map/ppermute | solution.py:24
  13.0 3.4 %collective-permute-start.5 = (bf16[256,256]{1,0:T(8,128)(2,1)S(1)}, bf16[256,256]{1,0:T(8,128)(2,1)S(1)}, u32[]{:S(2)}, u32[]{:S(2)}) collective-permute-start(bf16[256,256]{1,0:T(8,128)(2,1)S(1)} %get-tuple-element.37), channel_id=1, source_target_pairs={{0,4},{2,6},{4,0},{6,2},{1,5},{3,7},{5,1},{7,3},{8,12},{10,14},{12... | collective-permute-start | bytes 393224 | tf_op jit(solution)/shard_map/ppermute | solution.py:24
  16.4 2.8 %collective-permute-start.2 = (bf16[256,256]{1,0:T(8,128)(2,1)S(1)}, bf16[256,256]{1,0:T(8,128)(2,1)S(1)}, u32[]{:S(2)}, u32[]{:S(2)}) collective-permute-start(bf16[256,256]{1,0:T(8,128)(2,1)S(1)} %get-tuple-element.33), channel_id=1, source_target_pairs={{0,4},{2,6},{4,0},{6,2},{1,5},{3,7},{5,1},{7,3},{8,12},{10,14},{12... | collective-permute-start | bytes 393224 | tf_op jit(solution)/shard_map/ppermute | solution.py:24
  19.1 6.5 %collective-permute-done.5.got_ref = bf16[256,256]{1,0:T(8,128)(2,1)S(1)} collective-permute-done((bf16[256,256]{1,0:T(8,128)(2,1)S(1)}, bf16[256,256]{1,0:T(8,128)(2,1)S(1)}, u32[]{:S(2)}, u32[]{:S(2)}) %collective-permute-start.5) | collective-permute-done | bytes 131104 | tf_op jit(solution)/shard_map/ppermute | solution.py:24
  26.2 1.3 collective-permute-done.2.got_ref
  28.7 3.3 %collective-permute-done.9.refs_2_ = bf16[256,256]{1,0:T(8,128)(2,1)S(1)} collective-permute-done((bf16[256,256]{1,0:T(8,128)(2,1)S(1)}, bf16[256,256]{1,0:T(8,128)(2,1)S(1)}, u32[]{:S(2)}, u32[]{:S(2)}) %collective-permute-start.9) | collective-permute-done | bytes 131104 | tf_op jit(solution)/shard_map/ppermute | solution.py:24
  32.0 1.4 collective-permute-done.7.refs_0_
  33.4 1.3 shard_map.49.y_ref
  34.7 1.5 %shard_map.50 = (f32[64,2048]{1,0:T(8,128)S(1)}, bf16[3,64,2048]{2,1,0:T(8,128)(2,1)S(1)}) custom-call(f32[256,2048]{1,0:T(8,128)S(1)} %shard_map.49.y_ref, bf16[1024,2048]{1,0:T(8,128)(2,1)S(1)} %get-tuple-element.26.x_ref.xo_ref, bf16[1024,2048]{1,0:T(8,128)(2,1)S(1)} %get-tuple-element.27.xt_ref.x_ref, ...), custom_call_target="tpu_custom_call" | custom-call | flops 1073741824 | bytes 1048576 | tf_op jit(solution)/shard_map/pallas_call | solution.py:50
  36.3 3.1 %collective-permute-start.11 = (bf16[64,2048]{1,0:T(8,128)(2,1)S(1)}, bf16[64,2048]{1,0:T(8,128)(2,1)S(1)}, u32[]{:S(2)}, u32[]{:S(2)}) collective-permute-start(bf16[64,2048]{1,0:T(8,128)(2,1)S(1)} %get-tuple-element.59), channel_id=1, source_target_pairs={{0,128},{1,17},{8,136},{9,25},{16,144},{17,1},{24,152},{25,9},{64,... | collective-permute-start | bytes 786440 | tf_op jit(solution)/shard_map/ppermute | solution.py:34
  39.5 1.1 collective-permute-start.13
  40.6 3.7 %collective-permute-done.11 = bf16[64,2048]{1,0:T(8,128)(2,1)S(1)} collective-permute-done((bf16[64,2048]{1,0:T(8,128)(2,1)S(1)}, bf16[64,2048]{1,0:T(8,128)(2,1)S(1)}, u32[]{:S(2)}, u32[]{:S(2)}) %collective-permute-start.11) | collective-permute-done | bytes 262176 | tf_op jit(solution)/shard_map/ppermute | solution.py:34
  44.3 2.8 %collective-permute-done.13 = bf16[64,2048]{1,0:T(8,128)(2,1)S(1)} collective-permute-done((bf16[64,2048]{1,0:T(8,128)(2,1)S(1)}, bf16[64,2048]{1,0:T(8,128)(2,1)S(1)}, u32[]{:S(2)}, u32[]{:S(2)}) %collective-permute-start.13) | collective-permute-done | bytes 262176 | tf_op jit(solution)/shard_map/ppermute | solution.py:34
  47.4 2.4 %collective-permute-start.14 = (bf16[16,2048]{1,0:T(8,128)(2,1)S(1)}, bf16[16,2048]{1,0:T(8,128)(2,1)S(1)}, u32[]{:S(2)}, u32[]{:S(2)}) collective-permute-start(bf16[16,2048]{1,0:T(8,128)(2,1)S(1)} %get-tuple-element.65), channel_id=1, source_target_pairs={{0,16},{1,129},{8,24},{9,137},{16,0},{17,145},{24,8},{25,153},{64,... | collective-permute-start | bytes 196616 | tf_op jit(solution)/shard_map/ppermute | solution.py:34
  49.8 2.4 %collective-permute-start.15 = (bf16[16,2048]{1,0:T(8,128)(2,1)S(1)}, bf16[16,2048]{1,0:T(8,128)(2,1)S(1)}, u32[]{:S(2)}, u32[]{:S(2)}) collective-permute-start(bf16[16,2048]{1,0:T(8,128)(2,1)S(1)} %get-tuple-element.67), channel_id=1, source_target_pairs={{0,8},{1,65},{8,0},{9,73},{16,24},{17,81},{24,16},{25,89},{64,72},... | collective-permute-start | bytes 196616 | tf_op jit(solution)/shard_map/ppermute | solution.py:34
  54.5 6.1 %collective-permute-start.17 = (bf16[16,2048]{1,0:T(8,128)(2,1)S(1)}, bf16[16,2048]{1,0:T(8,128)(2,1)S(1)}, u32[]{:S(2)}, u32[]{:S(2)}) collective-permute-start(bf16[16,2048]{1,0:T(8,128)(2,1)S(1)} %fusion.4), channel_id=1, source_target_pairs={{0,32},{32,0},{1,33},{33,1},{2,34},{34,2},{3,35},{35,3},{4,36},{36... | collective-permute-start | bytes 196616 | tf_op jit(solution)/shard_map/ppermute | solution.py:24
  60.5 2.3 %collective-permute-done.17 = bf16[16,2048]{1,0:T(8,128)(2,1)S(1)} collective-permute-done((bf16[16,2048]{1,0:T(8,128)(2,1)S(1)}, bf16[16,2048]{1,0:T(8,128)(2,1)S(1)}, u32[]{:S(2)}, u32[]{:S(2)}) %collective-permute-start.17) | collective-permute-done | bytes 65568 | tf_op jit(solution)/shard_map/ppermute | solution.py:24
  62.9 1.8 %collective-permute-start.20 = (bf16[16,2048]{1,0:T(8,128)(2,1)S(1)}, bf16[16,2048]{1,0:T(8,128)(2,1)S(1)}, u32[]{:S(2)}, u32[]{:S(2)}) collective-permute-start(bf16[16,2048]{1,0:T(8,128)(2,1)S(1)} %get-tuple-element.52), channel_id=1, source_target_pairs={{0,24},{1,193},{8,16},{9,201},{16,8},{17,209},{24,0},{25,217},{64,... | collective-permute-start | bytes 196616 | tf_op jit(solution)/shard_map/ppermute | solution.py:34
  64.7 2.6 %collective-permute-start.19 = (bf16[16,2048]{1,0:T(8,128)(2,1)S(1)}, bf16[16,2048]{1,0:T(8,128)(2,1)S(1)}, u32[]{:S(2)}, u32[]{:S(2)}) collective-permute-start(bf16[16,2048]{1,0:T(8,128)(2,1)S(1)} %get-tuple-element.52), channel_id=1, source_target_pairs={{0,16},{1,129},{8,24},{9,137},{16,0},{17,145},{24,8},{25,153},{64,... | collective-permute-start | bytes 196616 | tf_op jit(solution)/shard_map/ppermute | solution.py:34
  67.3 3.2 %collective-permute-done.19 = bf16[16,2048]{1,0:T(8,128)(2,1)S(1)} collective-permute-done((bf16[16,2048]{1,0:T(8,128)(2,1)S(1)}, bf16[16,2048]{1,0:T(8,128)(2,1)S(1)}, u32[]{:S(2)}, u32[]{:S(2)}) %collective-permute-start.19) | collective-permute-done | bytes 65568 | tf_op jit(solution)/shard_map/ppermute | solution.py:34
  71.6 4.0 %collective-permute-start.23 = (bf16[64,2048]{1,0:T(8,128)(2,1)S(1)}, bf16[64,2048]{1,0:T(8,128)(2,1)S(1)}, u32[]{:S(2)}, u32[]{:S(2)}) collective-permute-start(bf16[64,2048]{1,0:T(8,128)(2,1)S(1)} %pad_maximum_fusion.refs_0_), channel_id=1, source_target_pairs={{0,192},{1,25},{8,200},{9,17},{16,208},{17,9},{24,216},{25,1},{64,... | collective-permute-start | bytes 786440 | tf_op jit(solution)/shard_map/ppermute | solution.py:34
  76.6 5.7 %collective-permute-done.23.refs_3_ = bf16[64,2048]{1,0:T(8,128)(2,1)S(1)} collective-permute-done((bf16[64,2048]{1,0:T(8,128)(2,1)S(1)}, bf16[64,2048]{1,0:T(8,128)(2,1)S(1)}, u32[]{:S(2)}, u32[]{:S(2)}) %collective-permute-start.23) | collective-permute-done | bytes 262176 | tf_op jit(solution)/shard_map/ppermute | solution.py:34
  82.3 1.2 collective-permute-done.22.refs_2_
  83.8 1.3 shard_map.53
  85.2 1.3 shard_map.52.own_ref
  87.4 2.0 %collective-permute-start.25 = (bf16[256,256]{1,0:T(8,128)(2,1)S(1)}, bf16[256,256]{1,0:T(8,128)(2,1)S(1)}, u32[]{:S(2)}, u32[]{:S(2)}) collective-permute-start(bf16[256,256]{1,0:T(8,128)(2,1)S(1)} %get-tuple-element.41), channel_id=1, source_target_pairs={{0,2},{2,0},{4,6},{6,4},{1,3},{3,1},{5,7},{7,5},{8,10},{10,8},{12,... | collective-permute-start | bytes 393224 | tf_op jit(solution)/shard_map/ppermute | solution.py:24
  89.4 4.2 %collective-permute-done.28.got_ref = bf16[256,256]{1,0:T(8,128)(2,1)S(1)} collective-permute-done((bf16[256,256]{1,0:T(8,128)(2,1)S(1)}, bf16[256,256]{1,0:T(8,128)(2,1)S(1)}, u32[]{:S(2)}, u32[]{:S(2)}) %collective-permute-start.28) | collective-permute-done | bytes 131104 | tf_op jit(solution)/shard_map/ppermute | solution.py:24
  93.6 1.9 %collective-permute-start.29 = (bf16[256,256]{1,0:T(8,128)(2,1)S(1)}, bf16[256,256]{1,0:T(8,128)(2,1)S(1)}, u32[]{:S(2)}, u32[]{:S(2)}) collective-permute-start(bf16[256,256]{1,0:T(8,128)(2,1)S(1)} %get-tuple-element.47), channel_id=1, source_target_pairs={{0,4},{2,6},{4,0},{6,2},{1,5},{3,7},{5,1},{7,3},{8,12},{10,14},{12... | collective-permute-start | bytes 393224 | tf_op jit(solution)/shard_map/ppermute | solution.py:24
  95.6 2.7 %collective-permute-start.26 = (bf16[256,256]{1,0:T(8,128)(2,1)S(1)}, bf16[256,256]{1,0:T(8,128)(2,1)S(1)}, u32[]{:S(2)}, u32[]{:S(2)}) collective-permute-start(bf16[256,256]{1,0:T(8,128)(2,1)S(1)} %get-tuple-element.43), channel_id=1, source_target_pairs={{0,4},{2,6},{4,0},{6,2},{1,5},{3,7},{5,1},{7,3},{8,12},{10,14},{12... | collective-permute-start | bytes 393224 | tf_op jit(solution)/shard_map/ppermute | solution.py:24
  98.4 7.1 %collective-permute-done.29.got_ref = bf16[256,256]{1,0:T(8,128)(2,1)S(1)} collective-permute-done((bf16[256,256]{1,0:T(8,128)(2,1)S(1)}, bf16[256,256]{1,0:T(8,128)(2,1)S(1)}, u32[]{:S(2)}, u32[]{:S(2)}) %collective-permute-start.29) | collective-permute-done | bytes 131104 | tf_op jit(solution)/shard_map/ppermute | solution.py:24
  105.6 1.5 %collective-permute-done.26.got_ref = bf16[256,256]{1,0:T(8,128)(2,1)S(1)} collective-permute-done((bf16[256,256]{1,0:T(8,128)(2,1)S(1)}, bf16[256,256]{1,0:T(8,128)(2,1)S(1)}, u32[]{:S(2)}, u32[]{:S(2)}) %collective-permute-start.26) | collective-permute-done | bytes 131104 | tf_op jit(solution)/shard_map/ppermute | solution.py:24
  108.5 3.0 %collective-permute-done.33.refs_2_ = bf16[256,256]{1,0:T(8,128)(2,1)S(1)} collective-permute-done((bf16[256,256]{1,0:T(8,128)(2,1)S(1)}, bf16[256,256]{1,0:T(8,128)(2,1)S(1)}, u32[]{:S(2)}, u32[]{:S(2)}) %collective-permute-start.33) | collective-permute-done | bytes 131104 | tf_op jit(solution)/shard_map/ppermute | solution.py:24
  111.5 1.4 collective-permute-done.31.refs_0_
  112.9 1.3 shard_map.60.y_ref
  114.2 1.5 %shard_map.61 = (f32[64,2048]{1,0:T(8,128)S(1)}, bf16[3,64,2048]{2,1,0:T(8,128)(2,1)S(1)}) custom-call(f32[256,2048]{1,0:T(8,128)S(1)} %shard_map.60.y_ref, bf16[1024,2048]{1,0:T(8,128)(2,1)S(1)} %get-tuple-element.26.x_ref.xo_ref, bf16[1024,2048]{1,0:T(8,128)(2,1)S(1)} %get-tuple-element.27.xt_ref.x_ref, ...), custom_call_target="tpu_custom_call" | custom-call | flops 1073741824 | bytes 1048576 | tf_op jit(solution)/shard_map/pallas_call | solution.py:50
  115.9 2.0 %collective-permute-start.35 = (bf16[64,2048]{1,0:T(8,128)(2,1)S(1)}, bf16[64,2048]{1,0:T(8,128)(2,1)S(1)}, u32[]{:S(2)}, u32[]{:S(2)}) collective-permute-start(bf16[64,2048]{1,0:T(8,128)(2,1)S(1)} %get-tuple-element.56), channel_id=1, source_target_pairs={{0,128},{1,17},{8,136},{9,25},{16,144},{17,1},{24,152},{25,9},{64,... | collective-permute-start | bytes 786440 | tf_op jit(solution)/shard_map/ppermute | solution.py:34
  117.9 2.3 %collective-permute-start.37 = (bf16[64,2048]{1,0:T(8,128)(2,1)S(1)}, bf16[64,2048]{1,0:T(8,128)(2,1)S(1)}, u32[]{:S(2)}, u32[]{:S(2)}) collective-permute-start(bf16[64,2048]{1,0:T(8,128)(2,1)S(1)} %get-tuple-element.57), channel_id=1, source_target_pairs={{0,192},{1,25},{8,200},{9,17},{16,208},{17,9},{24,216},{25,1},{64,... | collective-permute-start | bytes 786440 | tf_op jit(solution)/shard_map/ppermute | solution.py:34
  120.1 3.8 %collective-permute-done.35 = bf16[64,2048]{1,0:T(8,128)(2,1)S(1)} collective-permute-done((bf16[64,2048]{1,0:T(8,128)(2,1)S(1)}, bf16[64,2048]{1,0:T(8,128)(2,1)S(1)}, u32[]{:S(2)}, u32[]{:S(2)}) %collective-permute-start.35) | collective-permute-done | bytes 262176 | tf_op jit(solution)/shard_map/ppermute | solution.py:34
  123.9 2.7 %collective-permute-done.37 = bf16[64,2048]{1,0:T(8,128)(2,1)S(1)} collective-permute-done((bf16[64,2048]{1,0:T(8,128)(2,1)S(1)}, bf16[64,2048]{1,0:T(8,128)(2,1)S(1)}, u32[]{:S(2)}, u32[]{:S(2)}) %collective-permute-start.37) | collective-permute-done | bytes 262176 | tf_op jit(solution)/shard_map/ppermute | solution.py:34
  127.1 1.6 %collective-permute-start.38 = (bf16[16,2048]{1,0:T(8,128)(2,1)S(1)}, bf16[16,2048]{1,0:T(8,128)(2,1)S(1)}, u32[]{:S(2)}, u32[]{:S(2)}) collective-permute-start(bf16[16,2048]{1,0:T(8,128)(2,1)S(1)} %get-tuple-element.62), channel_id=1, source_target_pairs={{0,16},{1,129},{8,24},{9,137},{16,0},{17,145},{24,8},{25,153},{64,... | collective-permute-start | bytes 196616 | tf_op jit(solution)/shard_map/ppermute | solution.py:34
  128.7 1.5 %collective-permute-start.40 = (bf16[16,2048]{1,0:T(8,128)(2,1)S(1)}, bf16[16,2048]{1,0:T(8,128)(2,1)S(1)}, u32[]{:S(2)}, u32[]{:S(2)}) collective-permute-start(bf16[16,2048]{1,0:T(8,128)(2,1)S(1)} %get-tuple-element.63), channel_id=1, source_target_pairs={{0,24},{1,193},{8,16},{9,201},{16,8},{17,209},{24,0},{25,217},{64,... | collective-permute-start | bytes 196616 | tf_op jit(solution)/shard_map/ppermute | solution.py:34
  130.2 1.7 %collective-permute-start.39 = (bf16[16,2048]{1,0:T(8,128)(2,1)S(1)}, bf16[16,2048]{1,0:T(8,128)(2,1)S(1)}, u32[]{:S(2)}, u32[]{:S(2)}) collective-permute-start(bf16[16,2048]{1,0:T(8,128)(2,1)S(1)} %get-tuple-element.64), channel_id=1, source_target_pairs={{0,8},{1,65},{8,0},{9,73},{16,24},{17,81},{24,16},{25,89},{64,72},... | collective-permute-start | bytes 196616 | tf_op jit(solution)/shard_map/ppermute | solution.py:34
  131.9 1.1 collective-permute-done.38
  134.5 5.1 %collective-permute-start.41 = (f32[8,2048]{1,0:T(8,128)S(1)}, f32[8,2048]{1,0:T(8,128)S(1)}, u32[]{:S(2)}, u32[]{:S(2)}) collective-permute-start(f32[8,2048]{1,0:T(8,128)S(1)} %constant_dynamic-slice_fusion), channel_id=1, source_target_pairs={{0,32},{32,0},{1,33},{33,1},{2,34},{34,2},{3,35},{35,3},{4,36},{36... | collective-permute-start | bytes 196616 | tf_op jit(solution)/shard_map/ppermute | solution.py:24
  140.2 2.5 %collective-permute-done.41 = f32[8,2048]{1,0:T(8,128)S(1)} collective-permute-done((f32[8,2048]{1,0:T(8,128)S(1)}, f32[8,2048]{1,0:T(8,128)S(1)}, u32[]{:S(2)}, u32[]{:S(2)}) %collective-permute-start.41) | collective-permute-done | bytes 65568 | tf_op jit(solution)/shard_map/ppermute | solution.py:24
  (70 shorter events, 13.9 us)
Async XLA Ops:
  4.5 2.0 %collective-permute-start = (bf16[1024,256]{1,0:T(8,128)(2,1)S(1)}, bf16[1024,256]{1,0:T(8,128)(2,1)S(1)}, u32[]{:S(2)}, u32[]{:S(2)}) collective-permute-start(bf16[1024,256]{1,0:T(8,128)(2,1)S(1)} %get-tuple-element.29), channel_id=1, source_target_pairs={{0,1},{1,0},{2,3},{3,2},{4,5},{5,4},{6,7},{7,6},{8,9},{9,8},{10,11... | collective-permute-start | bytes 1572872 | tf_op jit(solution)/shard_map/ppermute | solution.py:24
  6.5 6.4 %collective-permute-start.4 = (bf16[256,256]{1,0:T(8,128)(2,1)S(1)}, bf16[256,256]{1,0:T(8,128)(2,1)S(1)}, u32[]{:S(2)}, u32[]{:S(2)}) collective-permute-start(bf16[256,256]{1,0:T(8,128)(2,1)S(1)} %get-tuple-element.35), channel_id=1, source_target_pairs={{0,2},{2,0},{4,6},{6,4},{1,3},{3,1},{5,7},{7,5},{8,10},{10,8},{12,... | collective-permute-start | bytes 393224 | tf_op jit(solution)/shard_map/ppermute | solution.py:24
  8.6 7.8 %collective-permute-start.1 = (bf16[256,256]{1,0:T(8,128)(2,1)S(1)}, bf16[256,256]{1,0:T(8,128)(2,1)S(1)}, u32[]{:S(2)}, u32[]{:S(2)}) collective-permute-start(bf16[256,256]{1,0:T(8,128)(2,1)S(1)} %get-tuple-element.31), channel_id=1, source_target_pairs={{0,2},{2,0},{4,6},{6,4},{1,3},{3,1},{5,7},{7,5},{8,10},{10,8},{12,... | collective-permute-start | bytes 393224 | tf_op jit(solution)/shard_map/ppermute | solution.py:24
  13.0 12.6 %collective-permute-start.5 = (bf16[256,256]{1,0:T(8,128)(2,1)S(1)}, bf16[256,256]{1,0:T(8,128)(2,1)S(1)}, u32[]{:S(2)}, u32[]{:S(2)}) collective-permute-start(bf16[256,256]{1,0:T(8,128)(2,1)S(1)} %get-tuple-element.37), channel_id=1, source_target_pairs={{0,4},{2,6},{4,0},{6,2},{1,5},{3,7},{5,1},{7,3},{8,12},{10,14},{12... | collective-permute-start | bytes 393224 | tf_op jit(solution)/shard_map/ppermute | solution.py:24
  16.4 11.1 %collective-permute-start.2 = (bf16[256,256]{1,0:T(8,128)(2,1)S(1)}, bf16[256,256]{1,0:T(8,128)(2,1)S(1)}, u32[]{:S(2)}, u32[]{:S(2)}) collective-permute-start(bf16[256,256]{1,0:T(8,128)(2,1)S(1)} %get-tuple-element.33), channel_id=1, source_target_pairs={{0,4},{2,6},{4,0},{6,2},{1,5},{3,7},{5,1},{7,3},{8,12},{10,14},{12... | collective-permute-start | bytes 393224 | tf_op jit(solution)/shard_map/ppermute | solution.py:24
  25.6 6.4 %collective-permute-start.9 = (bf16[256,256]{1,0:T(8,128)(2,1)S(1)}, bf16[256,256]{1,0:T(8,128)(2,1)S(1)}, u32[]{:S(2)}, u32[]{:S(2)}) collective-permute-start(bf16[256,256]{1,0:T(8,128)(2,1)S(1)} %shard_map.48.refs_2_), channel_id=1, source_target_pairs={{0,2},{2,0},{4,6},{6,4},{1,3},{3,1},{5,7},{7,5},{8,10},{10,8},{12,... | collective-permute-start | bytes 393224 | tf_op jit(solution)/shard_map/ppermute | solution.py:24
  27.5 5.9 %collective-permute-start.7 = (bf16[256,256]{1,0:T(8,128)(2,1)S(1)}, bf16[256,256]{1,0:T(8,128)(2,1)S(1)}, u32[]{:S(2)}, u32[]{:S(2)}) collective-permute-start(bf16[256,256]{1,0:T(8,128)(2,1)S(1)} %shard_map.45.refs_0_), channel_id=1, source_target_pairs={{0,2},{2,0},{4,6},{6,4},{1,3},{3,1},{5,7},{7,5},{8,10},{10,8},{12,... | collective-permute-start | bytes 393224 | tf_op jit(solution)/shard_map/ppermute | solution.py:24
  28.1 5.3 %collective-permute-start.6 = (bf16[256,256]{1,0:T(8,128)(2,1)S(1)}, bf16[256,256]{1,0:T(8,128)(2,1)S(1)}, u32[]{:S(2)}, u32[]{:S(2)}) collective-permute-start(bf16[256,256]{1,0:T(8,128)(2,1)S(1)} %shard_map.48.refs_2_), channel_id=1, source_target_pairs={{0,1},{1,0},{2,3},{3,2},{4,5},{5,4},{6,7},{7,6},{8,9},{9,8},{10,11... | collective-permute-start | bytes 393224 | tf_op jit(solution)/shard_map/ppermute | solution.py:24
  28.1 5.3 %collective-permute-start.3 = (bf16[256,256]{1,0:T(8,128)(2,1)S(1)}, bf16[256,256]{1,0:T(8,128)(2,1)S(1)}, u32[]{:S(2)}, u32[]{:S(2)}) collective-permute-start(bf16[256,256]{1,0:T(8,128)(2,1)S(1)} %shard_map.45.refs_0_), channel_id=1, source_target_pairs={{0,1},{1,0},{2,3},{3,2},{4,5},{5,4},{6,7},{7,6},{8,9},{9,8},{10,11... | collective-permute-start | bytes 393224 | tf_op jit(solution)/shard_map/ppermute | solution.py:24
  32.0 2.7 %collective-permute-start.10 = (bf16[256,256]{1,0:T(8,128)(2,1)S(1)}, bf16[256,256]{1,0:T(8,128)(2,1)S(1)}, u32[]{:S(2)}, u32[]{:S(2)}) collective-permute-start(bf16[256,256]{1,0:T(8,128)(2,1)S(1)} %collective-permute-done.9.refs_2_), channel_id=1, source_target_pairs={{0,1},{1,0},{2,3},{3,2},{4,5},{5,4},{6,7},{7,6},{8,9},{9,8},{10,11... | collective-permute-start | bytes 393224 | tf_op jit(solution)/shard_map/ppermute | solution.py:24
  33.4 1.3 collective-permute-start.8
  36.3 8.0 %collective-permute-start.11 = (bf16[64,2048]{1,0:T(8,128)(2,1)S(1)}, bf16[64,2048]{1,0:T(8,128)(2,1)S(1)}, u32[]{:S(2)}, u32[]{:S(2)}) collective-permute-start(bf16[64,2048]{1,0:T(8,128)(2,1)S(1)} %get-tuple-element.59), channel_id=1, source_target_pairs={{0,128},{1,17},{8,136},{9,25},{16,144},{17,1},{24,152},{25,9},{64,... | collective-permute-start | bytes 786440 | tf_op jit(solution)/shard_map/ppermute | solution.py:34
  39.5 7.7 %collective-permute-start.13 = (bf16[64,2048]{1,0:T(8,128)(2,1)S(1)}, bf16[64,2048]{1,0:T(8,128)(2,1)S(1)}, u32[]{:S(2)}, u32[]{:S(2)}) collective-permute-start(bf16[64,2048]{1,0:T(8,128)(2,1)S(1)} %get-tuple-element.60), channel_id=1, source_target_pairs={{0,192},{1,25},{8,200},{9,17},{16,208},{17,9},{24,216},{25,1},{64,... | collective-permute-start | bytes 786440 | tf_op jit(solution)/shard_map/ppermute | solution.py:34
  40.6 6.6 %collective-permute-start.12 = (bf16[64,2048]{1,0:T(8,128)(2,1)S(1)}, bf16[64,2048]{1,0:T(8,128)(2,1)S(1)}, u32[]{:S(2)}, u32[]{:S(2)}) collective-permute-start(bf16[64,2048]{1,0:T(8,128)(2,1)S(1)} %get-tuple-element.61), channel_id=1, source_target_pairs={{0,64},{1,9},{8,72},{9,1},{16,80},{17,25},{24,88},{25,17},{64,0},{... | collective-permute-start | bytes 786440 | tf_op jit(solution)/shard_map/ppermute | solution.py:34
  47.4 5.9 %collective-permute-start.14 = (bf16[16,2048]{1,0:T(8,128)(2,1)S(1)}, bf16[16,2048]{1,0:T(8,128)(2,1)S(1)}, u32[]{:S(2)}, u32[]{:S(2)}) collective-permute-start(bf16[16,2048]{1,0:T(8,128)(2,1)S(1)} %get-tuple-element.65), channel_id=1, source_target_pairs={{0,16},{1,129},{8,24},{9,137},{16,0},{17,145},{24,8},{25,153},{64,... | collective-permute-start | bytes 196616 | tf_op jit(solution)/shard_map/ppermute | solution.py:34
  49.8 4.3 %collective-permute-start.16 = (bf16[16,2048]{1,0:T(8,128)(2,1)S(1)}, bf16[16,2048]{1,0:T(8,128)(2,1)S(1)}, u32[]{:S(2)}, u32[]{:S(2)}) collective-permute-start(bf16[16,2048]{1,0:T(8,128)(2,1)S(1)} %get-tuple-element.66), channel_id=1, source_target_pairs={{0,24},{1,193},{8,16},{9,201},{16,8},{17,209},{24,0},{25,217},{64,... | collective-permute-start | bytes 196616 | tf_op jit(solution)/shard_map/ppermute | solution.py:34
  49.8 4.7 %collective-permute-start.15 = (bf16[16,2048]{1,0:T(8,128)(2,1)S(1)}, bf16[16,2048]{1,0:T(8,128)(2,1)S(1)}, u32[]{:S(2)}, u32[]{:S(2)}) collective-permute-start(bf16[16,2048]{1,0:T(8,128)(2,1)S(1)} %get-tuple-element.67), channel_id=1, source_target_pairs={{0,8},{1,65},{8,0},{9,73},{16,24},{17,81},{24,16},{25,89},{64,72},... | collective-permute-start | bytes 196616 | tf_op jit(solution)/shard_map/ppermute | solution.py:34
  54.5 8.4 %collective-permute-start.17 = (bf16[16,2048]{1,0:T(8,128)(2,1)S(1)}, bf16[16,2048]{1,0:T(8,128)(2,1)S(1)}, u32[]{:S(2)}, u32[]{:S(2)}) collective-permute-start(bf16[16,2048]{1,0:T(8,128)(2,1)S(1)} %fusion.4), channel_id=1, source_target_pairs={{0,32},{32,0},{1,33},{33,1},{2,34},{34,2},{3,35},{35,3},{4,36},{36... | collective-permute-start | bytes 196616 | tf_op jit(solution)/shard_map/ppermute | solution.py:24
  62.9 4.4 %collective-permute-start.20 = (bf16[16,2048]{1,0:T(8,128)(2,1)S(1)}, bf16[16,2048]{1,0:T(8,128)(2,1)S(1)}, u32[]{:S(2)}, u32[]{:S(2)}) collective-permute-start(bf16[16,2048]{1,0:T(8,128)(2,1)S(1)} %get-tuple-element.52), channel_id=1, source_target_pairs={{0,24},{1,193},{8,16},{9,201},{16,8},{17,209},{24,0},{25,217},{64,... | collective-permute-start | bytes 196616 | tf_op jit(solution)/shard_map/ppermute | solution.py:34
  64.7 5.8 %collective-permute-start.19 = (bf16[16,2048]{1,0:T(8,128)(2,1)S(1)}, bf16[16,2048]{1,0:T(8,128)(2,1)S(1)}, u32[]{:S(2)}, u32[]{:S(2)}) collective-permute-start(bf16[16,2048]{1,0:T(8,128)(2,1)S(1)} %get-tuple-element.52), channel_id=1, source_target_pairs={{0,16},{1,129},{8,24},{9,137},{16,0},{17,145},{24,8},{25,153},{64,... | collective-permute-start | bytes 196616 | tf_op jit(solution)/shard_map/ppermute | solution.py:34
  67.3 4.3 %collective-permute-start.18 = (bf16[16,2048]{1,0:T(8,128)(2,1)S(1)}, bf16[16,2048]{1,0:T(8,128)(2,1)S(1)}, u32[]{:S(2)}, u32[]{:S(2)}) collective-permute-start(bf16[16,2048]{1,0:T(8,128)(2,1)S(1)} %get-tuple-element.52), channel_id=1, source_target_pairs={{0,8},{1,65},{8,0},{9,73},{16,24},{17,81},{24,16},{25,89},{64,72},... | collective-permute-start | bytes 196616 | tf_op jit(solution)/shard_map/ppermute | solution.py:34
  71.6 10.7 %collective-permute-start.23 = (bf16[64,2048]{1,0:T(8,128)(2,1)S(1)}, bf16[64,2048]{1,0:T(8,128)(2,1)S(1)}, u32[]{:S(2)}, u32[]{:S(2)}) collective-permute-start(bf16[64,2048]{1,0:T(8,128)(2,1)S(1)} %pad_maximum_fusion.refs_0_), channel_id=1, source_target_pairs={{0,192},{1,25},{8,200},{9,17},{16,208},{17,9},{24,216},{25,1},{64,... | collective-permute-start | bytes 786440 | tf_op jit(solution)/shard_map/ppermute | solution.py:34
  75.6 7.9 %collective-permute-start.22 = (bf16[64,2048]{1,0:T(8,128)(2,1)S(1)}, bf16[64,2048]{1,0:T(8,128)(2,1)S(1)}, u32[]{:S(2)}, u32[]{:S(2)}) collective-permute-start(bf16[64,2048]{1,0:T(8,128)(2,1)S(1)} %pad_maximum_fusion.refs_0_), channel_id=1, source_target_pairs={{0,128},{1,17},{8,136},{9,25},{16,144},{17,1},{24,152},{25,9},{64,... | collective-permute-start | bytes 786440 | tf_op jit(solution)/shard_map/ppermute | solution.py:34
  75.9 7.9 %collective-permute-start.21 = (bf16[64,2048]{1,0:T(8,128)(2,1)S(1)}, bf16[64,2048]{1,0:T(8,128)(2,1)S(1)}, u32[]{:S(2)}, u32[]{:S(2)}) collective-permute-start(bf16[64,2048]{1,0:T(8,128)(2,1)S(1)} %pad_maximum_fusion.refs_0_), channel_id=1, source_target_pairs={{0,64},{1,9},{8,72},{9,1},{16,80},{17,25},{24,88},{25,17},{64,0},{... | collective-permute-start | bytes 786440 | tf_op jit(solution)/shard_map/ppermute | solution.py:34
  85.1 2.0 %collective-permute-start.24 = (bf16[1024,256]{1,0:T(8,128)(2,1)S(1)}, bf16[1024,256]{1,0:T(8,128)(2,1)S(1)}, u32[]{:S(2)}, u32[]{:S(2)}) collective-permute-start(bf16[1024,256]{1,0:T(8,128)(2,1)S(1)} %shard_map.53), channel_id=1, source_target_pairs={{0,1},{1,0},{2,3},{3,2},{4,5},{5,4},{6,7},{7,6},{8,9},{9,8},{10,11... | collective-permute-start | bytes 1572872 | tf_op jit(solution)/shard_map/ppermute | solution.py:24
  87.2 6.4 %collective-permute-start.28 = (bf16[256,256]{1,0:T(8,128)(2,1)S(1)}, bf16[256,256]{1,0:T(8,128)(2,1)S(1)}, u32[]{:S(2)}, u32[]{:S(2)}) collective-permute-start(bf16[256,256]{1,0:T(8,128)(2,1)S(1)} %get-tuple-element.45), channel_id=1, source_target_pairs={{0,2},{2,0},{4,6},{6,4},{1,3},{3,1},{5,7},{7,5},{8,10},{10,8},{12,... | collective-permute-start | bytes 393224 | tf_op jit(solution)/shard_map/ppermute | solution.py:24
  87.4 8.2 %collective-permute-start.25 = (bf16[256,256]{1,0:T(8,128)(2,1)S(1)}, bf16[256,256]{1,0:T(8,128)(2,1)S(1)}, u32[]{:S(2)}, u32[]{:S(2)}) collective-permute-start(bf16[256,256]{1,0:T(8,128)(2,1)S(1)} %get-tuple-element.41), channel_id=1, source_target_pairs={{0,2},{2,0},{4,6},{6,4},{1,3},{3,1},{5,7},{7,5},{8,10},{10,8},{12,... | collective-permute-start | bytes 393224 | tf_op jit(solution)/shard_map/ppermute | solution.py:24
  93.6 11.8 %collective-permute-start.29 = (bf16[256,256]{1,0:T(8,128)(2,1)S(1)}, bf16[256,256]{1,0:T(8,128)(2,1)S(1)}, u32[]{:S(2)}, u32[]{:S(2)}) collective-permute-start(bf16[256,256]{1,0:T(8,128)(2,1)S(1)} %get-tuple-element.47), channel_id=1, source_target_pairs={{0,4},{2,6},{4,0},{6,2},{1,5},{3,7},{5,1},{7,3},{8,12},{10,14},{12... | collective-permute-start | bytes 393224 | tf_op jit(solution)/shard_map/ppermute | solution.py:24
  95.6 11.4 %collective-permute-start.26 = (bf16[256,256]{1,0:T(8,128)(2,1)S(1)}, bf16[256,256]{1,0:T(8,128)(2,1)S(1)}, u32[]{:S(2)}, u32[]{:S(2)}) collective-permute-start(bf16[256,256]{1,0:T(8,128)(2,1)S(1)} %get-tuple-element.43), channel_id=1, source_target_pairs={{0,4},{2,6},{4,0},{6,2},{1,5},{3,7},{5,1},{7,3},{8,12},{10,14},{12... | collective-permute-start | bytes 393224 | tf_op jit(solution)/shard_map/ppermute | solution.py:24
  105.5 6.0 %collective-permute-start.33 = (bf16[256,256]{1,0:T(8,128)(2,1)S(1)}, bf16[256,256]{1,0:T(8,128)(2,1)S(1)}, u32[]{:S(2)}, u32[]{:S(2)}) collective-permute-start(bf16[256,256]{1,0:T(8,128)(2,1)S(1)} %shard_map.59.refs_2_), channel_id=1, source_target_pairs={{0,2},{2,0},{4,6},{6,4},{1,3},{3,1},{5,7},{7,5},{8,10},{10,8},{12,... | collective-permute-start | bytes 393224 | tf_op jit(solution)/shard_map/ppermute | solution.py:24
  107.1 5.8 %collective-permute-start.31 = (bf16[256,256]{1,0:T(8,128)(2,1)S(1)}, bf16[256,256]{1,0:T(8,128)(2,1)S(1)}, u32[]{:S(2)}, u32[]{:S(2)}) collective-permute-start(bf16[256,256]{1,0:T(8,128)(2,1)S(1)} %shard_map.56.refs_0_), channel_id=1, source_target_pairs={{0,2},{2,0},{4,6},{6,4},{1,3},{3,1},{5,7},{7,5},{8,10},{10,8},{12,... | collective-permute-start | bytes 393224 | tf_op jit(solution)/shard_map/ppermute | solution.py:24
  108.0 4.9 %collective-permute-start.30 = (bf16[256,256]{1,0:T(8,128)(2,1)S(1)}, bf16[256,256]{1,0:T(8,128)(2,1)S(1)}, u32[]{:S(2)}, u32[]{:S(2)}) collective-permute-start(bf16[256,256]{1,0:T(8,128)(2,1)S(1)} %shard_map.59.refs_2_), channel_id=1, source_target_pairs={{0,1},{1,0},{2,3},{3,2},{4,5},{5,4},{6,7},{7,6},{8,9},{9,8},{10,11... | collective-permute-start | bytes 393224 | tf_op jit(solution)/shard_map/ppermute | solution.py:24
  108.0 4.9 %collective-permute-start.27 = (bf16[256,256]{1,0:T(8,128)(2,1)S(1)}, bf16[256,256]{1,0:T(8,128)(2,1)S(1)}, u32[]{:S(2)}, u32[]{:S(2)}) collective-permute-start(bf16[256,256]{1,0:T(8,128)(2,1)S(1)} %shard_map.56.refs_0_), channel_id=1, source_target_pairs={{0,1},{1,0},{2,3},{3,2},{4,5},{5,4},{6,7},{7,6},{8,9},{9,8},{10,11... | collective-permute-start | bytes 393224 | tf_op jit(solution)/shard_map/ppermute | solution.py:24
  111.5 2.7 %collective-permute-start.34 = (bf16[256,256]{1,0:T(8,128)(2,1)S(1)}, bf16[256,256]{1,0:T(8,128)(2,1)S(1)}, u32[]{:S(2)}, u32[]{:S(2)}) collective-permute-start(bf16[256,256]{1,0:T(8,128)(2,1)S(1)} %collective-permute-done.33.refs_2_), channel_id=1, source_target_pairs={{0,1},{1,0},{2,3},{3,2},{4,5},{5,4},{6,7},{7,6},{8,9},{9,8},{10,11... | collective-permute-start | bytes 393224 | tf_op jit(solution)/shard_map/ppermute | solution.py:24
  112.9 1.3 collective-permute-start.32
  115.9 8.1 %collective-permute-start.35 = (bf16[64,2048]{1,0:T(8,128)(2,1)S(1)}, bf16[64,2048]{1,0:T(8,128)(2,1)S(1)}, u32[]{:S(2)}, u32[]{:S(2)}) collective-permute-start(bf16[64,2048]{1,0:T(8,128)(2,1)S(1)} %get-tuple-element.56), channel_id=1, source_target_pairs={{0,128},{1,17},{8,136},{9,25},{16,144},{17,1},{24,152},{25,9},{64,... | collective-permute-start | bytes 786440 | tf_op jit(solution)/shard_map/ppermute | solution.py:34
  117.9 8.8 %collective-permute-start.37 = (bf16[64,2048]{1,0:T(8,128)(2,1)S(1)}, bf16[64,2048]{1,0:T(8,128)(2,1)S(1)}, u32[]{:S(2)}, u32[]{:S(2)}) collective-permute-start(bf16[64,2048]{1,0:T(8,128)(2,1)S(1)} %get-tuple-element.57), channel_id=1, source_target_pairs={{0,192},{1,25},{8,200},{9,17},{16,208},{17,9},{24,216},{25,1},{64,... | collective-permute-start | bytes 786440 | tf_op jit(solution)/shard_map/ppermute | solution.py:34
  120.1 6.8 %collective-permute-start.36 = (bf16[64,2048]{1,0:T(8,128)(2,1)S(1)}, bf16[64,2048]{1,0:T(8,128)(2,1)S(1)}, u32[]{:S(2)}, u32[]{:S(2)}) collective-permute-start(bf16[64,2048]{1,0:T(8,128)(2,1)S(1)} %get-tuple-element.58), channel_id=1, source_target_pairs={{0,64},{1,9},{8,72},{9,1},{16,80},{17,25},{24,88},{25,17},{64,0},{... | collective-permute-start | bytes 786440 | tf_op jit(solution)/shard_map/ppermute | solution.py:34
  127.1 5.9 %collective-permute-start.38 = (bf16[16,2048]{1,0:T(8,128)(2,1)S(1)}, bf16[16,2048]{1,0:T(8,128)(2,1)S(1)}, u32[]{:S(2)}, u32[]{:S(2)}) collective-permute-start(bf16[16,2048]{1,0:T(8,128)(2,1)S(1)} %get-tuple-element.62), channel_id=1, source_target_pairs={{0,16},{1,129},{8,24},{9,137},{16,0},{17,145},{24,8},{25,153},{64,... | collective-permute-start | bytes 196616 | tf_op jit(solution)/shard_map/ppermute | solution.py:34
  128.7 4.9 %collective-permute-start.40 = (bf16[16,2048]{1,0:T(8,128)(2,1)S(1)}, bf16[16,2048]{1,0:T(8,128)(2,1)S(1)}, u32[]{:S(2)}, u32[]{:S(2)}) collective-permute-start(bf16[16,2048]{1,0:T(8,128)(2,1)S(1)} %get-tuple-element.63), channel_id=1, source_target_pairs={{0,24},{1,193},{8,16},{9,201},{16,8},{17,209},{24,0},{25,217},{64,... | collective-permute-start | bytes 196616 | tf_op jit(solution)/shard_map/ppermute | solution.py:34
  130.2 4.3 %collective-permute-start.39 = (bf16[16,2048]{1,0:T(8,128)(2,1)S(1)}, bf16[16,2048]{1,0:T(8,128)(2,1)S(1)}, u32[]{:S(2)}, u32[]{:S(2)}) collective-permute-start(bf16[16,2048]{1,0:T(8,128)(2,1)S(1)} %get-tuple-element.64), channel_id=1, source_target_pairs={{0,8},{1,65},{8,0},{9,73},{16,24},{17,81},{24,16},{25,89},{64,72},... | collective-permute-start | bytes 196616 | tf_op jit(solution)/shard_map/ppermute | solution.py:34
  134.5 8.3 %collective-permute-start.41 = (f32[8,2048]{1,0:T(8,128)S(1)}, f32[8,2048]{1,0:T(8,128)S(1)}, u32[]{:S(2)}, u32[]{:S(2)}) collective-permute-start(f32[8,2048]{1,0:T(8,128)S(1)} %constant_dynamic-slice_fusion), channel_id=1, source_target_pairs={{0,32},{32,0},{1,33},{33,1},{2,34},{34,2},{3,35},{35,3},{4,36},{36... | collective-permute-start | bytes 196616 | tf_op jit(solution)/shard_map/ppermute | solution.py:24
